TPU v7x, 1024 devices: a whole 8x8x8 slice. The times are simulated.
1024 devices in a mesh: slab: 32 (over z_lo, y, core), plane: 32 (over x, z_hi).
Axes of the slice: x: 8, y: 8, z: 8 (z_hi: 4, z_lo: 2; z = z_hi * 2 + z_lo), core: 2. Of those that a mesh axis runs over, the one named last changes fastest.
Arguments:
- start_disp: float32 [3, 512, 512, 128], P(None, 'slab', 'plane'), may hold values from -6 to 6
- load: float32 [3, 512, 512, 128], P(None, 'slab', 'plane'), may hold values from -6 to 6
- shift: float32 [512, 512, 128], P('slab', 'plane'), may hold values from 0.25 to 2
- coarse: float32 [3, 256, 256, 128], P(None, 'slab', 'plane'), may hold values from -6 to 6
- aggregate: int32 [512, 512], P('slab', 'plane'), may hold values from 0 to 65535, as said below
- consistency: float32 [512, 512, 128], P('slab', 'plane'), may hold values from 0.5 to 2
Outputs:
- displacement: float32 [3, 512, 512, 128], P(None, 'slab', 'plane')
- recovered: float32 [6, 512, 512, 128], P(None, 'slab', 'plane')
- indicator: float32 [512, 512, 128], P('slab', 'plane')
Inputs may be any that keep to these rules, and one draw needn't show every extreme that they name: aggregate[i, j] = a * 256 + b with |a - i // 2| <= 1 and |b - j // 2| <= 1.
All inputs are finite; a program needn't handle non-finite values.
Results may differ from a plain program's by a relative error of at most 0.000029.
Values sent between devices are 32-bit elements; how exact they have to be, the bound alone decides.
No kernel may reach another device: no remote copies, remote signals or barrier semaphores. Data moves between devices by JAX's collectives and lax.ppermute only.
A program may use at most 32 MiB of HBM per device.

v0:
```python
import jax
import jax.numpy as jnp
from jax import lax
from jax.sharding import PartitionSpec as P

DEGREE = 4


THETA = 4.5
DELTA_C = 3.5


def extended(block, sides, width):
    for axis, dim in sides:
        count = lax.axis_size(axis)
        forward = [(i, i + 1) for i in range(count - 1)]
        backward = [(target, source) for source, target in forward]
        low = lax.ppermute(
            lax.slice_in_dim(block, block.shape[dim] - width, None, axis=dim), axis, forward
        )
        high = lax.ppermute(lax.slice_in_dim(block, 0, width, axis=dim), axis, backward)
        block = jnp.concatenate([low, block, high], axis=dim)
    return block


def stiff_apply(padded, shift_part):
    zpad = jnp.pad(padded, ((0, 0), (0, 0), (0, 0), (1, 1)))
    along_z = zpad[..., :-2] + zpad[..., 1:-1] + zpad[..., 2:]
    along_x = along_z[:, :-2] + along_z[:, 1:-1] + along_z[:, 2:]
    boxed = along_x[:, :, :-2] + along_x[:, :, 1:-1] + along_x[:, :, 2:]
    centre = padded[:, 1:-1, 1:-1]
    return (3.0 + shift_part) * centre - boxed / 3.0


def element_stress(corners, consist):
    zpad = jnp.pad(corners, ((0, 0), (0, 0), (0, 0), (0, 1)))
    diff_x = zpad[:, 1:] - zpad[:, :-1]
    grad_x = 0.25 * (
        diff_x[:, :, :-1, :-1]
        + diff_x[:, :, 1:, :-1]
        + diff_x[:, :, :-1, 1:]
        + diff_x[:, :, 1:, 1:]
    )
    diff_y = zpad[:, :, 1:] - zpad[:, :, :-1]
    grad_y = 0.25 * (
        diff_y[:, :-1, :, :-1]
        + diff_y[:, 1:, :, :-1]
        + diff_y[:, :-1, :, 1:]
        + diff_y[:, 1:, :, 1:]
    )
    diff_z = zpad[..., 1:] - zpad[..., :-1]
    grad_z = 0.25 * (
        diff_z[:, :-1, :-1] + diff_z[:, 1:, :-1] + diff_z[:, :-1, 1:] + diff_z[:, 1:, 1:]
    )
    exx = grad_x[0]
    eyy = grad_y[1]
    ezz = grad_z[2]
    exy = 0.5 * (grad_y[0] + grad_x[1])
    eyz = 0.5 * (grad_z[1] + grad_y[2])
    ezx = 0.5 * (grad_x[2] + grad_z[0])
    trace = exx + eyy + ezz
    sxx = exx - trace / 3.0
    syy = eyy - trace / 3.0
    szz = ezz - trace / 3.0
    equiv = (
        2.0 / 3.0 * (sxx * sxx + syy * syy + szz * szz + 2.0 * (exy * exy + eyz * eyz + ezx * ezx))
    )
    visc = consist * (0.01 + 3.0 * equiv) ** ((0.15 - 1.0) / 2.0)
    sig = [
        2.0 * visc * sxx + 4.0 * trace,
        2.0 * visc * syy + 4.0 * trace,
        2.0 * visc * szz + 4.0 * trace,
        2.0 * visc * exy,
        2.0 * visc * eyz,
        2.0 * visc * ezx,
    ]
    norm_sq = (
        sig[0] * sig[0]
        + sig[1] * sig[1]
        + sig[2] * sig[2]
        + 2.0 * (sig[3] * sig[3] + sig[4] * sig[4] + sig[5] * sig[5])
    )
    return jnp.stack(sig + [norm_sq], 0)


def corner_valid(start_x, start_y, rows_x, rows_y, total_x, total_y, depth):
    gx = start_x + jnp.arange(rows_x)[:, None, None]
    gy = start_y + jnp.arange(rows_y)[None, :, None]
    gz = jnp.arange(depth)[None, None, :]
    return (
        (gx >= 0) & (gx <= total_x - 2) & (gy >= 0) & (gy <= total_y - 2) & (gz <= depth - 2)
    ).astype(jnp.float32)


def prolong_local(start_disp, coarse, aggregate):
    rows_x, rows_y, depth = (start_disp.shape[1], start_disp.shape[2], start_disp.shape[3])
    coarse_x, coarse_y = (coarse.shape[1], coarse.shape[2])
    coarse_cols = coarse_y * lax.axis_size("plane")
    wide_coarse = extended(coarse, (("slab", 1), ("plane", 2)), 1)
    local_a = aggregate // coarse_cols - (lax.axis_index("slab") * coarse_x - 1)
    local_b = aggregate % coarse_cols - (lax.axis_index("plane") * coarse_y - 1)
    flat = (local_a * (coarse_y + 2) + local_b).reshape(-1)
    table = wide_coarse.reshape(3, (coarse_x + 2) * (coarse_y + 2), depth)
    moved = jnp.take(table, flat, axis=1).reshape(3, rows_x, rows_y, depth)
    return start_disp + moved


def body(start_disp, load, shift, coarse, aggregate, consistency):
    rows_x, rows_y, depth = (start_disp.shape[1], start_disp.shape[2], start_disp.shape[3])
    total_x = rows_x * lax.axis_size("slab")
    total_y = rows_y * lax.axis_size("plane")
    first_x = lax.axis_index("slab") * rows_x
    first_y = lax.axis_index("plane") * rows_y
    sigma = THETA / DELTA_C
    disp = prolong_local(start_disp, coarse, aggregate)

    def stiff(field):
        padded = extended(field, (("slab", 1), ("plane", 2)), 1)
        return stiff_apply(padded, shift)

    resid = load - stiff(disp)
    direction = resid / THETA
    rho = 1.0 / sigma
    for step in range(DEGREE):
        disp = disp + direction
        if step < DEGREE - 1:
            resid = resid - stiff(direction)
            rho_new = 1.0 / (2.0 * sigma - rho)
            direction = rho_new * rho * direction + 2.0 * rho_new / DELTA_C * resid
            rho = rho_new
    ghosted = extended(
        jnp.concatenate([disp, consistency[None]], 0), (("slab", 1), ("plane", 2)), 1
    )
    near = ghosted[0:3]
    near_consist = ghosted[3]
    valid = corner_valid(first_x - 1, first_y - 1, rows_x + 1, rows_y + 1, total_x, total_y, depth)
    elem = element_stress(near, near_consist[: rows_x + 1, : rows_y + 1]) * valid
    sum_x = elem[:, 1:] + elem[:, :-1]
    sum_y = sum_x[:, :, 1:] + sum_x[:, :, :-1]
    front = jnp.pad(sum_y, ((0, 0), (0, 0), (0, 0), (1, 0)))
    total = front[..., 1:] + front[..., :-1]
    gx = first_x + jnp.arange(rows_x)[:, None, None]
    gy = first_y + jnp.arange(rows_y)[None, :, None]
    gz = jnp.arange(depth)[None, None, :]
    count = (
        ((gx >= 1).astype(jnp.float32) + (gx <= total_x - 2).astype(jnp.float32))
        * ((gy >= 1).astype(jnp.float32) + (gy <= total_y - 2).astype(jnp.float32))
        * ((gz >= 1).astype(jnp.float32) + (gz <= depth - 2).astype(jnp.float32))
    )
    rec = total[:6] / count
    norm_rec = (
        rec[0] * rec[0]
        + rec[1] * rec[1]
        + rec[2] * rec[2]
        + 2.0 * (rec[3] * rec[3] + rec[4] * rec[4] + rec[5] * rec[5])
    )
    return (disp, rec, total[6] / count - norm_rec)


def solution(mesh):
    in_specs = (
        P(None, "slab", "plane", None),
        P(None, "slab", "plane", None),
        P("slab", "plane", None),
        P(None, "slab", "plane", None),
        P("slab", "plane"),
        P("slab", "plane", None),
    )
    out_specs = (
        P(None, "slab", "plane", None),
        P(None, "slab", "plane", None),
        P("slab", "plane", None),
    )
    return jax.shard_map(body, mesh=mesh, in_specs=in_specs, out_specs=out_specs, check_vma=False)
```

profile of v0, /device:TPU:121, one launch (start us, length us, event | category | flops | bytes accessed | tf_op | source)
XLA Modules:
  0.0 147.1 jit_solution(1355889762225187743)
XLA Ops:
  1.4 3.9 %collective-permute-start = (f32[3,1,8,128]{3,2,1,0:T(8,128)S(1)}, f32[3,1,8,128]{3,2,1,0:T(8,128)S(1)}, u32[]{:S(2)}, u32[]{:S(2)}) collective-permute-start(f32[3,1,8,128]{3,2,1,0:T(8,128)S(1)} %get-tuple-element.37), channel_id=1, source_target_pairs={{0,32},{32,64},{64,96},{96,128},{128,160},{160,192},{192,224},{224... | collective-permute-start | bytes 36872 | tf_op jit(solution)/shard_map/ppermute | solution.py:18
  9.0 3.5 %collective-permute-done.1 = f32[3,1,8,128]{3,2,1,0:T(8,128)S(1)} collective-permute-done((f32[3,1,8,128]{3,2,1,0:T(8,128)S(1)}, f32[3,1,8,128]{3,2,1,0:T(8,128)S(1)}, u32[]{:S(2)}, u32[]{:S(2)}) %collective-permute-start.1) | collective-permute-done | bytes 12320 | tf_op jit(solution)/shard_map/ppermute | solution.py:21
  12.4 7.6 %collective-permute-start.2 = (f32[3,10,1,128]{3,2,1,0:T(1,128)S(1)}, f32[3,10,1,128]{3,2,1,0:T(1,128)S(1)}, u32[]{:S(2)}, u32[]{:S(2)}) collective-permute-start(f32[3,10,1,128]{3,2,1,0:T(1,128)S(1)} %get-tuple-element.34), channel_id=1, source_target_pairs={{0,1},{1,2},{2,3},{3,4},{4,5},{5,6},{6,7},{7,8},{8,9},{9,10},{10,1... | collective-permute-start | bytes 46088 | tf_op jit(solution)/shard_map/ppermute | solution.py:18
  20.1 9.5 %collective-permute-start.3 = (f32[3,10,1,128]{3,2,1,0:T(1,128)S(1)}, f32[3,10,1,128]{3,2,1,0:T(1,128)S(1)}, u32[]{:S(2)}, u32[]{:S(2)}) collective-permute-start(f32[3,10,1,128]{3,2,1,0:T(1,128)S(1)} %get-tuple-element.35), channel_id=1, source_target_pairs={{1,0},{2,1},{3,2},{4,3},{5,4},{6,5},{7,6},{8,7},{9,8},{10,9},{11,1... | collective-permute-start | bytes 46088 | tf_op jit(solution)/shard_map/ppermute | solution.py:21
  31.7 3.2 %collective-permute-start.4 = (f32[3,1,16,128]{3,2,1,0:T(8,128)S(1)}, f32[3,1,16,128]{3,2,1,0:T(8,128)S(1)}, u32[]{:S(2)}, u32[]{:S(2)}) collective-permute-start(f32[3,1,16,128]{3,2,1,0:T(8,128)S(1)} %get-tuple-element.30), channel_id=1, source_target_pairs={{0,32},{32,64},{64,96},{96,128},{128,160},{160,192},{192,224},{224... | collective-permute-start | bytes 73736 | tf_op jit(solution)/shard_map/ppermute | solution.py:18
  36.9 5.3 %collective-permute-done.5 = f32[3,1,16,128]{3,2,1,0:T(8,128)S(1)} collective-permute-done((f32[3,1,16,128]{3,2,1,0:T(8,128)S(1)}, f32[3,1,16,128]{3,2,1,0:T(8,128)S(1)}, u32[]{:S(2)}, u32[]{:S(2)}) %collective-permute-start.5) | collective-permute-done | bytes 24608 | tf_op jit(solution)/shard_map/ppermute | solution.py:21
  42.2 4.9 %collective-permute-start.6 = (f32[3,18,1,128]{3,2,1,0:T(1,128)S(1)}, f32[3,18,1,128]{3,2,1,0:T(1,128)S(1)}, u32[]{:S(2)}, u32[]{:S(2)}) collective-permute-start(f32[3,18,1,128]{3,2,1,0:T(1,128)S(1)} %get-tuple-element.22), channel_id=1, source_target_pairs={{0,1},{1,2},{2,3},{3,4},{4,5},{5,6},{6,7},{7,8},{8,9},{9,10},{10,1... | collective-permute-start | bytes 82952 | tf_op jit(solution)/shard_map/ppermute | solution.py:18
  47.0 5.2 %collective-permute-start.7 = (f32[3,18,1,128]{3,2,1,0:T(1,128)S(1)}, f32[3,18,1,128]{3,2,1,0:T(1,128)S(1)}, u32[]{:S(2)}, u32[]{:S(2)}) collective-permute-start(f32[3,18,1,128]{3,2,1,0:T(1,128)S(1)} %get-tuple-element.23), channel_id=1, source_target_pairs={{1,0},{2,1},{3,2},{4,3},{5,4},{6,5},{7,6},{8,7},{9,8},{10,9},{11,1... | collective-permute-start | bytes 82952 | tf_op jit(solution)/shard_map/ppermute | solution.py:21
  54.9 2.8 %collective-permute-start.8 = (f32[3,1,16,128]{3,2,1,0:T(8,128)S(1)}, f32[3,1,16,128]{3,2,1,0:T(8,128)S(1)}, u32[]{:S(2)}, u32[]{:S(2)}) collective-permute-start(f32[3,1,16,128]{3,2,1,0:T(8,128)S(1)} %get-tuple-element.28), channel_id=1, source_target_pairs={{0,32},{32,64},{64,96},{96,128},{128,160},{160,192},{192,224},{224... | collective-permute-start | bytes 73736 | tf_op jit(solution)/shard_map/ppermute | solution.py:18
  59.7 5.3 %collective-permute-done.9 = f32[3,1,16,128]{3,2,1,0:T(8,128)S(1)} collective-permute-done((f32[3,1,16,128]{3,2,1,0:T(8,128)S(1)}, f32[3,1,16,128]{3,2,1,0:T(8,128)S(1)}, u32[]{:S(2)}, u32[]{:S(2)}) %collective-permute-start.9) | collective-permute-done | bytes 24608 | tf_op jit(solution)/shard_map/ppermute | solution.py:21
  65.0 5.7 %collective-permute-start.10 = (f32[3,18,1,128]{3,2,1,0:T(1,128)S(1)}, f32[3,18,1,128]{3,2,1,0:T(1,128)S(1)}, u32[]{:S(2)}, u32[]{:S(2)}) collective-permute-start(f32[3,18,1,128]{3,2,1,0:T(1,128)S(1)} %get-tuple-element.20), channel_id=1, source_target_pairs={{0,1},{1,2},{2,3},{3,4},{4,5},{5,6},{6,7},{7,8},{8,9},{9,10},{10,1... | collective-permute-start | bytes 82952 | tf_op jit(solution)/shard_map/ppermute | solution.py:18
  70.7 4.4 %collective-permute-start.11 = (f32[3,18,1,128]{3,2,1,0:T(1,128)S(1)}, f32[3,18,1,128]{3,2,1,0:T(1,128)S(1)}, u32[]{:S(2)}, u32[]{:S(2)}) collective-permute-start(f32[3,18,1,128]{3,2,1,0:T(1,128)S(1)} %get-tuple-element.21), channel_id=1, source_target_pairs={{1,0},{2,1},{3,2},{4,3},{5,4},{6,5},{7,6},{8,7},{9,8},{10,9},{11,1... | collective-permute-start | bytes 82952 | tf_op jit(solution)/shard_map/ppermute | solution.py:21
  76.9 3.4 %collective-permute-start.12 = (f32[3,1,16,128]{3,2,1,0:T(8,128)S(1)}, f32[3,1,16,128]{3,2,1,0:T(8,128)S(1)}, u32[]{:S(2)}, u32[]{:S(2)}) collective-permute-start(f32[3,1,16,128]{3,2,1,0:T(8,128)S(1)} %get-tuple-element.26), channel_id=1, source_target_pairs={{0,32},{32,64},{64,96},{96,128},{128,160},{160,192},{192,224},{224... | collective-permute-start | bytes 73736 | tf_op jit(solution)/shard_map/ppermute | solution.py:18
  82.3 5.3 %collective-permute-done.13 = f32[3,1,16,128]{3,2,1,0:T(8,128)S(1)} collective-permute-done((f32[3,1,16,128]{3,2,1,0:T(8,128)S(1)}, f32[3,1,16,128]{3,2,1,0:T(8,128)S(1)}, u32[]{:S(2)}, u32[]{:S(2)}) %collective-permute-start.13) | collective-permute-done | bytes 24608 | tf_op jit(solution)/shard_map/ppermute | solution.py:21
  87.6 3.7 %collective-permute-start.14 = (f32[3,18,1,128]{3,2,1,0:T(1,128)S(1)}, f32[3,18,1,128]{3,2,1,0:T(1,128)S(1)}, u32[]{:S(2)}, u32[]{:S(2)}) collective-permute-start(f32[3,18,1,128]{3,2,1,0:T(1,128)S(1)} %get-tuple-element.18), channel_id=1, source_target_pairs={{0,1},{1,2},{2,3},{3,4},{4,5},{5,6},{6,7},{7,8},{8,9},{9,10},{10,1... | collective-permute-start | bytes 82952 | tf_op jit(solution)/shard_map/ppermute | solution.py:18
  91.4 5.8 %collective-permute-start.15 = (f32[3,18,1,128]{3,2,1,0:T(1,128)S(1)}, f32[3,18,1,128]{3,2,1,0:T(1,128)S(1)}, u32[]{:S(2)}, u32[]{:S(2)}) collective-permute-start(f32[3,18,1,128]{3,2,1,0:T(1,128)S(1)} %get-tuple-element.19), channel_id=1, source_target_pairs={{1,0},{2,1},{3,2},{4,3},{5,4},{6,5},{7,6},{8,7},{9,8},{10,9},{11,1... | collective-permute-start | bytes 82952 | tf_op jit(solution)/shard_map/ppermute | solution.py:21
  98.9 3.1 %collective-permute-start.16 = (f32[3,1,16,128]{3,2,1,0:T(8,128)S(1)}, f32[3,1,16,128]{3,2,1,0:T(8,128)S(1)}, u32[]{:S(2)}, u32[]{:S(2)}) collective-permute-start(f32[3,1,16,128]{3,2,1,0:T(8,128)S(1)} %get-tuple-element.24), channel_id=1, source_target_pairs={{0,32},{32,64},{64,96},{96,128},{128,160},{160,192},{192,224},{224... | collective-permute-start | bytes 73736 | tf_op jit(solution)/shard_map/ppermute | solution.py:18
  101.9 1.9 %collective-permute-start.17 = (f32[3,1,16,128]{3,2,1,0:T(8,128)S(1)}, f32[3,1,16,128]{3,2,1,0:T(8,128)S(1)}, u32[]{:S(2)}, u32[]{:S(2)}) collective-permute-start(f32[3,1,16,128]{3,2,1,0:T(8,128)S(1)} %get-tuple-element.25), channel_id=1, source_target_pairs={{32,0},{64,32},{96,64},{128,96},{160,128},{192,160},{224,192},{256... | collective-permute-start | bytes 73736 | tf_op jit(solution)/shard_map/ppermute | solution.py:21
  103.9 5.3 %collective-permute-done.17 = f32[3,1,16,128]{3,2,1,0:T(8,128)S(1)} collective-permute-done((f32[3,1,16,128]{3,2,1,0:T(8,128)S(1)}, f32[3,1,16,128]{3,2,1,0:T(8,128)S(1)}, u32[]{:S(2)}, u32[]{:S(2)}) %collective-permute-start.17) | collective-permute-done | bytes 24608 | tf_op jit(solution)/shard_map/ppermute | solution.py:21
  109.2 2.8 %collective-permute-start.18 = (f32[3,18,1,128]{3,2,1,0:T(1,128)S(1)}, f32[3,18,1,128]{3,2,1,0:T(1,128)S(1)}, u32[]{:S(2)}, u32[]{:S(2)}) collective-permute-start(f32[3,18,1,128]{3,2,1,0:T(1,128)S(1)} %get-tuple-element.16), channel_id=1, source_target_pairs={{0,1},{1,2},{2,3},{3,4},{4,5},{5,6},{6,7},{7,8},{8,9},{9,10},{10,1... | collective-permute-start | bytes 82952 | tf_op jit(solution)/shard_map/ppermute | solution.py:18
  112.1 7.2 %collective-permute-start.19 = (f32[3,18,1,128]{3,2,1,0:T(1,128)S(1)}, f32[3,18,1,128]{3,2,1,0:T(1,128)S(1)}, u32[]{:S(2)}, u32[]{:S(2)}) collective-permute-start(f32[3,18,1,128]{3,2,1,0:T(1,128)S(1)} %get-tuple-element.17), channel_id=1, source_target_pairs={{1,0},{2,1},{3,2},{4,3},{5,4},{6,5},{7,6},{8,7},{9,8},{10,9},{11,1... | collective-permute-start | bytes 82952 | tf_op jit(solution)/shard_map/ppermute | solution.py:21
  121.8 2.8 %collective-permute-start.20 = (f32[4,1,16,128]{3,2,1,0:T(8,128)S(1)}, f32[4,1,16,128]{3,2,1,0:T(8,128)S(1)}, u32[]{:S(2)}, u32[]{:S(2)}) collective-permute-start(f32[4,1,16,128]{3,2,1,0:T(8,128)S(1)} %get-tuple-element.14), channel_id=1, source_target_pairs={{0,32},{32,64},{64,96},{96,128},{128,160},{160,192},{192,224},{224... | collective-permute-start | bytes 98312 | tf_op jit(solution)/shard_map/ppermute | solution.py:18
  126.5 5.4 %collective-permute-done.21 = f32[4,1,16,128]{3,2,1,0:T(8,128)S(1)} collective-permute-done((f32[4,1,16,128]{3,2,1,0:T(8,128)S(1)}, f32[4,1,16,128]{3,2,1,0:T(8,128)S(1)}, u32[]{:S(2)}, u32[]{:S(2)}) %collective-permute-start.21) | collective-permute-done | bytes 32800 | tf_op jit(solution)/shard_map/ppermute | solution.py:21
  133.9 8.2 %collective-permute-start.23 = (f32[4,18,1,128]{3,2,1,0:T(1,128)S(1)}, f32[4,18,1,128]{3,2,1,0:T(1,128)S(1)}, u32[]{:S(2)}, u32[]{:S(2)}) collective-permute-start(f32[4,18,1,128]{3,2,1,0:T(1,128)S(1)} %get-tuple-element.13), channel_id=1, source_target_pairs={{1,0},{2,1},{3,2},{4,3},{5,4},{6,5},{7,6},{8,7},{9,8},{10,9},{11,1... | collective-permute-start | bytes 110600 | tf_op jit(solution)/shard_map/ppermute | solution.py:21
  (105 shorter events, 29.9 us)
Async XLA Ops:
  1.4 6.6 %collective-permute-start = (f32[3,1,8,128]{3,2,1,0:T(8,128)S(1)}, f32[3,1,8,128]{3,2,1,0:T(8,128)S(1)}, u32[]{:S(2)}, u32[]{:S(2)}) collective-permute-start(f32[3,1,8,128]{3,2,1,0:T(8,128)S(1)} %get-tuple-element.37), channel_id=1, source_target_pairs={{0,32},{32,64},{64,96},{96,128},{128,160},{160,192},{192,224},{224... | collective-permute-start | bytes 36872 | tf_op jit(solution)/shard_map/ppermute | solution.py:18
  5.3 7.1 %collective-permute-start.1 = (f32[3,1,8,128]{3,2,1,0:T(8,128)S(1)}, f32[3,1,8,128]{3,2,1,0:T(8,128)S(1)}, u32[]{:S(2)}, u32[]{:S(2)}) collective-permute-start(f32[3,1,8,128]{3,2,1,0:T(8,128)S(1)} %get-tuple-element.36), channel_id=1, source_target_pairs={{32,0},{64,32},{96,64},{128,96},{160,128},{192,160},{224,192},{256... | collective-permute-start | bytes 36872 | tf_op jit(solution)/shard_map/ppermute | solution.py:21
  12.4 17.2 %collective-permute-start.2 = (f32[3,10,1,128]{3,2,1,0:T(1,128)S(1)}, f32[3,10,1,128]{3,2,1,0:T(1,128)S(1)}, u32[]{:S(2)}, u32[]{:S(2)}) collective-permute-start(f32[3,10,1,128]{3,2,1,0:T(1,128)S(1)} %get-tuple-element.34), channel_id=1, source_target_pairs={{0,1},{1,2},{2,3},{3,4},{4,5},{5,6},{6,7},{7,8},{8,9},{9,10},{10,1... | collective-permute-start | bytes 46088 | tf_op jit(solution)/shard_map/ppermute | solution.py:18
  20.1 10.3 %collective-permute-start.3 = (f32[3,10,1,128]{3,2,1,0:T(1,128)S(1)}, f32[3,10,1,128]{3,2,1,0:T(1,128)S(1)}, u32[]{:S(2)}, u32[]{:S(2)}) collective-permute-start(f32[3,10,1,128]{3,2,1,0:T(1,128)S(1)} %get-tuple-element.35), channel_id=1, source_target_pairs={{1,0},{2,1},{3,2},{4,3},{5,4},{6,5},{7,6},{8,7},{9,8},{10,9},{11,1... | collective-permute-start | bytes 46088 | tf_op jit(solution)/shard_map/ppermute | solution.py:21
  31.7 5.1 %collective-permute-start.4 = (f32[3,1,16,128]{3,2,1,0:T(8,128)S(1)}, f32[3,1,16,128]{3,2,1,0:T(8,128)S(1)}, u32[]{:S(2)}, u32[]{:S(2)}) collective-permute-start(f32[3,1,16,128]{3,2,1,0:T(8,128)S(1)} %get-tuple-element.30), channel_id=1, source_target_pairs={{0,32},{32,64},{64,96},{96,128},{128,160},{160,192},{192,224},{224... | collective-permute-start | bytes 73736 | tf_op jit(solution)/shard_map/ppermute | solution.py:18
  34.9 7.3 %collective-permute-start.5 = (f32[3,1,16,128]{3,2,1,0:T(8,128)S(1)}, f32[3,1,16,128]{3,2,1,0:T(8,128)S(1)}, u32[]{:S(2)}, u32[]{:S(2)}) collective-permute-start(f32[3,1,16,128]{3,2,1,0:T(8,128)S(1)} %get-tuple-element.31), channel_id=1, source_target_pairs={{32,0},{64,32},{96,64},{128,96},{160,128},{192,160},{224,192},{256... | collective-permute-start | bytes 73736 | tf_op jit(solution)/shard_map/ppermute | solution.py:21
  42.2 10.1 %collective-permute-start.6 = (f32[3,18,1,128]{3,2,1,0:T(1,128)S(1)}, f32[3,18,1,128]{3,2,1,0:T(1,128)S(1)}, u32[]{:S(2)}, u32[]{:S(2)}) collective-permute-start(f32[3,18,1,128]{3,2,1,0:T(1,128)S(1)} %get-tuple-element.22), channel_id=1, source_target_pairs={{0,1},{1,2},{2,3},{3,4},{4,5},{5,6},{6,7},{7,8},{8,9},{9,10},{10,1... | collective-permute-start | bytes 82952 | tf_op jit(solution)/shard_map/ppermute | solution.py:18
  47.0 6.2 %collective-permute-start.7 = (f32[3,18,1,128]{3,2,1,0:T(1,128)S(1)}, f32[3,18,1,128]{3,2,1,0:T(1,128)S(1)}, u32[]{:S(2)}, u32[]{:S(2)}) collective-permute-start(f32[3,18,1,128]{3,2,1,0:T(1,128)S(1)} %get-tuple-element.23), channel_id=1, source_target_pairs={{1,0},{2,1},{3,2},{4,3},{5,4},{6,5},{7,6},{8,7},{9,8},{10,9},{11,1... | collective-permute-start | bytes 82952 | tf_op jit(solution)/shard_map/ppermute | solution.py:21
  54.9 4.7 %collective-permute-start.8 = (f32[3,1,16,128]{3,2,1,0:T(8,128)S(1)}, f32[3,1,16,128]{3,2,1,0:T(8,128)S(1)}, u32[]{:S(2)}, u32[]{:S(2)}) collective-permute-start(f32[3,1,16,128]{3,2,1,0:T(8,128)S(1)} %get-tuple-element.28), channel_id=1, source_target_pairs={{0,32},{32,64},{64,96},{96,128},{128,160},{160,192},{192,224},{224... | collective-permute-start | bytes 73736 | tf_op jit(solution)/shard_map/ppermute | solution.py:18
  57.7 7.3 %collective-permute-start.9 = (f32[3,1,16,128]{3,2,1,0:T(8,128)S(1)}, f32[3,1,16,128]{3,2,1,0:T(8,128)S(1)}, u32[]{:S(2)}, u32[]{:S(2)}) collective-permute-start(f32[3,1,16,128]{3,2,1,0:T(8,128)S(1)} %get-tuple-element.29), channel_id=1, source_target_pairs={{32,0},{64,32},{96,64},{128,96},{160,128},{192,160},{224,192},{256... | collective-permute-start | bytes 73736 | tf_op jit(solution)/shard_map/ppermute | solution.py:21
  65.0 10.2 %collective-permute-start.10 = (f32[3,18,1,128]{3,2,1,0:T(1,128)S(1)}, f32[3,18,1,128]{3,2,1,0:T(1,128)S(1)}, u32[]{:S(2)}, u32[]{:S(2)}) collective-permute-start(f32[3,18,1,128]{3,2,1,0:T(1,128)S(1)} %get-tuple-element.20), channel_id=1, source_target_pairs={{0,1},{1,2},{2,3},{3,4},{4,5},{5,6},{6,7},{7,8},{8,9},{9,10},{10,1... | collective-permute-start | bytes 82952 | tf_op jit(solution)/shard_map/ppermute | solution.py:18
  70.7 5.5 %collective-permute-start.11 = (f32[3,18,1,128]{3,2,1,0:T(1,128)S(1)}, f32[3,18,1,128]{3,2,1,0:T(1,128)S(1)}, u32[]{:S(2)}, u32[]{:S(2)}) collective-permute-start(f32[3,18,1,128]{3,2,1,0:T(1,128)S(1)} %get-tuple-element.21), channel_id=1, source_target_pairs={{1,0},{2,1},{3,2},{4,3},{5,4},{6,5},{7,6},{8,7},{9,8},{10,9},{11,1... | collective-permute-start | bytes 82952 | tf_op jit(solution)/shard_map/ppermute | solution.py:21
  76.9 5.3 %collective-permute-start.12 = (f32[3,1,16,128]{3,2,1,0:T(8,128)S(1)}, f32[3,1,16,128]{3,2,1,0:T(8,128)S(1)}, u32[]{:S(2)}, u32[]{:S(2)}) collective-permute-start(f32[3,1,16,128]{3,2,1,0:T(8,128)S(1)} %get-tuple-element.26), channel_id=1, source_target_pairs={{0,32},{32,64},{64,96},{96,128},{128,160},{160,192},{192,224},{224... | collective-permute-start | bytes 73736 | tf_op jit(solution)/shard_map/ppermute | solution.py:18
  80.3 7.3 %collective-permute-start.13 = (f32[3,1,16,128]{3,2,1,0:T(8,128)S(1)}, f32[3,1,16,128]{3,2,1,0:T(8,128)S(1)}, u32[]{:S(2)}, u32[]{:S(2)}) collective-permute-start(f32[3,1,16,128]{3,2,1,0:T(8,128)S(1)} %get-tuple-element.27), channel_id=1, source_target_pairs={{32,0},{64,32},{96,64},{128,96},{160,128},{192,160},{224,192},{256... | collective-permute-start | bytes 73736 | tf_op jit(solution)/shard_map/ppermute | solution.py:21
  87.6 9.6 %collective-permute-start.14 = (f32[3,18,1,128]{3,2,1,0:T(1,128)S(1)}, f32[3,18,1,128]{3,2,1,0:T(1,128)S(1)}, u32[]{:S(2)}, u32[]{:S(2)}) collective-permute-start(f32[3,18,1,128]{3,2,1,0:T(1,128)S(1)} %get-tuple-element.18), channel_id=1, source_target_pairs={{0,1},{1,2},{2,3},{3,4},{4,5},{5,6},{6,7},{7,8},{8,9},{9,10},{10,1... | collective-permute-start | bytes 82952 | tf_op jit(solution)/shard_map/ppermute | solution.py:18
  91.4 6.7 %collective-permute-start.15 = (f32[3,18,1,128]{3,2,1,0:T(1,128)S(1)}, f32[3,18,1,128]{3,2,1,0:T(1,128)S(1)}, u32[]{:S(2)}, u32[]{:S(2)}) collective-permute-start(f32[3,18,1,128]{3,2,1,0:T(1,128)S(1)} %get-tuple-element.19), channel_id=1, source_target_pairs={{1,0},{2,1},{3,2},{4,3},{5,4},{6,5},{7,6},{8,7},{9,8},{10,9},{11,1... | collective-permute-start | bytes 82952 | tf_op jit(solution)/shard_map/ppermute | solution.py:21
  98.9 5.0 %collective-permute-start.16 = (f32[3,1,16,128]{3,2,1,0:T(8,128)S(1)}, f32[3,1,16,128]{3,2,1,0:T(8,128)S(1)}, u32[]{:S(2)}, u32[]{:S(2)}) collective-permute-start(f32[3,1,16,128]{3,2,1,0:T(8,128)S(1)} %get-tuple-element.24), channel_id=1, source_target_pairs={{0,32},{32,64},{64,96},{96,128},{128,160},{160,192},{192,224},{224... | collective-permute-start | bytes 73736 | tf_op jit(solution)/shard_map/ppermute | solution.py:18
  101.9 7.3 %collective-permute-start.17 = (f32[3,1,16,128]{3,2,1,0:T(8,128)S(1)}, f32[3,1,16,128]{3,2,1,0:T(8,128)S(1)}, u32[]{:S(2)}, u32[]{:S(2)}) collective-permute-start(f32[3,1,16,128]{3,2,1,0:T(8,128)S(1)} %get-tuple-element.25), channel_id=1, source_target_pairs={{32,0},{64,32},{96,64},{128,96},{160,128},{192,160},{224,192},{256... | collective-permute-start | bytes 73736 | tf_op jit(solution)/shard_map/ppermute | solution.py:21
  109.2 10.2 %collective-permute-start.18 = (f32[3,18,1,128]{3,2,1,0:T(1,128)S(1)}, f32[3,18,1,128]{3,2,1,0:T(1,128)S(1)}, u32[]{:S(2)}, u32[]{:S(2)}) collective-permute-start(f32[3,18,1,128]{3,2,1,0:T(1,128)S(1)} %get-tuple-element.16), channel_id=1, source_target_pairs={{0,1},{1,2},{2,3},{3,4},{4,5},{5,6},{6,7},{7,8},{8,9},{9,10},{10,1... | collective-permute-start | bytes 82952 | tf_op jit(solution)/shard_map/ppermute | solution.py:18
  112.1 8.2 %collective-permute-start.19 = (f32[3,18,1,128]{3,2,1,0:T(1,128)S(1)}, f32[3,18,1,128]{3,2,1,0:T(1,128)S(1)}, u32[]{:S(2)}, u32[]{:S(2)}) collective-permute-start(f32[3,18,1,128]{3,2,1,0:T(1,128)S(1)} %get-tuple-element.17), channel_id=1, source_target_pairs={{1,0},{2,1},{3,2},{4,3},{5,4},{6,5},{7,6},{8,7},{9,8},{10,9},{11,1... | collective-permute-start | bytes 82952 | tf_op jit(solution)/shard_map/ppermute | solution.py:21
  121.8 4.7 %collective-permute-start.20 = (f32[4,1,16,128]{3,2,1,0:T(8,128)S(1)}, f32[4,1,16,128]{3,2,1,0:T(8,128)S(1)}, u32[]{:S(2)}, u32[]{:S(2)}) collective-permute-start(f32[4,1,16,128]{3,2,1,0:T(8,128)S(1)} %get-tuple-element.14), channel_id=1, source_target_pairs={{0,32},{32,64},{64,96},{96,128},{128,160},{160,192},{192,224},{224... | collective-permute-start | bytes 98312 | tf_op jit(solution)/shard_map/ppermute | solution.py:18
  124.5 7.3 %collective-permute-start.21 = (f32[4,1,16,128]{3,2,1,0:T(8,128)S(1)}, f32[4,1,16,128]{3,2,1,0:T(8,128)S(1)}, u32[]{:S(2)}, u32[]{:S(2)}) collective-permute-start(f32[4,1,16,128]{3,2,1,0:T(8,128)S(1)} %get-tuple-element.15), channel_id=1, source_target_pairs={{32,0},{64,32},{96,64},{128,96},{160,128},{192,160},{224,192},{256... | collective-permute-start | bytes 98312 | tf_op jit(solution)/shard_map/ppermute | solution.py:21
  131.9 10.2 %collective-permute-start.22 = (f32[4,18,1,128]{3,2,1,0:T(1,128)S(1)}, f32[4,18,1,128]{3,2,1,0:T(1,128)S(1)}, u32[]{:S(2)}, u32[]{:S(2)}) collective-permute-start(f32[4,18,1,128]{3,2,1,0:T(1,128)S(1)} %get-tuple-element.12), channel_id=1, source_target_pairs={{0,1},{1,2},{2,3},{3,4},{4,5},{5,6},{6,7},{7,8},{8,9},{9,10},{10,1... | collective-permute-start | bytes 110600 | tf_op jit(solution)/shard_map/ppermute | solution.py:18
  133.9 9.2 %collective-permute-start.23 = (f32[4,18,1,128]{3,2,1,0:T(1,128)S(1)}, f32[4,18,1,128]{3,2,1,0:T(1,128)S(1)}, u32[]{:S(2)}, u32[]{:S(2)}) collective-permute-start(f32[4,18,1,128]{3,2,1,0:T(1,128)S(1)} %get-tuple-element.13), channel_id=1, source_target_pairs={{1,0},{2,1},{3,2},{4,3},{5,4},{6,5},{7,6},{8,7},{9,8},{10,9},{11,1... | collective-permute-start | bytes 110600 | tf_op jit(solution)/shard_map/ppermute | solution.py:21
  (6 other events, 64.2 us)
where the time goes:
time: 148 us; the launch traced here: 147 us
  starting transfers between devices  97.4 us (66%)
  waiting for transfers between devices  35.4 us (24%)
  other arithmetic  8.66 us (6%)
  local copies, waits for them, and re-layouts  4.31 us (3%)
    ppermute x12, starting transfers between devices, extended(): lax.ppermute(lax.slice_in_dim(block, 0, width, axis=dim), axis, backward)  51.8 us
    ppermute x12, starting transfers between devices, extended(): lax.ppermute(lax.slice_in_dim(block, block.shape[dim] - width, None, axis...  45.6 us
    ppermute x12, waiting for transfers between devices, extended(): lax.ppermute(lax.slice_in_dim(block, 0, width, axis=dim), axis, backward)  35.4 us
  transfers between devices with their start and end apart: 24, of which 12 were waited for; matrix products, arithmetic and copies ran while one was open for 1% of the time, Pallas kernels for 0%

commit v1 on v0

v1 whole, which is shorter than its diff:
```python
import functools

import jax
import jax.numpy as jnp
from jax import lax
from jax.experimental import pallas as pl
from jax.experimental.pallas import tpu as pltpu
from jax.sharding import PartitionSpec as P

B = 16
CB = 8
Z = 128
W = 24
ROWS = 26

DEGREE = 4
THETA = 4.5
DELTA_C = 3.5
F32 = jnp.float32

PS, PL_, PH, PK, PA, PC = 0, 240, 432, 496, 592, 608
PF_ROWS, PB_ROWS = 624, 608

QS, QL, QH, QC, QK, QX, QA = 0, 360, 648, 744, 768, 960, 1008
Q_ROWS = 1016


def place(col):
    index = col + 4
    return (index % 3) * 8 + index // 3


def pack_kernel(start, load, shift, cons, coarse, agg, fwd, bwd):
    slab = lax.axis_index("slab")
    plane = lax.axis_index("plane")
    coarse_cols = CB * lax.axis_size("plane")
    for c in range(3):
        for w in range(5):
            row = PS + 16 * (5 * c + w)
            fwd[row : row + 16, :] = start[pl.ds(256 * c + 11 + w, 16, stride=16), :]
            bwd[row : row + 16, :] = start[pl.ds(256 * c + w, 16, stride=16), :]
        for w in range(4):
            row = PL_ + 16 * (4 * c + w)
            fwd[row : row + 16, :] = load[pl.ds(256 * c + 12 + w, 16, stride=16), :]
            bwd[row : row + 16, :] = load[pl.ds(256 * c + w, 16, stride=16), :]
            row = PK + 8 * (4 * c + w)
            fwd[row : row + 8, :] = coarse[pl.ds(64 * c + 4 + w, 8, stride=8), :]
            bwd[row : row + 8, :] = coarse[pl.ds(64 * c + w, 8, stride=8), :]
    for w in range(4):
        row = PH + 16 * w
        fwd[row : row + 16, :] = shift[pl.ds(12 + w, 16, stride=16), :]
        bwd[row : row + 16, :] = shift[pl.ds(w, 16, stride=16), :]
    fwd[PC : PC + 16, :] = cons[pl.ds(15, 16, stride=16), :]
    value = agg[...]
    step_a = value // coarse_cols - (slab * CB + lax.broadcasted_iota(jnp.int32, (B, B), 0) // 2) + 1
    step_b = value % coarse_cols - (plane * CB + lax.broadcasted_iota(jnp.int32, (B, B), 1) // 2) + 1
    code = (1 + 16 * step_a + step_b).astype(F32)
    for out in (fwd, bwd):
        out[PA : PA + 16, :] = jnp.zeros((16, Z), F32)
        out[PA : PA + 16, 0:B] = code


OWN = ((0, 2, 2, 5), (1, 1, 0, 6), (2, 1, 1, 5))


def own_kernel(start, load, shift, cons, coarse, fwd, es, el, eh, ec, ek, ea):
    def rows(ci, carry):
        for l, s0, j0, n in OWN:
            for src, dst in ((start, es), (load, el)):
                dst[ci, 8 * l + s0 : 8 * l + s0 + n, :] = src[ci, pl.ds(j0, n, stride=3), :]
        return carry

    lax.fori_loop(0, 3 * B, rows, 0, unroll=4)

    def rows1(ci, carry):
        for l, s0, j0, n in OWN:
            for src, dst in ((shift, eh), (cons, ec)):
                dst[ci, 8 * l + s0 : 8 * l + s0 + n, :] = src[ci, pl.ds(j0, n, stride=3), :]
        return carry

    lax.fori_loop(0, B, rows1, 0, unroll=4)
    for ca in range(3 * CB):
        ek[ca, 4:12, :] = coarse[ca]
    ea[...] = pltpu.roll(fwd[PA : PA + 16, :], 5, 1)


def join_kernel(low, high, es, el, eh, ec, ek, ea, es_o, el_o, eh_o, ec_o, ek_o, ea_o, ex_o, on, off):
    del es, el, eh, ec, ek
    for c in range(3):
        for w in range(5):
            row = PS + 16 * (5 * c + w)
            if w > 0:
                es_o[pl.ds(384 * c + place(w - 5), 16, stride=24), :] = low[row : row + 16, :]
            else:
                ex_o[2 * c] = low[row : row + 16, :]
            if w < 4:
                es_o[pl.ds(384 * c + place(16 + w), 16, stride=24), :] = high[row : row + 16, :]
            else:
                ex_o[2 * c + 1] = high[row : row + 16, :]
        for w in range(4):
            row = PL_ + 16 * (4 * c + w)
            el_o[pl.ds(384 * c + place(w - 4), 16, stride=24), :] = low[row : row + 16, :]
            el_o[pl.ds(384 * c + place(16 + w), 16, stride=24), :] = high[row : row + 16, :]
            row = PK + 8 * (4 * c + w)
            ek_o[pl.ds(128 * c + w, 8, stride=16), :] = low[row : row + 8, :]
            ek_o[pl.ds(128 * c + 12 + w, 8, stride=16), :] = high[row : row + 8, :]
    for w in range(4):
        row = PH + 16 * w
        eh_o[pl.ds(place(w - 4), 16, stride=24), :] = low[row : row + 16, :]
        eh_o[pl.ds(place(16 + w), 16, stride=24), :] = high[row : row + 16, :]
    ec_o[pl.ds(place(-1), 16, stride=24), :] = low[PC : PC + 16, :]
    lane = lax.broadcasted_iota(jnp.int32, (B, Z), 1)
    left = pltpu.roll(low[PA : PA + 16, :], Z - 11, 1)
    right = pltpu.roll(high[PA : PA + 16, :], 21, 1)
    code = jnp.where(lane < 5, left, jnp.where(lane < 21, ea[...], jnp.where(lane < 26, right, 0.0)))
    ea_o[...] = code
    odd = lax.axis_index("slab") % 2
    for out, top in ((on, 1 - odd), (off, odd)):
        for c in range(3):
            out[QS + 120 * c : QS + 120 * (c + 1), :] = es_o[
                pl.ds(pl.multiple_of(384 * c + top * (11 * W), 8), 120), :
            ]
            out[QL + 96 * c : QL + 96 * (c + 1), :] = el_o[
                pl.ds(pl.multiple_of(384 * c + top * (12 * W), 8), 96), :
            ]
            out[QK + 64 * c : QK + 64 * (c + 1), :] = ek_o[
                pl.ds(pl.multiple_of(128 * c + top * 64, 8), 64), :
            ]
        out[QH : QH + 96, :] = eh_o[pl.ds(pl.multiple_of(top * (12 * W), 8), 96), :]
        out[QC : QC + 24, :] = ec_o[pl.ds(pl.multiple_of(top * (15 * W), 8), 24), :]
        for q in range(6):
            out[QX + 8 * q : QX + 8 * (q + 1), :] = ex_o[q, pl.ds(pl.multiple_of(top * 8, 8), 8), :]
        out[QA : QA + 8, :] = ea_o[pl.ds(pl.multiple_of(top * 8, 8), 8), :]


def smooth_kernel(
    on, off, es, el, eh, ec, ek, ea, ex,
    disp, rec, ind,
    fd, fr, fh, fc, fk, fx, fa, d0, d1, d2, d3, gx, ey, st,
):
    slab = lax.axis_index("slab")
    plane = lax.axis_index("plane")
    n_slab = lax.axis_size("slab")
    n_plane = lax.axis_size("plane")
    odd = slab % 2

    def aligned(index):
        return pl.multiple_of(index, 8)

    for c in range(3):
        fd[c, 5 * W : 21 * W, :] = es[384 * c : 384 * (c + 1), :]
        fr[c, 5 * W : 21 * W, :] = el[384 * c : 384 * (c + 1), :]
        fk[c, 64:192, :] = ek[128 * c : 128 * (c + 1), :]
    fh[5 * W : 21 * W, :] = eh[...]
    fc[5 * W : 21 * W, :] = ec[...]
    for q in range(6):
        fx[q, 8:24, :] = ex[q]
    fa[8:24, :] = ea[...]
    for src, below in ((on.at[1 - odd], odd), (off, 1 - odd)):
        above = 1 - below
        for c in range(3):
            fd[c, pl.ds(aligned(above * (21 * W)), 120), :] = src[QS + 120 * c : QS + 120 * (c + 1), :]
            fr[c, pl.ds(aligned(W + above * (20 * W)), 96), :] = src[QL + 96 * c : QL + 96 * (c + 1), :]
            fk[c, pl.ds(aligned(above * 192), 64), :] = src[QK + 64 * c : QK + 64 * (c + 1), :]
        fh[pl.ds(aligned(W + above * (20 * W)), 96), :] = src[QH : QH + 96, :]
        fc[pl.ds(aligned(4 * W + above * (17 * W)), 24), :] = src[QC : QC + 24, :]
        for q in range(6):
            fx[q, pl.ds(aligned(above * 24), 8), :] = src[QX + 8 * q : QX + 8 * (q + 1), :]
        fa[pl.ds(aligned(above * 24), 8), :] = src[QA : QA + 8, :]

    row = lax.broadcasted_iota(jnp.int32, (32, Z), 0)
    lane = lax.broadcasted_iota(jnp.int32, (32, Z), 1)
    code = fa[...]
    base = 16 * ((row - 8 + 16) // 2 - 8 + 3) + ((lane - 5 + 16) // 2 - 8 + 3) - 1
    inside = (row >= 3) & (row <= 28) & (lane < 26) & (code > 0.0)
    fa[...] = jnp.where(inside, code + base.astype(F32), -1.0)
    sub = lax.broadcasted_iota(jnp.int32, (W, Z), 0)
    lane_w = lax.broadcasted_iota(jnp.int32, (W, Z), 1)
    here = lane_w == 3 * (sub % 8) + sub // 8 + 1
    index = fa[...]
    spread = [jnp.where(here, jnp.broadcast_to(index[e + 3 : e + 4, :], (W, Z)), 0.0) for e in range(ROWS)]
    spread += [jnp.where(lane == 25 * q, index, 0.0) for q in range(2)]
    spread = jnp.concatenate(spread, axis=0).astype(jnp.bfloat16)
    columns = 2 * Z
    wide = jnp.dot(spread, jnp.ones((Z, columns), jnp.bfloat16), preferred_element_type=F32)
    count_nodes = ROWS * W + 64
    which = lax.broadcasted_iota(jnp.int32, (count_nodes, columns), 1).astype(F32)
    hot = (wide == which).astype(F32).astype(jnp.bfloat16)
    for c in range(3):
        table = fk[c]
        high = table.astype(jnp.bfloat16)
        rest = table - high.astype(F32)
        mid = rest.astype(jnp.bfloat16)
        low = (rest - mid.astype(F32)).astype(jnp.bfloat16)
        moved = (
            jnp.dot(hot, high, preferred_element_type=F32)
            + jnp.dot(hot, mid, preferred_element_type=F32)
            + jnp.dot(hot, low, preferred_element_type=F32)
        )
        fd[c] = fd[c] + moved[0 : ROWS * W]
        for q in range(2):
            fx[2 * c + q] = fx[2 * c + q] + moved[ROWS * W + 32 * q : ROWS * W + 32 * (q + 1)]

    place_s = lax.broadcasted_iota(jnp.int32, (8, Z), 0)
    place_z = lax.broadcasted_iota(jnp.int32, (8, Z), 1)
    first_z = place_z == 0
    last_z = place_z == Z - 1
    cols = [plane * B + 3 * place_s + l - 4 for l in range(3)]
    total_y = n_plane * B
    total_x = n_slab * B
    col_in = [((g >= 0) & (g < total_y)).astype(F32) for g in cols]

    def boxed(src, c, e, extra):
        v0, v1, v2 = (src[c, pl.ds(aligned(e * W + 8 * l), 8), :] for l in range(3))
        up = pltpu.roll(v2, 1, 0)
        down = pltpu.roll(v0, 7, 0)
        if extra is not None:
            up = jnp.where(place_s == 0, extra[2 * c, pl.ds(e + 3, 1), :], up)
            down = jnp.where(place_s == 7, extra[2 * c + 1, pl.ds(e + 3, 1), :], down)
        pair = v0 + v1
        out = []
        for t in (pair + up, pair + v2, v1 + v2 + down):
            out.append(
                t
                + jnp.where(first_z, 0.0, pltpu.roll(t, 1, 1))
                + jnp.where(last_z, 0.0, pltpu.roll(t, Z - 1, 1))
            )
        return out

    def stage(src, dst, extra, first, last, keep, gain):
        def sums(e):
            return [boxed(src, c, e, extra) for c in range(3)]

        def step(e, carry):
            before, mid = carry
            after = sums(e + 1)
            row_in = jnp.where((slab * B + e - 5 >= 0) & (slab * B + e - 5 < total_x), gain, 0.0)
            for l in range(3):
                at = pl.ds(aligned(e * W + 8 * l), 8)
                diagonal = 3.0 + fh[at, :]
                weight = col_in[l] * row_in
                for c in range(3):
                    here_v = src[c, at, :]
                    box = before[c][l] + mid[c][l] + after[c][l]
                    r = fr[c, at, :] - (diagonal * here_v - box * (1.0 / 3.0))
                    fr[c, at, :] = r
                    if keep is None:
                        dst[c, at, :] = weight * r
                    else:
                        dst[c, at, :] = keep * here_v + weight * r
            return mid, after

        lax.fori_loop(first, last + 1, step, (sums(first - 1), sums(first)), unroll=2)

    sigma = THETA / DELTA_C
    rho = 1.0 / sigma
    steps = []
    for _ in range(DEGREE - 1):
        rho_new = 1.0 / (2.0 * sigma - rho)
        steps.append((rho_new * rho, 2.0 * rho_new / DELTA_C))
        rho = rho_new
    stage(fd, d0, fx, 1, 24, None, 1.0 / THETA)
    stage(d0, d1, None, 2, 23, *steps[0])
    stage(d1, d2, None, 3, 22, *steps[1])
    stage(d2, d3, None, 4, 21, *steps[2])

    def gather_row(e, carry):
        for c in range(3):
            v = []
            for l in range(3):
                at = pl.ds(aligned(e * W + 8 * l), 8)
                u = fd[c, at, :] + d0[c, at, :] + d1[c, at, :] + d2[c, at, :] + d3[c, at, :]
                st[c * 18 + e - 4, pl.ds(l, 8, stride=3), :] = u
                v.append(u)
            nxt = [v[1], v[2], pltpu.roll(v[0], 7, 0)]
            for l in range(3):
                both = v[l] + nxt[l]
                diff = nxt[l] - v[l]
                both_z = pltpu.roll(both, Z - 1, 1)
                at = pl.ds(aligned((e - 4) * W + 8 * l), 8)
                gx[c, at, :] = both + both_z
                gx[3 + c, at, :] = diff + pltpu.roll(diff, Z - 1, 1)
                gx[6 + c, at, :] = both_z - both
        return carry

    lax.fori_loop(4, 22, gather_row, 0, unroll=2)

    col_ok = [((g >= 0) & (g <= total_y - 2) & (place_z <= Z - 2)).astype(F32) for g in cols]

    def element_row(n, carry):
        gi = slab * B + n - 1
        row_ok = jnp.where((gi >= 0) & (gi <= total_x - 2), 1.0, 0.0)
        made = []
        for l in range(3):
            at = pl.ds(aligned(n * W + 8 * l), 8)
            at_next = pl.ds(aligned((n + 1) * W + 8 * l), 8)
            grad = [[None] * 3 for _ in range(3)]
            for c in range(3):
                grad[c][0] = gx[c, at_next, :] - gx[c, at, :]
                grad[c][1] = gx[3 + c, at_next, :] + gx[3 + c, at, :]
                grad[c][2] = gx[6 + c, at_next, :] + gx[6 + c, at, :]
            exx = 0.25 * grad[0][0]
            eyy = 0.25 * grad[1][1]
            ezz = 0.25 * grad[2][2]
            exy = 0.125 * (grad[0][1] + grad[1][0])
            eyz = 0.125 * (grad[1][2] + grad[2][1])
            ezx = 0.125 * (grad[2][0] + grad[0][2])
            trace = exx + eyy + ezz
            third = trace * (1.0 / 3.0)
            sxx, syy, szz = exx - third, eyy - third, ezz - third
            equiv = (2.0 / 3.0) * (
                sxx * sxx + syy * syy + szz * szz + 2.0 * (exy * exy + eyz * eyz + ezx * ezx)
            )
            ok = col_ok[l] * row_ok
            cons = fc[pl.ds(aligned((n + 4) * W + 8 * l), 8), :]
            power = jnp.exp(((0.15 - 1.0) / 2.0) * jnp.log(0.01 + 3.0 * equiv))
            visc = (2.0 * ok) * (cons * power)
            bulk = (4.0 * ok) * trace
            sig = [
                jnp.where(ok > 0.0, visc * sxx + bulk, 0.0),
                jnp.where(ok > 0.0, visc * syy + bulk, 0.0),
                jnp.where(ok > 0.0, visc * szz + bulk, 0.0),
                jnp.where(ok > 0.0, visc * exy, 0.0),
                jnp.where(ok > 0.0, visc * eyz, 0.0),
                jnp.where(ok > 0.0, visc * ezx, 0.0),
            ]
            norm = (
                sig[0] * sig[0]
                + sig[1] * sig[1]
                + sig[2] * sig[2]
                + 2.0 * (sig[3] * sig[3] + sig[4] * sig[4] + sig[5] * sig[5])
            )
            made.append(sig + [norm])
        for q in range(7):
            a, b, c_ = made[0][q], made[1][q], made[2][q]
            for l, t in enumerate((a + pltpu.roll(c_, 1, 0), a + b, b + c_)):
                ey[q, pl.ds(aligned(n * W + 8 * l), 8), :] = t + pltpu.roll(t, 1, 1)
        return carry

    lax.fori_loop(0, 17, element_row, 0)

    half_z = jnp.where(first_z | last_z, 1.0, 0.5)
    col_half = [jnp.where((g == 0) | (g == total_y - 1), half_z, 0.5 * half_z) for g in cols]

    def node_row(i, carry):
        gi = slab * B + i
        row_half = jnp.where((gi == 0) | (gi == total_x - 1), 1.0, 0.5)
        for l in range(3):
            inverse = col_half[l] * row_half
            at = pl.ds(aligned(i * W + 8 * l), 8)
            at_next = pl.ds(aligned((i + 1) * W + 8 * l), 8)
            mean = [(ey[q, at, :] + ey[q, at_next, :]) * inverse for q in range(7)]
            norm = (
                mean[0] * mean[0]
                + mean[1] * mean[1]
                + mean[2] * mean[2]
                + 2.0 * (mean[3] * mean[3] + mean[4] * mean[4] + mean[5] * mean[5])
            )
            mean[6] = mean[6] - norm
            for q in range(7):
                st[54 + q * 16 + i, pl.ds(l, 8, stride=3), :] = mean[q]
        return carry

    lax.fori_loop(0, B, node_row, 0)

    def put(i, carry):
        for c in range(3):
            disp[c * 16 + i] = st[c * 18 + i + 1, 4:20, :]
        for q in range(6):
            rec[q * 16 + i] = st[54 + q * 16 + i, 4:20, :]
        ind[i] = st[54 + 96 + i, 4:20, :]
        return carry

    lax.fori_loop(0, B, put, 0, unroll=2)


def call(kernel, outs, args, scratch=(), aliases=None, cost=0):
    params = pltpu.CompilerParams(vmem_limit_bytes=48 * 1024 * 1024)
    whole = pl.BlockSpec(memory_space=pltpu.VMEM)
    return pl.pallas_call(
        kernel,
        out_shape=[jax.ShapeDtypeStruct(s, F32) for s in outs],
        in_specs=[whole] * len(args),
        out_specs=[whole] * len(outs),
        scratch_shapes=list(scratch),
        input_output_aliases=aliases or {},
        compiler_params=params,
        cost_estimate=pl.CostEstimate(flops=cost, bytes_accessed=2_000_000, transcendentals=0),
    )(*args)


def body(start_disp, load, shift, coarse, aggregate, consistency):
    start = start_disp.reshape(3 * B * B, Z)
    load2 = load.reshape(3 * B * B, Z)
    shift2 = shift.reshape(B * B, Z)
    cons2 = consistency.reshape(B * B, Z)
    coarse2 = coarse.reshape(3 * CB * CB, Z)
    n_plane = lax.axis_size("plane")
    n_slab = lax.axis_size("slab")
    forward = [(i, i + 1) for i in range(n_plane - 1)]
    backward = [(b, a) for a, b in forward]
    fwd, bwd = call(
        pack_kernel,
        [(PF_ROWS, Z), (PB_ROWS, Z)],
        [start, load2, shift2, cons2, coarse2, aggregate],
        cost=1_000_000,
    )
    low = lax.ppermute(fwd, "plane", forward)
    high = lax.ppermute(bwd, "plane", backward)
    own = call(
        own_kernel,
        [(48, W, Z), (48, W, Z), (16, W, Z), (16, W, Z), (24, 16, Z), (16, Z)],
        [
            start.reshape(48, B, Z),
            load2.reshape(48, B, Z),
            shift2.reshape(B, B, Z),
            cons2.reshape(B, B, Z),
            coarse2.reshape(24, CB, Z),
            fwd,
        ],
        cost=1_000_000,
    )
    flat = [a.reshape(-1, Z) for a in own]
    *ext, ex, on, off = call(
        join_kernel,
        [a.shape for a in flat] + [(6, 16, Z), (Q_ROWS, Z), (Q_ROWS, Z)],
        [low, high, *flat],
        aliases={2 + k: k for k in range(6)},
        cost=1_000_000,
    )
    pairs = [(i, i + 1) for i in range(1, n_slab - 1, 2)]
    pairs += [(b, a) for a, b in pairs]
    off = lax.ppermute(off, "slab", pairs)
    on = lax.all_gather(on, "slab", axis_index_groups=[[i, i + 1] for i in range(0, n_slab, 2)])
    field = (3, ROWS * W, Z)
    disp, rec, ind = call(
        smooth_kernel,
        [(48, B, Z), (96, B, Z), (B, B, Z)],
        [on, off, *ext, ex],
        scratch=[
            pltpu.VMEM(field, F32),
            pltpu.VMEM(field, F32),
            pltpu.VMEM((ROWS * W, Z), F32),
            pltpu.VMEM((ROWS * W, Z), F32),
            pltpu.VMEM((3, 256, Z), F32),
            pltpu.VMEM((6, 32, Z), F32),
            pltpu.VMEM((32, Z), F32),
            pltpu.VMEM(field, F32),
            pltpu.VMEM(field, F32),
            pltpu.VMEM(field, F32),
            pltpu.VMEM(field, F32),
            pltpu.VMEM((9, 18 * W, Z), F32),
            pltpu.VMEM((7, 17 * W, Z), F32),
            pltpu.VMEM((54 + 112, W, Z), F32),
        ],
        cost=50_000_000,
    )
    return disp.reshape(3, B, B, Z), rec.reshape(6, B, B, Z), ind


def solution(mesh):
    in_specs = (
        P(None, "slab", "plane", None),
        P(None, "slab", "plane", None),
        P("slab", "plane", None),
        P(None, "slab", "plane", None),
        P("slab", "plane"),
        P("slab", "plane", None),
    )
    out_specs = (
        P(None, "slab", "plane", None),
        P(None, "slab", "plane", None),
        P("slab", "plane", None),
    )
    return jax.shard_map(body, mesh=mesh, in_specs=in_specs, out_specs=out_specs, check_vma=False)
```

time: 148 us -> 63.1 us (0.43)
  the two profiles are of different devices: /device:TPU:121 before, /device:TPU:61 now
where the time goes in v1:
time: 63.1 us; the launch traced here: 62.8 us
  starting transfers between devices  28.5 us (45%)
  waiting for transfers between devices  13.6 us (22%)
  Pallas kernels  12.2 us (19%)
  local copies, waits for them, and re-layouts  5.38 us (9%)
  blocking collectives  2.55 us (4%)
  between operations  0.68 us (1%)
    pallas_call x4, Pallas kernels, call(): pl.pallas_call(kernel, out_shape=[jax.ShapeDtypeStruct(s, F32) for s in o...  12.2 us
    ppermute x1, starting transfers between devices, body(): high = lax.ppermute(bwd, 'plane', backward)  11.3 us
    ppermute x1, starting transfers between devices, body(): off = lax.ppermute(off, 'slab', pairs)  9.55 us
    ppermute x1, waiting for transfers between devices, body(): high = lax.ppermute(bwd, 'plane', backward)  8.44 us
    ppermute x1, starting transfers between devices, body(): low = lax.ppermute(fwd, 'plane', forward)  7.63 us
    unnamed x12, local copies, waits for them, and re-layouts  5.38 us
    ppermute x1, waiting for transfers between devices, body(): off = lax.ppermute(off, 'slab', pairs)  4.26 us
    all_gather x1, blocking collectives, body(): lax.all_gather(on, 'slab', axis_index_groups=[[i, i + 1] for i in range(0...  2.55 us
  transfers between devices with their start and end apart: 3, of which 3 were waited for; matrix products, arithmetic and copies ran while one was open for 0% of the time, Pallas kernels for 0%

profile of v1, /device:TPU:61, one launch (start us, length us, event | category | flops | bytes accessed | tf_op | source)
XLA Modules:
  0.0 62.8 jit_solution(346427089912712658)
XLA Ops:
  0.6 0.0 copy-start.5
  0.6 0.7 %copy-done.5 = s32[16,16]{1,0:T(8,128)S(1)} copy-done((s32[16,16]{1,0:T(8,128)S(1)}, s32[16,16]{1,0:T(8,128)}, u32[]{:S(2)}) %copy-start.5) | copy-done | bytes 1048
  1.3 0.0 copy-start
  1.3 1.0 %copy-done = f32[3,16,16,128]{3,2,1,0:T(8,128)S(1)} copy-done((f32[3,16,16,128]{3,2,1,0:T(8,128)S(1)}, f32[3,16,16,128]{3,2,1,0:T(8,128)}, u32[]{:S(2)}) %copy-start) | copy-done | bytes 393240
  2.3 0.0 copy-start.1
  2.3 1.0 %copy-done.1 = f32[3,16,16,128]{3,2,1,0:T(8,128)S(1)} copy-done((f32[3,16,16,128]{3,2,1,0:T(8,128)S(1)}, f32[3,16,16,128]{3,2,1,0:T(8,128)}, u32[]{:S(2)}) %copy-start.1) | copy-done | bytes 393240
  3.3 0.0 copy-start.2
  3.3 0.9 %copy-done.2 = f32[16,16,128]{2,1,0:T(8,128)S(1)} copy-done((f32[16,16,128]{2,1,0:T(8,128)S(1)}, f32[16,16,128]{2,1,0:T(8,128)}, u32[]{:S(2)}) %copy-start.2) | copy-done | bytes 131096
  4.2 0.0 copy-start.3
  4.2 0.9 %copy-done.3 = f32[16,16,128]{2,1,0:T(8,128)S(1)} copy-done((f32[16,16,128]{2,1,0:T(8,128)S(1)}, f32[16,16,128]{2,1,0:T(8,128)}, u32[]{:S(2)}) %copy-start.3) | copy-done | bytes 131096
  5.1 0.0 copy-start.4
  5.1 0.9 %copy-done.4 = f32[3,8,8,128]{3,2,1,0:T(8,128)S(1)} copy-done((f32[3,8,8,128]{3,2,1,0:T(8,128)S(1)}, f32[3,8,8,128]{3,2,1,0:T(8,128)}, u32[]{:S(2)}) %copy-start.4) | copy-done | bytes 98328
  6.0 0.2 shard_map.85
  6.2 7.6 %collective-permute-start = (f32[624,128]{1,0:T(8,128)S(1)}, f32[624,128]{1,0:T(8,128)S(1)}, u32[]{:S(2)}, u32[]{:S(2)}) collective-permute-start(f32[624,128]{1,0:T(8,128)S(1)} %get-tuple-element.23.fwd), channel_id=1, source_target_pairs={{0,1},{1,2},{2,3},{3,4},{4,5},{5,6},{6,7},{7,8},{8,9},{9,10},{10,1... | collective-permute-start | bytes 958472 | tf_op jit(solution)/shard_map/ppermute | solution.py:408
  13.8 11.3 %collective-permute-start.1 = (f32[608,128]{1,0:T(8,128)S(1)}, f32[608,128]{1,0:T(8,128)S(1)}, u32[]{:S(2)}, u32[]{:S(2)}) collective-permute-start(f32[608,128]{1,0:T(8,128)S(1)} %get-tuple-element.24), channel_id=1, source_target_pairs={{1,0},{2,1},{3,2},{4,3},{5,4},{6,5},{7,6},{8,7},{9,8},{10,9},{11,1... | collective-permute-start | bytes 933896 | tf_op jit(solution)/shard_map/ppermute | solution.py:409
  25.1 0.3 shard_map.86
  25.4 8.4 %collective-permute-done.1.high = f32[608,128]{1,0:T(8,128)S(1)} collective-permute-done((f32[608,128]{1,0:T(8,128)S(1)}, f32[608,128]{1,0:T(8,128)S(1)}, u32[]{:S(2)}, u32[]{:S(2)}) %collective-permute-start.1) | collective-permute-done | bytes 311328 | tf_op jit(solution)/shard_map/ppermute | solution.py:409
  33.9 0.9 %collective-permute-done.low = f32[624,128]{1,0:T(8,128)S(1)} collective-permute-done((f32[624,128]{1,0:T(8,128)S(1)}, f32[624,128]{1,0:T(8,128)S(1)}, u32[]{:S(2)}, u32[]{:S(2)}) %collective-permute-start) | collective-permute-done | bytes 319520 | tf_op jit(solution)/shard_map/ppermute | solution.py:408
  34.7 0.2 shard_map.87
  34.9 9.6 %collective-permute-start.2 = (f32[1016,128]{1,0:T(8,128)S(1)}, f32[1016,128]{1,0:T(8,128)S(1)}, u32[]{:S(2)}, u32[]{:S(2)}) collective-permute-start(f32[1016,128]{1,0:T(8,128)S(1)} %get-tuple-element.32), channel_id=1, source_target_pairs={{32,64},{96,128},{160,192},{224,256},{288,320},{352,384},{416,448}... | collective-permute-start | bytes 1560584 | tf_op jit(solution)/shard_map/ppermute | solution.py:433
  44.5 2.6 %all-gather = f32[2032,128]{1,0:T(8,128)S(1)} all-gather(f32[1016,128]{1,0:T(8,128)S(1)} %get-tuple-element.31), channel_id=2, replica_groups={{0,32},{64,96},{128,160},{192,224},{256,288},{320,352},{384,416},{448,4..., dimensions={0}, use_global_device_ids=true | all-gather | bytes 1560576 | tf_op jit(solution)/shard_map/all_gather | solution.py:434
  47.0 4.3 %collective-permute-done.2.off = f32[1016,128]{1,0:T(8,128)S(1)} collective-permute-done((f32[1016,128]{1,0:T(8,128)S(1)}, f32[1016,128]{1,0:T(8,128)S(1)}, u32[]{:S(2)}, u32[]{:S(2)}) %collective-permute-start.2) | collective-permute-done | bytes 520224 | tf_op jit(solution)/shard_map/ppermute | solution.py:433
  51.3 11.5 %shard_map.88 = (f32[48,16,128]{2,1,0:T(8,128)}, f32[96,16,128]{2,1,0:T(8,128)}, f32[16,16,128]{2,1,0:T(8,128)}) custom-call(f32[2,1016,128]{2,1,0:T(8,128)S(1)} %bitcast.16, f32[1016,128]{1,0:T(8,128)S(1)} %collective-permute-done.2.off, f32[1152,128]{1,0:T(8,128)S(1)} %get-tuple-element.33.es, f32[1152,128]{1,0:T(8,128)S(1)} %get-tuple-element.34.el, ...), custom_call_target="tpu_custom_call" | custom-call | flops 50000000 | bytes 2000000 | tf_op jit(solution)/shard_map/pallas_call | solution.py:380
Async XLA Ops:
  0.6 0.7 %copy-start.5 = (s32[16,16]{1,0:T(8,128)S(1)}, s32[16,16]{1,0:T(8,128)}, u32[]{:S(2)}) copy-start(s32[16,16]{1,0:T(8,128)} %agg.1) | copy-start | bytes 3076
  1.3 1.0 %copy-start = (f32[3,16,16,128]{3,2,1,0:T(8,128)S(1)}, f32[3,16,16,128]{3,2,1,0:T(8,128)}, u32[]{:S(2)}) copy-start(f32[3,16,16,128]{3,2,1,0:T(8,128)} %param.6) | copy-start | bytes 1179652
  2.3 1.0 %copy-start.1 = (f32[3,16,16,128]{3,2,1,0:T(8,128)S(1)}, f32[3,16,16,128]{3,2,1,0:T(8,128)}, u32[]{:S(2)}) copy-start(f32[3,16,16,128]{3,2,1,0:T(8,128)} %param.7) | copy-start | bytes 1179652
  3.3 0.9 %copy-start.2 = (f32[16,16,128]{2,1,0:T(8,128)S(1)}, f32[16,16,128]{2,1,0:T(8,128)}, u32[]{:S(2)}) copy-start(f32[16,16,128]{2,1,0:T(8,128)} %shift.1) | copy-start | bytes 393220
  4.2 0.9 %copy-start.3 = (f32[16,16,128]{2,1,0:T(8,128)S(1)}, f32[16,16,128]{2,1,0:T(8,128)}, u32[]{:S(2)}) copy-start(f32[16,16,128]{2,1,0:T(8,128)} %cons.1) | copy-start | bytes 393220
  5.1 0.9 %copy-start.4 = (f32[3,8,8,128]{3,2,1,0:T(8,128)S(1)}, f32[3,8,8,128]{3,2,1,0:T(8,128)}, u32[]{:S(2)}) copy-start(f32[3,8,8,128]{3,2,1,0:T(8,128)} %param.9) | copy-start | bytes 294916
  6.2 28.5 %collective-permute-start = (f32[624,128]{1,0:T(8,128)S(1)}, f32[624,128]{1,0:T(8,128)S(1)}, u32[]{:S(2)}, u32[]{:S(2)}) collective-permute-start(f32[624,128]{1,0:T(8,128)S(1)} %get-tuple-element.23.fwd), channel_id=1, source_target_pairs={{0,1},{1,2},{2,3},{3,4},{4,5},{5,6},{6,7},{7,8},{8,9},{9,10},{10,1... | collective-permute-start | bytes 958472 | tf_op jit(solution)/shard_map/ppermute | solution.py:408
  13.8 20.0 %collective-permute-start.1 = (f32[608,128]{1,0:T(8,128)S(1)}, f32[608,128]{1,0:T(8,128)S(1)}, u32[]{:S(2)}, u32[]{:S(2)}) collective-permute-start(f32[608,128]{1,0:T(8,128)S(1)} %get-tuple-element.24), channel_id=1, source_target_pairs={{1,0},{2,1},{3,2},{4,3},{5,4},{6,5},{7,6},{8,7},{9,8},{10,9},{11,1... | collective-permute-start | bytes 933896 | tf_op jit(solution)/shard_map/ppermute | solution.py:409
  34.9 16.4 %collective-permute-start.2 = (f32[1016,128]{1,0:T(8,128)S(1)}, f32[1016,128]{1,0:T(8,128)S(1)}, u32[]{:S(2)}, u32[]{:S(2)}) collective-permute-start(f32[1016,128]{1,0:T(8,128)S(1)} %get-tuple-element.32), channel_id=1, source_target_pairs={{32,64},{96,128},{160,192},{224,256},{288,320},{352,384},{416,448}... | collective-permute-start | bytes 1560584 | tf_op jit(solution)/shard_map/ppermute | solution.py:433

commit v2 on v1

--- a/solution.py
+++ b/solution.py
@@ -1,5 +1,3 @@
-import functools
-
 import jax
 import jax.numpy as jnp
 from jax import lax
@@ -17,12 +15,15 @@
 THETA = 4.5
 DELTA_C = 3.5
 F32 = jnp.float32
+FULL = 60 * 1024 * 1024
 
 PS, PL_, PH, PK, PA, PC = 0, 240, 432, 496, 592, 608
 PF_ROWS, PB_ROWS = 624, 608
 
 QS, QL, QH, QC, QK, QX, QA = 0, 360, 648, 744, 768, 960, 1008
 Q_ROWS = 1016
+TS, TL, TH, TK, TC, TA = 0, 152, 248, 280, 376, 384
+T_ROWS = 392
 
 
 def place(col):
@@ -30,7 +31,20 @@
     return (index % 3) * 8 + index // 3
 
 
-def pack_kernel(start, load, shift, cons, coarse, agg, fwd, bwd):
+def fetch(sources, targets, sems):
+    copies = [pltpu.make_async_copy(a, b, sems.at[k]) for k, (a, b) in enumerate(zip(sources, targets))]
+    for copy in copies:
+        copy.start()
+    for copy in copies:
+        copy.wait()
+
+
+def pack_kernel(
+    start_h, load_h, shift_h, cons_h, coarse_h, agg_h, fwd, bwd, code_o, start, load, shift, cons, coarse, agg, sems
+):
+    fetch(
+        (start_h, load_h, shift_h, cons_h, coarse_h, agg_h), (start, load, shift, cons, coarse, agg), sems
+    )
     slab = lax.axis_index("slab")
     plane = lax.axis_index("plane")
     coarse_cols = CB * lax.axis_size("plane")
@@ -55,86 +69,91 @@
     step_a = value // coarse_cols - (slab * CB + lax.broadcasted_iota(jnp.int32, (B, B), 0) // 2) + 1
     step_b = value % coarse_cols - (plane * CB + lax.broadcasted_iota(jnp.int32, (B, B), 1) // 2) + 1
     code = (1 + 16 * step_a + step_b).astype(F32)
-    for out in (fwd, bwd):
-        out[PA : PA + 16, :] = jnp.zeros((16, Z), F32)
-        out[PA : PA + 16, 0:B] = code
+    for out, row in ((fwd, PA), (bwd, PA), (code_o, 0)):
+        out[row : row + 16, :] = jnp.zeros((16, Z), F32)
+        out[row : row + 16, 0:B] = code
 
 
 OWN = ((0, 2, 2, 5), (1, 1, 0, 6), (2, 1, 1, 5))
 
 
-def own_kernel(start, load, shift, cons, coarse, fwd, es, el, eh, ec, ek, ea):
-    def rows(ci, carry):
+def top_rows(top, src, c, rows, width, size):
+    return src[pl.ds(pl.multiple_of(c * rows * width + top * (rows * width - size), 8), size), :]
+
+
+def own_kernel(
+    start_h, load_h, shift_h, cons_h, coarse_h, code, es, el, eh, ec, ek, ea, off, start, load, shift, cons, coarse, sems
+):
+    fetch((start_h, load_h, shift_h, cons_h, coarse_h), (start, load, shift, cons, coarse), sems)
+
+    for ci in range(3 * B):
         for l, s0, j0, n in OWN:
-            for src, dst in ((start, es), (load, el)):
-                dst[ci, 8 * l + s0 : 8 * l + s0 + n, :] = src[ci, pl.ds(j0, n, stride=3), :]
-        return carry
-
-    lax.fori_loop(0, 3 * B, rows, 0, unroll=4)
-
-    def rows1(ci, carry):
-        for l, s0, j0, n in OWN:
-            for src, dst in ((shift, eh), (cons, ec)):
-                dst[ci, 8 * l + s0 : 8 * l + s0 + n, :] = src[ci, pl.ds(j0, n, stride=3), :]
-        return carry
-
-    lax.fori_loop(0, B, rows1, 0, unroll=4)
+            at = ci * W + 8 * l + s0
+            for src, dst in ((start, es), (load, el)) + (((shift, eh), (cons, ec)) if ci < B else ()):
+                dst[at : at + n, :] = src[pl.ds(ci * B + j0, n, stride=3), :]
     for ca in range(3 * CB):
-        ek[ca, 4:12, :] = coarse[ca]
-    ea[...] = pltpu.roll(fwd[PA : PA + 16, :], 5, 1)
-
-
-def join_kernel(low, high, es, el, eh, ec, ek, ea, es_o, el_o, eh_o, ec_o, ek_o, ea_o, ex_o, on, off):
-    del es, el, eh, ec, ek
+        ek[16 * ca + 4 : 16 * ca + 12, :] = coarse[8 * ca : 8 * ca + 8, :]
+    ea[...] = pltpu.roll(code[...], 5, 1)
+    top = lax.axis_index("slab") % 2
+    whole_rows(top, off, es, el, eh, ec, ek)
+
+
+def whole_rows(top, out, es, el, eh, ec, ek):
     for c in range(3):
-        for w in range(5):
-            row = PS + 16 * (5 * c + w)
-            if w > 0:
-                es_o[pl.ds(384 * c + place(w - 5), 16, stride=24), :] = low[row : row + 16, :]
-            else:
-                ex_o[2 * c] = low[row : row + 16, :]
-            if w < 4:
-                es_o[pl.ds(384 * c + place(16 + w), 16, stride=24), :] = high[row : row + 16, :]
-            else:
-                ex_o[2 * c + 1] = high[row : row + 16, :]
+        out[QS + 120 * c : QS + 120 * (c + 1), :] = top_rows(top, es, c, B, W, 120)
+        out[QL + 96 * c : QL + 96 * (c + 1), :] = top_rows(top, el, c, B, W, 96)
+        out[QK + 64 * c : QK + 64 * (c + 1), :] = top_rows(top, ek, c, CB, 16, 64)
+    out[QH : QH + 96, :] = top_rows(top, eh, 0, B, W, 96)
+    out[QC : QC + 24, :] = top_rows(top, ec, 0, B, W, 24)
+
+
+def halo_columns(low, high):
+    for side, src in ((0, low), (1, high)):
+        for c in range(3):
+            for w in range(5):
+                yield src, PS + 16 * (5 * c + w), "start", c, w - 5 + 21 * side
+            for w in range(4):
+                yield src, PL_ + 16 * (4 * c + w), "load", c, w - 4 + 20 * side
+                yield src, PK + 8 * (4 * c + w), "coarse", c, w + 12 * side
         for w in range(4):
-            row = PL_ + 16 * (4 * c + w)
-            el_o[pl.ds(384 * c + place(w - 4), 16, stride=24), :] = low[row : row + 16, :]
-            el_o[pl.ds(384 * c + place(16 + w), 16, stride=24), :] = high[row : row + 16, :]
-            row = PK + 8 * (4 * c + w)
-            ek_o[pl.ds(128 * c + w, 8, stride=16), :] = low[row : row + 8, :]
-            ek_o[pl.ds(128 * c + 12 + w, 8, stride=16), :] = high[row : row + 8, :]
-    for w in range(4):
-        row = PH + 16 * w
-        eh_o[pl.ds(place(w - 4), 16, stride=24), :] = low[row : row + 16, :]
-        eh_o[pl.ds(place(16 + w), 16, stride=24), :] = high[row : row + 16, :]
-    ec_o[pl.ds(place(-1), 16, stride=24), :] = low[PC : PC + 16, :]
+            yield src, PH + 16 * w, "shift", 0, w - 4 + 20 * side
+    yield low, PC, "cons", 0, -1
+
+
+def join_kernel(low, high, es, el, eh, ec, ek, ea, code_o, on, off):
     lane = lax.broadcasted_iota(jnp.int32, (B, Z), 1)
     left = pltpu.roll(low[PA : PA + 16, :], Z - 11, 1)
     right = pltpu.roll(high[PA : PA + 16, :], 21, 1)
     code = jnp.where(lane < 5, left, jnp.where(lane < 21, ea[...], jnp.where(lane < 26, right, 0.0)))
-    ea_o[...] = code
+    code_o[...] = code
     odd = lax.axis_index("slab") % 2
-    for out, top in ((on, 1 - odd), (off, odd)):
-        for c in range(3):
-            out[QS + 120 * c : QS + 120 * (c + 1), :] = es_o[
-                pl.ds(pl.multiple_of(384 * c + top * (11 * W), 8), 120), :
-            ]
-            out[QL + 96 * c : QL + 96 * (c + 1), :] = el_o[
-                pl.ds(pl.multiple_of(384 * c + top * (12 * W), 8), 96), :
-            ]
-            out[QK + 64 * c : QK + 64 * (c + 1), :] = ek_o[
-                pl.ds(pl.multiple_of(128 * c + top * 64, 8), 64), :
-            ]
-        out[QH : QH + 96, :] = eh_o[pl.ds(pl.multiple_of(top * (12 * W), 8), 96), :]
-        out[QC : QC + 24, :] = ec_o[pl.ds(pl.multiple_of(top * (15 * W), 8), 24), :]
-        for q in range(6):
-            out[QX + 8 * q : QX + 8 * (q + 1), :] = ex_o[q, pl.ds(pl.multiple_of(top * 8, 8), 8), :]
-        out[QA : QA + 8, :] = ea_o[pl.ds(pl.multiple_of(top * 8, 8), 8), :]
+    whole_rows(1 - odd, on, es, el, eh, ec, ek)
+    for on_top in (0, 1):
+
+        @pl.when(odd == 1 - on_top)
+        def _(on_top=on_top):
+            on[QA : QA + 8, :] = code[8 * on_top : 8 * on_top + 8, :]
+            off[TA : TA + 8, :] = code[8 * (1 - on_top) : 8 * (1 - on_top) + 8, :]
+            at = {"start": TS, "load": TL, "shift": TH, "coarse": TK, "cons": TC}
+            for src, row, kind, c, col in halo_columns(low, high):
+                rows = CB if kind == "coarse" else B
+                n = {"start": 5, "cons": 1}.get(kind, 4)
+                first_on = row + (rows - n) * on_top
+                first_off = row + (rows - n) * (1 - on_top)
+                off[at[kind] : at[kind] + n, :] = src[first_off : first_off + n, :]
+                at[kind] += n
+                if kind == "coarse":
+                    on[pl.ds(QK + 64 * c + col, n, stride=16), :] = src[first_on : first_on + n, :]
+                elif kind == "start" and col in (-5, 20):
+                    x = QX + 8 * (2 * c + (col > 0))
+                    on[x : x + 8, :] = src[row + 8 * on_top : row + 8 * on_top + 8, :]
+                else:
+                    base = {"start": QS + 120 * c, "load": QL + 96 * c, "shift": QH, "cons": QC}[kind]
+                    on[pl.ds(base + place(col), n, stride=W), :] = src[first_on : first_on + n, :]
 
 
 def smooth_kernel(
-    on, off, es, el, eh, ec, ek, ea, ex,
+    on, off, corner, low, high, es, el, eh, ec, ek, code_own,
     disp, rec, ind,
     fd, fr, fh, fc, fk, fx, fa, d0, d1, d2, d3, gx, ey, st,
 ):
@@ -153,9 +172,7 @@
         fk[c, 64:192, :] = ek[128 * c : 128 * (c + 1), :]
     fh[5 * W : 21 * W, :] = eh[...]
     fc[5 * W : 21 * W, :] = ec[...]
-    for q in range(6):
-        fx[q, 8:24, :] = ex[q]
-    fa[8:24, :] = ea[...]
+    fa[8:24, :] = code_own[...]
     for src, below in ((on.at[1 - odd], odd), (off, 1 - odd)):
         above = 1 - below
         for c in range(3):
@@ -164,9 +181,34 @@
             fk[c, pl.ds(aligned(above * 192), 64), :] = src[QK + 64 * c : QK + 64 * (c + 1), :]
         fh[pl.ds(aligned(W + above * (20 * W)), 96), :] = src[QH : QH + 96, :]
         fc[pl.ds(aligned(4 * W + above * (17 * W)), 24), :] = src[QC : QC + 24, :]
-        for q in range(6):
-            fx[q, pl.ds(aligned(above * 24), 8), :] = src[QX + 8 * q : QX + 8 * (q + 1), :]
-        fa[pl.ds(aligned(above * 24), 8), :] = src[QA : QA + 8, :]
+    for q in range(6):
+        fx[q, pl.ds(aligned((1 - odd) * 24), 8), :] = on[1 - odd, QX + 8 * q : QX + 8 * (q + 1), :]
+    fa[pl.ds(aligned((1 - odd) * 24), 8), :] = on[1 - odd, QA : QA + 8, :]
+    fa[pl.ds(aligned(odd * 24), 8), :] = corner[TA : TA + 8, :]
+
+    def put_column(kind, c, col, row, n, value):
+        if kind == "coarse":
+            fk[c, pl.ds(16 * (row + 4) + col, n, stride=16), :] = value
+        elif kind == "start" and col in (-5, 20):
+            fx[2 * c + (col > 0), row + 8 : row + 8 + n, :] = value
+        elif kind in ("start", "load"):
+            {"start": fd, "load": fr}[kind][c, pl.ds((row + 5) * W + place(col), n, stride=W), :] = value
+        else:
+            {"shift": fh, "cons": fc}[kind][pl.ds((row + 5) * W + place(col), n, stride=W), :] = value
+
+    for src, row, kind, c, col in halo_columns(low, high):
+        n = CB if kind == "coarse" else B
+        put_column(kind, c, col, 0, n, src[row : row + n, :])
+    for off_below in (0, 1):
+
+        @pl.when(odd == 1 - off_below)
+        def _(off_below=off_below):
+            at = {"start": TS, "load": TL, "shift": TH, "coarse": TK, "cons": TC}
+            for _, _, kind, c, col in halo_columns(low, high):
+                rows = CB if kind == "coarse" else B
+                n = {"start": 5, "cons": 1}.get(kind, 4)
+                put_column(kind, c, col, -n if off_below else rows, n, corner[at[kind] : at[kind] + n, :])
+                at[kind] += n
 
     row = lax.broadcasted_iota(jnp.int32, (32, Z), 0)
     lane = lax.broadcasted_iota(jnp.int32, (32, Z), 1)
@@ -250,7 +292,7 @@
                         dst[c, at, :] = keep * here_v + weight * r
             return mid, after
 
-        lax.fori_loop(first, last + 1, step, (sums(first - 1), sums(first)), unroll=2)
+        lax.fori_loop(first, last + 1, step, (sums(first - 1), sums(first)), unroll=8)
 
     sigma = THETA / DELTA_C
     rho = 1.0 / sigma
@@ -283,7 +325,7 @@
                 gx[6 + c, at, :] = both_z - both
         return carry
 
-    lax.fori_loop(4, 22, gather_row, 0, unroll=2)
+    lax.fori_loop(4, 22, gather_row, 0, unroll=6)
 
     col_ok = [((g >= 0) & (g <= total_y - 2) & (place_z <= Z - 2)).astype(F32) for g in cols]
 
@@ -337,7 +379,7 @@
                 ey[q, pl.ds(aligned(n * W + 8 * l), 8), :] = t + pltpu.roll(t, 1, 1)
         return carry
 
-    lax.fori_loop(0, 17, element_row, 0)
+    lax.fori_loop(0, 17, element_row, 0, unroll=4)
 
     half_z = jnp.where(first_z | last_z, 1.0, 0.5)
     col_half = [jnp.where((g == 0) | (g == total_y - 1), half_z, 0.5 * half_z) for g in cols]
@@ -361,7 +403,7 @@
                 st[54 + q * 16 + i, pl.ds(l, 8, stride=3), :] = mean[q]
         return carry
 
-    lax.fori_loop(0, B, node_row, 0)
+    lax.fori_loop(0, B, node_row, 0, unroll=4)
 
     def put(i, carry):
         for c in range(3):
@@ -374,85 +416,72 @@
     lax.fori_loop(0, B, put, 0, unroll=2)
 
 
-def call(kernel, outs, args, scratch=(), aliases=None, cost=0):
-    params = pltpu.CompilerParams(vmem_limit_bytes=48 * 1024 * 1024)
+def call(kernel, outs, args, scratch=(), in_hbm=0, cost=0, vmem=48 * 1024 * 1024):
     whole = pl.BlockSpec(memory_space=pltpu.VMEM)
     return pl.pallas_call(
         kernel,
         out_shape=[jax.ShapeDtypeStruct(s, F32) for s in outs],
-        in_specs=[whole] * len(args),
+        in_specs=[pl.BlockSpec(memory_space=pltpu.HBM)] * in_hbm + [whole] * (len(args) - in_hbm),
         out_specs=[whole] * len(outs),
         scratch_shapes=list(scratch),
-        input_output_aliases=aliases or {},
-        compiler_params=params,
+        compiler_params=pltpu.CompilerParams(vmem_limit_bytes=vmem),
         cost_estimate=pl.CostEstimate(flops=cost, bytes_accessed=2_000_000, transcendentals=0),
     )(*args)
 
 
+def landing(args):
+    return [pltpu.VMEM(a.shape, a.dtype) for a in args] + [pltpu.SemaphoreType.DMA((len(args),))]
+
+
 def body(start_disp, load, shift, coarse, aggregate, consistency):
-    start = start_disp.reshape(3 * B * B, Z)
-    load2 = load.reshape(3 * B * B, Z)
-    shift2 = shift.reshape(B * B, Z)
-    cons2 = consistency.reshape(B * B, Z)
-    coarse2 = coarse.reshape(3 * CB * CB, Z)
+    fields = [
+        start_disp.reshape(3 * B * B, Z),
+        load.reshape(3 * B * B, Z),
+        shift.reshape(B * B, Z),
+        consistency.reshape(B * B, Z),
+        coarse.reshape(3 * CB * CB, Z),
+    ]
     n_plane = lax.axis_size("plane")
     n_slab = lax.axis_size("slab")
     forward = [(i, i + 1) for i in range(n_plane - 1)]
     backward = [(b, a) for a, b in forward]
-    fwd, bwd = call(
+    swap = [(i, i + 1) for i in range(1, n_slab - 1, 2)]
+    swap += [(b, a) for a, b in swap]
+
+    args = [*fields, aggregate]
+    fwd, bwd, code = call(
         pack_kernel,
-        [(PF_ROWS, Z), (PB_ROWS, Z)],
-        [start, load2, shift2, cons2, coarse2, aggregate],
+        [(PF_ROWS, Z), (PB_ROWS, Z), (16, Z)],
+        args,
+        landing(args),
+        in_hbm=6,
         cost=1_000_000,
+        vmem=FULL,
     )
     low = lax.ppermute(fwd, "plane", forward)
     high = lax.ppermute(bwd, "plane", backward)
-    own = call(
+    *own, off = call(
         own_kernel,
-        [(48, W, Z), (48, W, Z), (16, W, Z), (16, W, Z), (24, 16, Z), (16, Z)],
-        [
-            start.reshape(48, B, Z),
-            load2.reshape(48, B, Z),
-            shift2.reshape(B, B, Z),
-            cons2.reshape(B, B, Z),
-            coarse2.reshape(24, CB, Z),
-            fwd,
-        ],
+        [(1152, Z), (1152, Z), (384, Z), (384, Z), (384, Z), (16, Z), (QX, Z)],
+        [*fields, code],
+        landing(fields),
+        in_hbm=5,
         cost=1_000_000,
     )
-    flat = [a.reshape(-1, Z) for a in own]
-    *ext, ex, on, off = call(
-        join_kernel,
-        [a.shape for a in flat] + [(6, 16, Z), (Q_ROWS, Z), (Q_ROWS, Z)],
-        [low, high, *flat],
-        aliases={2 + k: k for k in range(6)},
-        cost=1_000_000,
-    )
-    pairs = [(i, i + 1) for i in range(1, n_slab - 1, 2)]
-    pairs += [(b, a) for a, b in pairs]
-    off = lax.ppermute(off, "slab", pairs)
+    off = lax.ppermute(off, "slab", swap)
+    code, on, corner = call(
+        join_kernel, [(16, Z), (Q_ROWS, Z), (T_ROWS, Z)], [low, high, *own], cost=1_000_000
+    )
+    corner = lax.ppermute(corner, "slab", swap)
     on = lax.all_gather(on, "slab", axis_index_groups=[[i, i + 1] for i in range(0, n_slab, 2)])
     field = (3, ROWS * W, Z)
+    shapes = [field, field, (ROWS * W, Z), (ROWS * W, Z), (3, 256, Z), (6, 32, Z), (32, Z)]
+    shapes += [field] * 4 + [(9, 18 * W, Z), (7, 17 * W, Z), (54 + 112, W, Z)]
     disp, rec, ind = call(
         smooth_kernel,
         [(48, B, Z), (96, B, Z), (B, B, Z)],
-        [on, off, *ext, ex],
-        scratch=[
-            pltpu.VMEM(field, F32),
-            pltpu.VMEM(field, F32),
-            pltpu.VMEM((ROWS * W, Z), F32),
-            pltpu.VMEM((ROWS * W, Z), F32),
-            pltpu.VMEM((3, 256, Z), F32),
-            pltpu.VMEM((6, 32, Z), F32),
-            pltpu.VMEM((32, Z), F32),
-            pltpu.VMEM(field, F32),
-            pltpu.VMEM(field, F32),
-            pltpu.VMEM(field, F32),
-            pltpu.VMEM(field, F32),
-            pltpu.VMEM((9, 18 * W, Z), F32),
-            pltpu.VMEM((7, 17 * W, Z), F32),
-            pltpu.VMEM((54 + 112, W, Z), F32),
-        ],
+        [on, off, corner, low, high, *own[:5], code],
+        [pltpu.VMEM(shape, F32) for shape in shapes],
         cost=50_000_000,
     )
     return disp.reshape(3, B, B, Z), rec.reshape(6, B, B, Z), ind

time: 63.1 us -> 54.6 us (0.87)
  the two profiles are of different devices: /device:TPU:61 before, /device:TPU:502 now
where the time goes in v2:
time: 54.6 us; the launch traced here: 54.3 us
  waiting for transfers between devices  24 us (44%)
  starting transfers between devices  14.4 us (26%)
  Pallas kernels  12 us (22%)
  blocking collectives  2.55 us (5%)
  between operations  0.77 us (1%)
  local copies, waits for them, and re-layouts  0.71 us (1%)
    ppermute x1, waiting for transfers between devices, body(): high = lax.ppermute(bwd, 'plane', backward)  21.4 us
    pallas_call x4, Pallas kernels, call(): pl.pallas_call(kernel, out_shape=[jax.ShapeDtypeStruct(s, F32) for s in o...  12 us
    ppermute x1, starting transfers between devices, body(): low = lax.ppermute(fwd, 'plane', forward)  8.22 us
    all_gather x1, blocking collectives, body(): lax.all_gather(on, 'slab', axis_index_groups=[[i, i + 1] for i in range(0...  2.55 us
    ppermute x1, waiting for transfers between devices, body(): corner = lax.ppermute(corner, 'slab', swap)  2.55 us
    ppermute x1, starting transfers between devices, body(): off = lax.ppermute(off, 'slab', swap)  2.3 us
    ppermute x1, starting transfers between devices, body(): corner = lax.ppermute(corner, 'slab', swap)  1.92 us
    ppermute x1, starting transfers between devices, body(): high = lax.ppermute(bwd, 'plane', backward)  1.92 us
  transfers between devices with their start and end apart: 4, of which 2 were waited for; matrix products, arithmetic and copies ran while one was open for 0% of the time, Pallas kernels for 2%

profile of v2, /device:TPU:502, one launch (start us, length us, event | category | flops | bytes accessed | tf_op | source)
XLA Modules:
  0.0 54.3 jit_solution(6357605526788844363)
XLA Ops:
  0.6 0.0 copy-start
  0.6 0.0 copy-start.1
  0.7 0.0 copy-start.2
  0.7 0.0 copy-start.3
  0.7 0.0 copy-start.4
  0.7 2.3 %shard_map.85 = (f32[624,128]{1,0:T(8,128)}, f32[608,128]{1,0:T(8,128)}, f32[16,128]{1,0:T(8,128)}) custom-call(f32[768,128]{1,0:T(8,128)} %bitcast.9, f32[768,128]{1,0:T(8,128)} %bitcast.11, f32[256,128]{1,0:T(8,128)} %bitcast.13, f32[256,128]{1,0:T(8,128)} %bitcast.15, f32[192,128]{1,0:T(8,128)} %bitcast.17, s32[16,16]{1,0:T(8,128)} %agg_h.1), custom_call_target="tpu_custom_call" | custom-call | flops 1000000 | bytes 2000000 | tf_op jit(solution)/shard_map/pallas_call | solution.py:421
  3.0 8.2 %collective-permute-start = (f32[624,128]{1,0:T(8,128)}, f32[624,128]{1,0:T(8,128)S(1)}, u32[]{:S(2)}, u32[]{:S(2)}) collective-permute-start(f32[624,128]{1,0:T(8,128)} %get-tuple-element.19), channel_id=1, source_target_pairs={{0,1},{1,2},{2,3},{3,4},{4,5},{5,6},{6,7},{7,8},{8,9},{9,10},{10,1... | collective-permute-start | bytes 958472 | tf_op jit(solution)/shard_map/ppermute | solution.py:461
  11.2 1.9 %collective-permute-start.1 = (f32[608,128]{1,0:T(8,128)}, f32[608,128]{1,0:T(8,128)S(1)}, u32[]{:S(2)}, u32[]{:S(2)}) collective-permute-start(f32[608,128]{1,0:T(8,128)} %get-tuple-element.20), channel_id=1, source_target_pairs={{1,0},{2,1},{3,2},{4,3},{5,4},{6,5},{7,6},{8,7},{9,8},{10,9},{11,1... | collective-permute-start | bytes 933896 | tf_op jit(solution)/shard_map/ppermute | solution.py:462
  13.1 0.0 copy-done
  13.1 0.0 copy-done.1
  13.1 0.0 copy-done.2
  13.2 0.0 copy-done.3
  13.2 0.0 copy-start.5
  13.2 0.7 %copy-done.5 = f32[16,128]{1,0:T(8,128)S(1)} copy-done((f32[16,128]{1,0:T(8,128)S(1)}, f32[16,128]{1,0:T(8,128)}, u32[]{:S(2)}) %copy-start.5) | copy-done | bytes 8216
  13.9 1.1 %shard_map.86 = (f32[1152,128]{1,0:T(8,128)S(1)}, f32[1152,128]{1,0:T(8,128)S(1)}, f32[384,128]{1,0:T(8,128)S(1)}, f32[384,128]{1,0:T(8,128)S(1)}, f32[384,128]{...) custom-call(f32[768,128]{1,0:T(8,128)S(1)} %bitcast.10, f32[768,128]{1,0:T(8,128)S(1)} %bitcast.12, ...), custom_call_target="tpu_custom_call" | custom-call | flops 1000000 | bytes 2000000 | tf_op jit(solution)/shard_map/pallas_call | solution.py:421
  15.0 2.3 %collective-permute-start.2 = (f32[960,128]{1,0:T(8,128)S(1)}, f32[960,128]{1,0:T(8,128)S(1)}, u32[]{:S(2)}, u32[]{:S(2)}) collective-permute-start(f32[960,128]{1,0:T(8,128)S(1)} %get-tuple-element.29), channel_id=1, source_target_pairs={{32,64},{96,128},{160,192},{224,256},{288,320},{352,384},{416,448}... | collective-permute-start | bytes 1474568 | tf_op jit(solution)/shard_map/ppermute | solution.py:471
  17.3 21.4 %collective-permute-done.1.high = f32[608,128]{1,0:T(8,128)S(1)} collective-permute-done((f32[608,128]{1,0:T(8,128)}, f32[608,128]{1,0:T(8,128)S(1)}, u32[]{:S(2)}, u32[]{:S(2)}) %collective-permute-start.1) | collective-permute-done | bytes 311328 | tf_op jit(solution)/shard_map/ppermute | solution.py:462
  38.7 0.0 collective-permute-done.low
  38.7 0.2 shard_map.87
  38.9 1.9 %collective-permute-start.3 = (f32[392,128]{1,0:T(8,128)S(1)}, f32[392,128]{1,0:T(8,128)S(1)}, u32[]{:S(2)}, u32[]{:S(2)}) collective-permute-start(f32[392,128]{1,0:T(8,128)S(1)} %get-tuple-element.30), channel_id=1, source_target_pairs={{32,64},{96,128},{160,192},{224,256},{288,320},{352,384},{416,448}... | collective-permute-start | bytes 602120 | tf_op jit(solution)/shard_map/ppermute | solution.py:475
  40.8 2.6 %all-gather = f32[2032,128]{1,0:T(8,128)S(1)} all-gather(f32[1016,128]{1,0:T(8,128)S(1)} %get-tuple-element.28), channel_id=2, replica_groups={{0,32},{64,96},{128,160},{192,224},{256,288},{320,352},{384,416},{448,4..., dimensions={0}, use_global_device_ids=true | all-gather | bytes 1560576 | tf_op jit(solution)/shard_map/all_gather | solution.py:476
  43.4 0.0 collective-permute-done.2.off
  43.4 2.5 %collective-permute-done.3.corner = f32[392,128]{1,0:T(8,128)S(1)} collective-permute-done((f32[392,128]{1,0:T(8,128)S(1)}, f32[392,128]{1,0:T(8,128)S(1)}, u32[]{:S(2)}, u32[]{:S(2)}) %collective-permute-start.3) | collective-permute-done | bytes 200736 | tf_op jit(solution)/shard_map/ppermute | solution.py:475
  45.9 8.4 %shard_map.88 = (f32[48,16,128]{2,1,0:T(8,128)}, f32[96,16,128]{2,1,0:T(8,128)}, f32[16,16,128]{2,1,0:T(8,128)}) custom-call(f32[2,1016,128]{2,1,0:T(8,128)S(1)} %bitcast.8, f32[960,128]{1,0:T(8,128)S(1)} %collective-permute-done.2.off, f32[392,128]{1,0:T(8,128)S(1)} %collective-permute-done.3.corner, f32[624,128]{1,0:T(8,128)S(1)} %collective-permute-done.low, ...), custom_call_target="tpu_custom_call" | custom-call | flops 50000000 | bytes 2000000 | tf_op jit(solution)/shard_map/pallas_call | solution.py:421
  (1 shorter events, 0.0 us)
Async XLA Ops:
  0.6 12.5 %copy-start = (f32[3,16,16,128]{3,2,1,0:T(8,128)S(1)}, f32[3,16,16,128]{3,2,1,0:T(8,128)}, u32[]{:S(2)}) copy-start(f32[3,16,16,128]{3,2,1,0:T(8,128)} %param.6) | copy-start | bytes 1179652
  0.6 12.5 %copy-start.1 = (f32[3,16,16,128]{3,2,1,0:T(8,128)S(1)}, f32[3,16,16,128]{3,2,1,0:T(8,128)}, u32[]{:S(2)}) copy-start(f32[3,16,16,128]{3,2,1,0:T(8,128)} %param.7) | copy-start | bytes 1179652
  0.7 12.5 %copy-start.2 = (f32[16,16,128]{2,1,0:T(8,128)S(1)}, f32[16,16,128]{2,1,0:T(8,128)}, u32[]{:S(2)}) copy-start(f32[16,16,128]{2,1,0:T(8,128)} %param.8) | copy-start | bytes 393220
  0.7 12.5 %copy-start.3 = (f32[16,16,128]{2,1,0:T(8,128)S(1)}, f32[16,16,128]{2,1,0:T(8,128)}, u32[]{:S(2)}) copy-start(f32[16,16,128]{2,1,0:T(8,128)} %param.11) | copy-start | bytes 393220
  0.7 12.5 %copy-start.4 = (f32[3,8,8,128]{3,2,1,0:T(8,128)S(1)}, f32[3,8,8,128]{3,2,1,0:T(8,128)}, u32[]{:S(2)}) copy-start(f32[3,8,8,128]{3,2,1,0:T(8,128)} %param.9) | copy-start | bytes 294916
  3.0 35.8 %collective-permute-start = (f32[624,128]{1,0:T(8,128)}, f32[624,128]{1,0:T(8,128)S(1)}, u32[]{:S(2)}, u32[]{:S(2)}) collective-permute-start(f32[624,128]{1,0:T(8,128)} %get-tuple-element.19), channel_id=1, source_target_pairs={{0,1},{1,2},{2,3},{3,4},{4,5},{5,6},{6,7},{7,8},{8,9},{9,10},{10,1... | collective-permute-start | bytes 958472 | tf_op jit(solution)/shard_map/ppermute | solution.py:461
  11.2 27.5 %collective-permute-start.1 = (f32[608,128]{1,0:T(8,128)}, f32[608,128]{1,0:T(8,128)S(1)}, u32[]{:S(2)}, u32[]{:S(2)}) collective-permute-start(f32[608,128]{1,0:T(8,128)} %get-tuple-element.20), channel_id=1, source_target_pairs={{1,0},{2,1},{3,2},{4,3},{5,4},{6,5},{7,6},{8,7},{9,8},{10,9},{11,1... | collective-permute-start | bytes 933896 | tf_op jit(solution)/shard_map/ppermute | solution.py:462
  13.2 0.7 %copy-start.5 = (f32[16,128]{1,0:T(8,128)S(1)}, f32[16,128]{1,0:T(8,128)}, u32[]{:S(2)}) copy-start(f32[16,128]{1,0:T(8,128)} %get-tuple-element.21.code) | copy-start | bytes 24580
  15.0 28.4 %collective-permute-start.2 = (f32[960,128]{1,0:T(8,128)S(1)}, f32[960,128]{1,0:T(8,128)S(1)}, u32[]{:S(2)}, u32[]{:S(2)}) collective-permute-start(f32[960,128]{1,0:T(8,128)S(1)} %get-tuple-element.29), channel_id=1, source_target_pairs={{32,64},{96,128},{160,192},{224,256},{288,320},{352,384},{416,448}... | collective-permute-start | bytes 1474568 | tf_op jit(solution)/shard_map/ppermute | solution.py:471
  38.9 7.0 %collective-permute-start.3 = (f32[392,128]{1,0:T(8,128)S(1)}, f32[392,128]{1,0:T(8,128)S(1)}, u32[]{:S(2)}, u32[]{:S(2)}) collective-permute-start(f32[392,128]{1,0:T(8,128)S(1)} %get-tuple-element.30), channel_id=1, source_target_pairs={{32,64},{96,128},{160,192},{224,256},{288,320},{352,384},{416,448}... | collective-permute-start | bytes 602120 | tf_op jit(solution)/shard_map/ppermute | solution.py:475

commit v3 on v2

--- a/solution.py
+++ b/solution.py
@@ -20,8 +20,8 @@
 PS, PL_, PH, PK, PA, PC = 0, 240, 432, 496, 592, 608
 PF_ROWS, PB_ROWS = 624, 608
 
-QS, QL, QH, QC, QK, QX, QA = 0, 360, 648, 744, 768, 960, 1008
-Q_ROWS = 1016
+QS, QL, QH, QC, QK = 0, 360, 648, 744, 768
+Q_ROWS = 960
 TS, TL, TH, TK, TC, TA = 0, 152, 248, 280, 376, 384
 T_ROWS = 392
 
@@ -35,28 +35,56 @@
     copies = [pltpu.make_async_copy(a, b, sems.at[k]) for k, (a, b) in enumerate(zip(sources, targets))]
     for copy in copies:
         copy.start()
-    for copy in copies:
-        copy.wait()
+    return copies
 
 
 def pack_kernel(
-    start_h, load_h, shift_h, cons_h, coarse_h, agg_h, fwd, bwd, code_o, start, load, shift, cons, coarse, agg, sems
+    start_h, load_h, shift_h, cons_h, coarse_h, agg_h, fwd_h, bwd_h, code_o,
+    start, load, shift, cons, coarse, agg, sems, fwd, bwd, sems_out,
 ):
-    fetch(
-        (start_h, load_h, shift_h, cons_h, coarse_h, agg_h), (start, load, shift, cons, coarse, agg), sems
-    )
     slab = lax.axis_index("slab")
     plane = lax.axis_index("plane")
     coarse_cols = CB * lax.axis_size("plane")
+    arrived = fetch(
+        (agg_h, start_h, load_h, shift_h, coarse_h, cons_h), (agg, start, load, shift, coarse, cons), sems
+    )
+    sent = []
+
+    def send(first, last):
+        for scratch, out in ((fwd, fwd_h), (bwd, bwd_h)):
+            size = min(last, scratch.shape[0]) - first
+            if size > 0:
+                at = pl.ds(first, size)
+                copy = pltpu.make_async_copy(scratch.at[at], out.at[at], sems_out.at[len(sent)])
+                copy.start()
+                sent.append(copy)
+
+    arrived[0].wait()
+    value = agg[...]
+    step_a = value // coarse_cols - (slab * CB + lax.broadcasted_iota(jnp.int32, (B, B), 0) // 2) + 1
+    step_b = value % coarse_cols - (plane * CB + lax.broadcasted_iota(jnp.int32, (B, B), 1) // 2) + 1
+    code = (1 + 16 * step_a + step_b).astype(F32)
+    for out, row in ((fwd, PA), (bwd, PA), (code_o, 0)):
+        out[row : row + 16, :] = jnp.zeros((16, Z), F32)
+        out[row : row + 16, 0:B] = code
+    arrived[1].wait()
     for c in range(3):
         for w in range(5):
             row = PS + 16 * (5 * c + w)
             fwd[row : row + 16, :] = start[pl.ds(256 * c + 11 + w, 16, stride=16), :]
             bwd[row : row + 16, :] = start[pl.ds(256 * c + w, 16, stride=16), :]
+    send(PS, PL_)
+    arrived[2].wait()
+    for c in range(3):
         for w in range(4):
             row = PL_ + 16 * (4 * c + w)
             fwd[row : row + 16, :] = load[pl.ds(256 * c + 12 + w, 16, stride=16), :]
             bwd[row : row + 16, :] = load[pl.ds(256 * c + w, 16, stride=16), :]
+    send(PL_, PH)
+    for copy in arrived[3:]:
+        copy.wait()
+    for c in range(3):
+        for w in range(4):
             row = PK + 8 * (4 * c + w)
             fwd[row : row + 8, :] = coarse[pl.ds(64 * c + 4 + w, 8, stride=8), :]
             bwd[row : row + 8, :] = coarse[pl.ds(64 * c + w, 8, stride=8), :]
@@ -65,13 +93,9 @@
         fwd[row : row + 16, :] = shift[pl.ds(12 + w, 16, stride=16), :]
         bwd[row : row + 16, :] = shift[pl.ds(w, 16, stride=16), :]
     fwd[PC : PC + 16, :] = cons[pl.ds(15, 16, stride=16), :]
-    value = agg[...]
-    step_a = value // coarse_cols - (slab * CB + lax.broadcasted_iota(jnp.int32, (B, B), 0) // 2) + 1
-    step_b = value % coarse_cols - (plane * CB + lax.broadcasted_iota(jnp.int32, (B, B), 1) // 2) + 1
-    code = (1 + 16 * step_a + step_b).astype(F32)
-    for out, row in ((fwd, PA), (bwd, PA), (code_o, 0)):
-        out[row : row + 16, :] = jnp.zeros((16, Z), F32)
-        out[row : row + 16, 0:B] = code
+    send(PH, PF_ROWS)
+    for copy in sent:
+        copy.wait()
 
 
 OWN = ((0, 2, 2, 5), (1, 1, 0, 6), (2, 1, 1, 5))
@@ -82,9 +106,11 @@
 
 
 def own_kernel(
-    start_h, load_h, shift_h, cons_h, coarse_h, code, es, el, eh, ec, ek, ea, off, start, load, shift, cons, coarse, sems
+    start_h, load_h, shift_h, cons_h, coarse_h, code, es, el, eh, ec, ek, ea, on, off,
+    start, load, shift, cons, coarse, sems,
 ):
-    fetch((start_h, load_h, shift_h, cons_h, coarse_h), (start, load, shift, cons, coarse), sems)
+    for copy in fetch((start_h, load_h, shift_h, cons_h, coarse_h), (start, load, shift, cons, coarse), sems):
+        copy.wait()
 
     for ci in range(3 * B):
         for l, s0, j0, n in OWN:
@@ -94,8 +120,9 @@
     for ca in range(3 * CB):
         ek[16 * ca + 4 : 16 * ca + 12, :] = coarse[8 * ca : 8 * ca + 8, :]
     ea[...] = pltpu.roll(code[...], 5, 1)
-    top = lax.axis_index("slab") % 2
-    whole_rows(top, off, es, el, eh, ec, ek)
+    odd = lax.axis_index("slab") % 2
+    for out, top in ((on, 1 - odd), (off, odd)):
+        whole_rows(top, out, es, el, eh, ec, ek)
 
 
 def whole_rows(top, out, es, el, eh, ec, ek):
@@ -120,40 +147,34 @@
     yield low, PC, "cons", 0, -1
 
 
-def join_kernel(low, high, es, el, eh, ec, ek, ea, code_o, on, off):
+def corner_columns(low, high):
+    at = {"start": TS, "load": TL, "shift": TH, "coarse": TK, "cons": TC}
+    for src, row, kind, c, col in halo_columns(low, high):
+        n = {"start": 5, "cons": 1}.get(kind, 4)
+        yield src, row, kind, c, col, at[kind], n
+        at[kind] += n
+
+
+def join_kernel(low, high, ea, code_o, on, off):
     lane = lax.broadcasted_iota(jnp.int32, (B, Z), 1)
     left = pltpu.roll(low[PA : PA + 16, :], Z - 11, 1)
     right = pltpu.roll(high[PA : PA + 16, :], 21, 1)
     code = jnp.where(lane < 5, left, jnp.where(lane < 21, ea[...], jnp.where(lane < 26, right, 0.0)))
     code_o[...] = code
     odd = lax.axis_index("slab") % 2
-    whole_rows(1 - odd, on, es, el, eh, ec, ek)
     for on_top in (0, 1):
 
         @pl.when(odd == 1 - on_top)
         def _(on_top=on_top):
-            on[QA : QA + 8, :] = code[8 * on_top : 8 * on_top + 8, :]
-            off[TA : TA + 8, :] = code[8 * (1 - on_top) : 8 * (1 - on_top) + 8, :]
-            at = {"start": TS, "load": TL, "shift": TH, "coarse": TK, "cons": TC}
-            for src, row, kind, c, col in halo_columns(low, high):
-                rows = CB if kind == "coarse" else B
-                n = {"start": 5, "cons": 1}.get(kind, 4)
-                first_on = row + (rows - n) * on_top
-                first_off = row + (rows - n) * (1 - on_top)
-                off[at[kind] : at[kind] + n, :] = src[first_off : first_off + n, :]
-                at[kind] += n
-                if kind == "coarse":
-                    on[pl.ds(QK + 64 * c + col, n, stride=16), :] = src[first_on : first_on + n, :]
-                elif kind == "start" and col in (-5, 20):
-                    x = QX + 8 * (2 * c + (col > 0))
-                    on[x : x + 8, :] = src[row + 8 * on_top : row + 8 * on_top + 8, :]
-                else:
-                    base = {"start": QS + 120 * c, "load": QL + 96 * c, "shift": QH, "cons": QC}[kind]
-                    on[pl.ds(base + place(col), n, stride=W), :] = src[first_on : first_on + n, :]
+            for out, top in ((on, on_top), (off, 1 - on_top)):
+                out[TA : TA + 8, :] = code[8 * top : 8 * top + 8, :]
+                for src, row, kind, _, _, at, n in corner_columns(low, high):
+                    first = row + ((CB if kind == "coarse" else B) - n) * top
+                    out[at : at + n, :] = src[first : first + n, :]
 
 
 def smooth_kernel(
-    on, off, corner, low, high, es, el, eh, ec, ek, code_own,
+    on, off, on_corner, off_corner, low, high, es, el, eh, ec, ek, code_own,
     disp, rec, ind,
     fd, fr, fh, fc, fk, fx, fa, d0, d1, d2, d3, gx, ey, st,
 ):
@@ -181,10 +202,8 @@
             fk[c, pl.ds(aligned(above * 192), 64), :] = src[QK + 64 * c : QK + 64 * (c + 1), :]
         fh[pl.ds(aligned(W + above * (20 * W)), 96), :] = src[QH : QH + 96, :]
         fc[pl.ds(aligned(4 * W + above * (17 * W)), 24), :] = src[QC : QC + 24, :]
-    for q in range(6):
-        fx[q, pl.ds(aligned((1 - odd) * 24), 8), :] = on[1 - odd, QX + 8 * q : QX + 8 * (q + 1), :]
-    fa[pl.ds(aligned((1 - odd) * 24), 8), :] = on[1 - odd, QA : QA + 8, :]
-    fa[pl.ds(aligned(odd * 24), 8), :] = corner[TA : TA + 8, :]
+    fa[pl.ds(aligned((1 - odd) * 24), 8), :] = on_corner[1 - odd, TA : TA + 8, :]
+    fa[pl.ds(aligned(odd * 24), 8), :] = off_corner[TA : TA + 8, :]
 
     def put_column(kind, c, col, row, n, value):
         if kind == "coarse":
@@ -203,12 +222,10 @@
 
         @pl.when(odd == 1 - off_below)
         def _(off_below=off_below):
-            at = {"start": TS, "load": TL, "shift": TH, "coarse": TK, "cons": TC}
-            for _, _, kind, c, col in halo_columns(low, high):
-                rows = CB if kind == "coarse" else B
-                n = {"start": 5, "cons": 1}.get(kind, 4)
-                put_column(kind, c, col, -n if off_below else rows, n, corner[at[kind] : at[kind] + n, :])
-                at[kind] += n
+            for corner, below in ((on_corner.at[off_below], 1 - off_below), (off_corner, off_below)):
+                for _, _, kind, c, col, at, n in corner_columns(low, high):
+                    first = -n if below else (CB if kind == "coarse" else B)
+                    put_column(kind, c, col, first, n, corner[at : at + n, :])
 
     row = lax.broadcasted_iota(jnp.int32, (32, Z), 0)
     lane = lax.broadcasted_iota(jnp.int32, (32, Z), 1)
@@ -416,13 +433,14 @@
     lax.fori_loop(0, B, put, 0, unroll=2)
 
 
-def call(kernel, outs, args, scratch=(), in_hbm=0, cost=0, vmem=48 * 1024 * 1024):
+def call(kernel, outs, args, scratch=(), in_hbm=0, out_hbm=0, cost=0, vmem=48 * 1024 * 1024):
+    hbm = pl.BlockSpec(memory_space=pltpu.HBM)
     whole = pl.BlockSpec(memory_space=pltpu.VMEM)
     return pl.pallas_call(
         kernel,
         out_shape=[jax.ShapeDtypeStruct(s, F32) for s in outs],
-        in_specs=[pl.BlockSpec(memory_space=pltpu.HBM)] * in_hbm + [whole] * (len(args) - in_hbm),
-        out_specs=[whole] * len(outs),
+        in_specs=[hbm] * in_hbm + [whole] * (len(args) - in_hbm),
+        out_specs=[hbm] * out_hbm + [whole] * (len(outs) - out_hbm),
         scratch_shapes=list(scratch),
         compiler_params=pltpu.CompilerParams(vmem_limit_bytes=vmem),
         cost_estimate=pl.CostEstimate(flops=cost, bytes_accessed=2_000_000, transcendentals=0),
@@ -453,34 +471,43 @@
         pack_kernel,
         [(PF_ROWS, Z), (PB_ROWS, Z), (16, Z)],
         args,
-        landing(args),
+        [
+            *landing(args),
+            pltpu.VMEM((PF_ROWS, Z), F32),
+            pltpu.VMEM((PB_ROWS, Z), F32),
+            pltpu.SemaphoreType.DMA((6,)),
+        ],
         in_hbm=6,
+        out_hbm=2,
         cost=1_000_000,
         vmem=FULL,
     )
     low = lax.ppermute(fwd, "plane", forward)
     high = lax.ppermute(bwd, "plane", backward)
-    *own, off = call(
+    *own, on, off = call(
         own_kernel,
-        [(1152, Z), (1152, Z), (384, Z), (384, Z), (384, Z), (16, Z), (QX, Z)],
+        [(1152, Z), (1152, Z), (384, Z), (384, Z), (384, Z), (16, Z), (Q_ROWS, Z), (Q_ROWS, Z)],
         [*fields, code],
         landing(fields),
         in_hbm=5,
         cost=1_000_000,
     )
+    cores = [[i, i + 1] for i in range(0, n_slab, 2)]
     off = lax.ppermute(off, "slab", swap)
-    code, on, corner = call(
-        join_kernel, [(16, Z), (Q_ROWS, Z), (T_ROWS, Z)], [low, high, *own], cost=1_000_000
-    )
-    corner = lax.ppermute(corner, "slab", swap)
-    on = lax.all_gather(on, "slab", axis_index_groups=[[i, i + 1] for i in range(0, n_slab, 2)])
+    on = lax.all_gather(on, "slab", axis_index_groups=cores)
+    low, high, on = lax.optimization_barrier((low, high, on))
+    code, on_corner, off_corner = call(
+        join_kernel, [(16, Z), (T_ROWS, Z), (T_ROWS, Z)], [low, high, own[5]], cost=1_000_000
+    )
+    off_corner = lax.ppermute(off_corner, "slab", swap)
+    on_corner = lax.all_gather(on_corner, "slab", axis_index_groups=cores)
     field = (3, ROWS * W, Z)
     shapes = [field, field, (ROWS * W, Z), (ROWS * W, Z), (3, 256, Z), (6, 32, Z), (32, Z)]
     shapes += [field] * 4 + [(9, 18 * W, Z), (7, 17 * W, Z), (54 + 112, W, Z)]
     disp, rec, ind = call(
         smooth_kernel,
         [(48, B, Z), (96, B, Z), (B, B, Z)],
-        [on, off, corner, low, high, *own[:5], code],
+        [on, off, on_corner, off_corner, low, high, *own[:5], code],
         [pltpu.VMEM(shape, F32) for shape in shapes],
         cost=50_000_000,
     )

time: 54.6 us -> 55.1 us (level)
  waiting for transfers between devices: 24 us -> 21.9 us
  blocking collectives: 2.55 us -> 4.6 us
    ppermute x1, waiting for transfers between devices: 21.4 us -> 18.9 us  [body(): high = lax.ppermute(bwd, 'plane', backward)]
    all_gather x1 -> x2, blocking collectives: 2.55 us -> 4.6 us  [the longest x1 2.51 us: body(): on = lax.all_gather(on, 'slab', axis_index_groups=cores)]
where the time goes in v3:
time: 55.1 us; the launch traced here: 54.8 us
  waiting for transfers between devices  21.9 us (40%)
  starting transfers between devices  14.4 us (26%)
  Pallas kernels  12.5 us (23%)
  blocking collectives  4.6 us (8%)
  between operations  0.78 us (1%)
  local copies, waits for them, and re-layouts  0.71 us (1%)
    ppermute x1, waiting for transfers between devices, body(): high = lax.ppermute(bwd, 'plane', backward)  18.9 us
    pallas_call x4, Pallas kernels, call(): pl.pallas_call(kernel, out_shape=[jax.ShapeDtypeStruct(s, F32) for s in o...  12.5 us
    ppermute x1, starting transfers between devices, body(): low = lax.ppermute(fwd, 'plane', forward)  8.22 us
    ppermute x1, waiting for transfers between devices, body(): off_corner = lax.ppermute(off_corner, 'slab', swap)  3.01 us
    all_gather x1, blocking collectives, body(): on = lax.all_gather(on, 'slab', axis_index_groups=cores)  2.51 us
    ppermute x1, starting transfers between devices, body(): off = lax.ppermute(off, 'slab', swap)  2.3 us
    all_gather x1, blocking collectives, body(): on_corner = lax.all_gather(on_corner, 'slab', axis_index_groups=cores)  2.09 us
    ppermute x1, starting transfers between devices, body(): off_corner = lax.ppermute(off_corner, 'slab', swap)  1.92 us
  transfers between devices with their start and end apart: 4, of which 2 were waited for; matrix products, arithmetic and copies ran while one was open for 0% of the time, Pallas kernels for 2%

profile of v3, /device:TPU:502, one launch (start us, length us, event | category | flops | bytes accessed | tf_op | source)
XLA Modules:
  0.0 54.8 jit_solution(7080927230334718836)
XLA Ops:
  0.6 0.0 copy-start
  0.6 0.0 copy-start.1
  0.7 0.0 copy-start.2
  0.7 0.0 copy-start.3
  0.7 0.0 copy-start.4
  0.7 2.7 %shard_map.85 = (f32[624,128]{1,0:T(8,128)}, f32[608,128]{1,0:T(8,128)}, f32[16,128]{1,0:T(8,128)}) custom-call(f32[768,128]{1,0:T(8,128)} %bitcast.11, f32[768,128]{1,0:T(8,128)} %bitcast.13, f32[256,128]{1,0:T(8,128)} %bitcast.15, f32[256,128]{1,0:T(8,128)} %bitcast.17, f32[192,128]{1,0:T(8,128)} %bitcast.19, s32[16,16]{1,0:T(8,128)} %agg_h.1), custom_call_target="tpu_custom_call" | custom-call | flops 1000000 | bytes 2000000 | tf_op jit(solution)/shard_map/pallas_call | solution.py:439
  3.4 8.2 %collective-permute-start = (f32[624,128]{1,0:T(8,128)}, f32[624,128]{1,0:T(8,128)S(1)}, u32[]{:S(2)}, u32[]{:S(2)}) collective-permute-start(f32[624,128]{1,0:T(8,128)} %get-tuple-element.23), channel_id=1, source_target_pairs={{0,1},{1,2},{2,3},{3,4},{4,5},{5,6},{6,7},{7,8},{8,9},{9,10},{10,1... | collective-permute-start | bytes 958472 | tf_op jit(solution)/shard_map/ppermute | solution.py:485
  11.6 1.9 %collective-permute-start.1 = (f32[608,128]{1,0:T(8,128)}, f32[608,128]{1,0:T(8,128)S(1)}, u32[]{:S(2)}, u32[]{:S(2)}) collective-permute-start(f32[608,128]{1,0:T(8,128)} %get-tuple-element.24), channel_id=1, source_target_pairs={{1,0},{2,1},{3,2},{4,3},{5,4},{6,5},{7,6},{8,7},{9,8},{10,9},{11,1... | collective-permute-start | bytes 933896 | tf_op jit(solution)/shard_map/ppermute | solution.py:486
  13.6 0.0 copy-done
  13.6 0.0 copy-done.1
  13.6 0.0 copy-done.2
  13.6 0.0 copy-start.5
  13.6 0.7 %copy-done.5 = f32[16,128]{1,0:T(8,128)S(1)} copy-done((f32[16,128]{1,0:T(8,128)S(1)}, f32[16,128]{1,0:T(8,128)}, u32[]{:S(2)}) %copy-start.5) | copy-done | bytes 8216
  14.3 1.2 %shard_map.86 = (f32[1152,128]{1,0:T(8,128)S(1)}, f32[1152,128]{1,0:T(8,128)S(1)}, f32[384,128]{1,0:T(8,128)S(1)}, f32[384,128]{1,0:T(8,128)S(1)}, f32[384,128]{...) custom-call(f32[768,128]{1,0:T(8,128)S(1)} %bitcast.12, ...), custom_call_target="tpu_custom_call" | custom-call | flops 1000000 | bytes 2000000 | tf_op jit(solution)/shard_map/pallas_call | solution.py:439
  15.5 2.3 %collective-permute-start.2 = (f32[960,128]{1,0:T(8,128)S(1)}, f32[960,128]{1,0:T(8,128)S(1)}, u32[]{:S(2)}, u32[]{:S(2)}) collective-permute-start(f32[960,128]{1,0:T(8,128)S(1)} %get-tuple-element.28), channel_id=1, source_target_pairs={{32,64},{96,128},{160,192},{224,256},{288,320},{352,384},{416,448}... | collective-permute-start | bytes 1474568 | tf_op jit(solution)/shard_map/ppermute | solution.py:496
  17.8 2.5 %all-gather = f32[1920,128]{1,0:T(8,128)S(1)} all-gather(f32[960,128]{1,0:T(8,128)S(1)} %get-tuple-element.26), channel_id=2, replica_groups={{0,32},{64,96},{128,160},{192,224},{256,288},{320,352},{384,416},{448,4..., dimensions={0}, use_global_device_ids=true | all-gather | bytes 1474560 | tf_op jit(solution)/shard_map/all_gather | solution.py:497
  20.3 18.9 %collective-permute-done.1.high = f32[608,128]{1,0:T(8,128)S(1)} collective-permute-done((f32[608,128]{1,0:T(8,128)}, f32[608,128]{1,0:T(8,128)S(1)}, u32[]{:S(2)}, u32[]{:S(2)}) %collective-permute-start.1) | collective-permute-done | bytes 311328 | tf_op jit(solution)/shard_map/ppermute | solution.py:486
  39.2 0.0 collective-permute-done.low
  39.2 0.1 shard_map.87
  39.3 1.9 %collective-permute-start.3 = (f32[392,128]{1,0:T(8,128)S(1)}, f32[392,128]{1,0:T(8,128)S(1)}, u32[]{:S(2)}, u32[]{:S(2)}) collective-permute-start(f32[392,128]{1,0:T(8,128)S(1)} %get-tuple-element.33), channel_id=1, source_target_pairs={{32,64},{96,128},{160,192},{224,256},{288,320},{352,384},{416,448}... | collective-permute-start | bytes 602120 | tf_op jit(solution)/shard_map/ppermute | solution.py:502
  41.2 2.1 %all-gather.1 = f32[784,128]{1,0:T(8,128)S(1)} all-gather(f32[392,128]{1,0:T(8,128)S(1)} %get-tuple-element.32), channel_id=3, replica_groups={{0,32},{64,96},{128,160},{192,224},{256,288},{320,352},{384,416},{448,4..., dimensions={0}, use_global_device_ids=true | all-gather | bytes 602112 | tf_op jit(solution)/shard_map/all_gather | solution.py:503
  43.3 0.0 collective-permute-done.2.off
  43.3 3.0 %collective-permute-done.3.off_corner = f32[392,128]{1,0:T(8,128)S(1)} collective-permute-done((f32[392,128]{1,0:T(8,128)S(1)}, f32[392,128]{1,0:T(8,128)S(1)}, u32[]{:S(2)}, u32[]{:S(2)}) %collective-permute-start.3) | collective-permute-done | bytes 200736 | tf_op jit(solution)/shard_map/ppermute | solution.py:502
  46.3 8.5 %shard_map.88 = (f32[48,16,128]{2,1,0:T(8,128)}, f32[96,16,128]{2,1,0:T(8,128)}, f32[16,16,128]{2,1,0:T(8,128)}) custom-call(f32[2,960,128]{2,1,0:T(8,128)S(1)} %bitcast.9, f32[960,128]{1,0:T(8,128)S(1)} %collective-permute-done.2.off, f32[2,392,128]{2,1,0:T(8,128)S(1)} %bitcast.10, f32[392,128]{1,0:T(8,128)S(1)} %collective-permute-done.3.off_corner, ...), custom_call_target="tpu_custom_call" | custom-call | flops 50000000 | bytes 2000000 | tf_op jit(solution)/shard_map/pallas_call | solution.py:439
  (2 shorter events, 0.0 us)
Async XLA Ops:
  0.6 12.9 %copy-start = (f32[3,16,16,128]{3,2,1,0:T(8,128)S(1)}, f32[3,16,16,128]{3,2,1,0:T(8,128)}, u32[]{:S(2)}) copy-start(f32[3,16,16,128]{3,2,1,0:T(8,128)} %param.6) | copy-start | bytes 1179652
  0.6 12.9 %copy-start.1 = (f32[3,16,16,128]{3,2,1,0:T(8,128)S(1)}, f32[3,16,16,128]{3,2,1,0:T(8,128)}, u32[]{:S(2)}) copy-start(f32[3,16,16,128]{3,2,1,0:T(8,128)} %param.7) | copy-start | bytes 1179652
  0.7 12.9 %copy-start.2 = (f32[16,16,128]{2,1,0:T(8,128)S(1)}, f32[16,16,128]{2,1,0:T(8,128)}, u32[]{:S(2)}) copy-start(f32[16,16,128]{2,1,0:T(8,128)} %param.8) | copy-start | bytes 393220
  0.7 12.9 %copy-start.3 = (f32[16,16,128]{2,1,0:T(8,128)S(1)}, f32[16,16,128]{2,1,0:T(8,128)}, u32[]{:S(2)}) copy-start(f32[16,16,128]{2,1,0:T(8,128)} %param.11) | copy-start | bytes 393220
  0.7 12.9 %copy-start.4 = (f32[3,8,8,128]{3,2,1,0:T(8,128)S(1)}, f32[3,8,8,128]{3,2,1,0:T(8,128)}, u32[]{:S(2)}) copy-start(f32[3,8,8,128]{3,2,1,0:T(8,128)} %param.9) | copy-start | bytes 294916
  3.4 35.8 %collective-permute-start = (f32[624,128]{1,0:T(8,128)}, f32[624,128]{1,0:T(8,128)S(1)}, u32[]{:S(2)}, u32[]{:S(2)}) collective-permute-start(f32[624,128]{1,0:T(8,128)} %get-tuple-element.23), channel_id=1, source_target_pairs={{0,1},{1,2},{2,3},{3,4},{4,5},{5,6},{6,7},{7,8},{8,9},{9,10},{10,1... | collective-permute-start | bytes 958472 | tf_op jit(solution)/shard_map/ppermute | solution.py:485
  11.6 27.5 %collective-permute-start.1 = (f32[608,128]{1,0:T(8,128)}, f32[608,128]{1,0:T(8,128)S(1)}, u32[]{:S(2)}, u32[]{:S(2)}) collective-permute-start(f32[608,128]{1,0:T(8,128)} %get-tuple-element.24), channel_id=1, source_target_pairs={{1,0},{2,1},{3,2},{4,3},{5,4},{6,5},{7,6},{8,7},{9,8},{10,9},{11,1... | collective-permute-start | bytes 933896 | tf_op jit(solution)/shard_map/ppermute | solution.py:486
  13.6 0.7 %copy-start.5 = (f32[16,128]{1,0:T(8,128)S(1)}, f32[16,128]{1,0:T(8,128)}, u32[]{:S(2)}) copy-start(f32[16,128]{1,0:T(8,128)} %get-tuple-element.25.code) | copy-start | bytes 24580
  15.5 27.9 %collective-permute-start.2 = (f32[960,128]{1,0:T(8,128)S(1)}, f32[960,128]{1,0:T(8,128)S(1)}, u32[]{:S(2)}, u32[]{:S(2)}) collective-permute-start(f32[960,128]{1,0:T(8,128)S(1)} %get-tuple-element.28), channel_id=1, source_target_pairs={{32,64},{96,128},{160,192},{224,256},{288,320},{352,384},{416,448}... | collective-permute-start | bytes 1474568 | tf_op jit(solution)/shard_map/ppermute | solution.py:496
  39.3 7.0 %collective-permute-start.3 = (f32[392,128]{1,0:T(8,128)S(1)}, f32[392,128]{1,0:T(8,128)S(1)}, u32[]{:S(2)}, u32[]{:S(2)}) collective-permute-start(f32[392,128]{1,0:T(8,128)S(1)} %get-tuple-element.33), channel_id=1, source_target_pairs={{32,64},{96,128},{160,192},{224,256},{288,320},{352,384},{416,448}... | collective-permute-start | bytes 602120 | tf_op jit(solution)/shard_map/ppermute | solution.py:502

commit v4 on v3

--- a/solution.py
+++ b/solution.py
@@ -18,7 +18,7 @@
 FULL = 60 * 1024 * 1024
 
 PS, PL_, PH, PK, PA, PC = 0, 240, 432, 496, 592, 608
-PF_ROWS, PB_ROWS = 624, 608
+P_ROWS = 624
 
 QS, QL, QH, QC, QK = 0, 360, 648, 744, 768
 Q_ROWS = 960
@@ -35,67 +35,58 @@
     copies = [pltpu.make_async_copy(a, b, sems.at[k]) for k, (a, b) in enumerate(zip(sources, targets))]
     for copy in copies:
         copy.start()
-    return copies
+    for copy in copies:
+        copy.wait()
+
+
+def by_side(first, second, run):
+    odd = lax.axis_index("plane") % 2
+    for side in (0, 1):
+
+        @pl.when(odd == side)
+        def _(side=side):
+            run(*((first, second) if side else (second, first)))
 
 
 def pack_kernel(
-    start_h, load_h, shift_h, cons_h, coarse_h, agg_h, fwd_h, bwd_h, code_o,
-    start, load, shift, cons, coarse, agg, sems, fwd, bwd, sems_out,
+    start_h, load_h, shift_h, cons_h, coarse_h, agg_h, first, second, code_o,
+    start, load, shift, cons, coarse, agg, sems,
 ):
     slab = lax.axis_index("slab")
     plane = lax.axis_index("plane")
     coarse_cols = CB * lax.axis_size("plane")
-    arrived = fetch(
-        (agg_h, start_h, load_h, shift_h, coarse_h, cons_h), (agg, start, load, shift, coarse, cons), sems
-    )
-    sent = []
-
-    def send(first, last):
-        for scratch, out in ((fwd, fwd_h), (bwd, bwd_h)):
-            size = min(last, scratch.shape[0]) - first
-            if size > 0:
-                at = pl.ds(first, size)
-                copy = pltpu.make_async_copy(scratch.at[at], out.at[at], sems_out.at[len(sent)])
-                copy.start()
-                sent.append(copy)
-
-    arrived[0].wait()
+    fetch(
+        (start_h, load_h, shift_h, cons_h, coarse_h, agg_h), (start, load, shift, cons, coarse, agg), sems
+    )
     value = agg[...]
     step_a = value // coarse_cols - (slab * CB + lax.broadcasted_iota(jnp.int32, (B, B), 0) // 2) + 1
     step_b = value % coarse_cols - (plane * CB + lax.broadcasted_iota(jnp.int32, (B, B), 1) // 2) + 1
     code = (1 + 16 * step_a + step_b).astype(F32)
-    for out, row in ((fwd, PA), (bwd, PA), (code_o, 0)):
+    for out, row in ((first, PA), (second, PA), (code_o, 0)):
         out[row : row + 16, :] = jnp.zeros((16, Z), F32)
         out[row : row + 16, 0:B] = code
-    arrived[1].wait()
-    for c in range(3):
-        for w in range(5):
-            row = PS + 16 * (5 * c + w)
-            fwd[row : row + 16, :] = start[pl.ds(256 * c + 11 + w, 16, stride=16), :]
-            bwd[row : row + 16, :] = start[pl.ds(256 * c + w, 16, stride=16), :]
-    send(PS, PL_)
-    arrived[2].wait()
-    for c in range(3):
+
+    def pack(bwd, fwd):
+        for c in range(3):
+            for w in range(5):
+                row = PS + 16 * (5 * c + w)
+                fwd[row : row + 16, :] = start[pl.ds(256 * c + 11 + w, 16, stride=16), :]
+                bwd[row : row + 16, :] = start[pl.ds(256 * c + w, 16, stride=16), :]
+            for w in range(4):
+                row = PL_ + 16 * (4 * c + w)
+                fwd[row : row + 16, :] = load[pl.ds(256 * c + 12 + w, 16, stride=16), :]
+                bwd[row : row + 16, :] = load[pl.ds(256 * c + w, 16, stride=16), :]
+                row = PK + 8 * (4 * c + w)
+                fwd[row : row + 8, :] = coarse[pl.ds(64 * c + 4 + w, 8, stride=8), :]
+                bwd[row : row + 8, :] = coarse[pl.ds(64 * c + w, 8, stride=8), :]
         for w in range(4):
-            row = PL_ + 16 * (4 * c + w)
-            fwd[row : row + 16, :] = load[pl.ds(256 * c + 12 + w, 16, stride=16), :]
-            bwd[row : row + 16, :] = load[pl.ds(256 * c + w, 16, stride=16), :]
-    send(PL_, PH)
-    for copy in arrived[3:]:
-        copy.wait()
-    for c in range(3):
-        for w in range(4):
-            row = PK + 8 * (4 * c + w)
-            fwd[row : row + 8, :] = coarse[pl.ds(64 * c + 4 + w, 8, stride=8), :]
-            bwd[row : row + 8, :] = coarse[pl.ds(64 * c + w, 8, stride=8), :]
-    for w in range(4):
-        row = PH + 16 * w
-        fwd[row : row + 16, :] = shift[pl.ds(12 + w, 16, stride=16), :]
-        bwd[row : row + 16, :] = shift[pl.ds(w, 16, stride=16), :]
-    fwd[PC : PC + 16, :] = cons[pl.ds(15, 16, stride=16), :]
-    send(PH, PF_ROWS)
-    for copy in sent:
-        copy.wait()
+            row = PH + 16 * w
+            fwd[row : row + 16, :] = shift[pl.ds(12 + w, 16, stride=16), :]
+            bwd[row : row + 16, :] = shift[pl.ds(w, 16, stride=16), :]
+        fwd[PC : PC + 16, :] = cons[pl.ds(15, 16, stride=16), :]
+        bwd[PC : PC + 16, :] = cons[pl.ds(0, 16, stride=16), :]
+
+    by_side(first, second, pack)
 
 
 OWN = ((0, 2, 2, 5), (1, 1, 0, 6), (2, 1, 1, 5))
@@ -109,8 +100,7 @@
     start_h, load_h, shift_h, cons_h, coarse_h, code, es, el, eh, ec, ek, ea, on, off,
     start, load, shift, cons, coarse, sems,
 ):
-    for copy in fetch((start_h, load_h, shift_h, cons_h, coarse_h), (start, load, shift, cons, coarse), sems):
-        copy.wait()
+    fetch((start_h, load_h, shift_h, cons_h, coarse_h), (start, load, shift, cons, coarse), sems)
 
     for ci in range(3 * B):
         for l, s0, j0, n in OWN:
@@ -155,26 +145,30 @@
         at[kind] += n
 
 
-def join_kernel(low, high, ea, code_o, on, off):
-    lane = lax.broadcasted_iota(jnp.int32, (B, Z), 1)
-    left = pltpu.roll(low[PA : PA + 16, :], Z - 11, 1)
-    right = pltpu.roll(high[PA : PA + 16, :], 21, 1)
-    code = jnp.where(lane < 5, left, jnp.where(lane < 21, ea[...], jnp.where(lane < 26, right, 0.0)))
-    code_o[...] = code
+def join_kernel(first, second, ea, code_o, on, off):
     odd = lax.axis_index("slab") % 2
-    for on_top in (0, 1):
-
-        @pl.when(odd == 1 - on_top)
-        def _(on_top=on_top):
-            for out, top in ((on, on_top), (off, 1 - on_top)):
-                out[TA : TA + 8, :] = code[8 * top : 8 * top + 8, :]
-                for src, row, kind, _, _, at, n in corner_columns(low, high):
-                    first = row + ((CB if kind == "coarse" else B) - n) * top
-                    out[at : at + n, :] = src[first : first + n, :]
+
+    def join(low, high):
+        lane = lax.broadcasted_iota(jnp.int32, (B, Z), 1)
+        left = pltpu.roll(low[PA : PA + 16, :], Z - 11, 1)
+        right = pltpu.roll(high[PA : PA + 16, :], 21, 1)
+        code = jnp.where(lane < 5, left, jnp.where(lane < 21, ea[...], jnp.where(lane < 26, right, 0.0)))
+        code_o[...] = code
+        for on_top in (0, 1):
+
+            @pl.when(odd == 1 - on_top)
+            def _(on_top=on_top):
+                for out, top in ((on, on_top), (off, 1 - on_top)):
+                    out[TA : TA + 8, :] = code[8 * top : 8 * top + 8, :]
+                    for src, row, kind, _, _, at, n in corner_columns(low, high):
+                        begin = row + ((CB if kind == "coarse" else B) - n) * top
+                        out[at : at + n, :] = src[begin : begin + n, :]
+
+    by_side(first, second, join)
 
 
 def smooth_kernel(
-    on, off, on_corner, off_corner, low, high, es, el, eh, ec, ek, code_own,
+    on, off, on_corner, off_corner, swap_first, swap_second, es, el, eh, ec, ek, code_own,
     disp, rec, ind,
     fd, fr, fh, fc, fk, fx, fa, d0, d1, d2, d3, gx, ey, st,
 ):
@@ -215,15 +209,18 @@
         else:
             {"shift": fh, "cons": fc}[kind][pl.ds((row + 5) * W + place(col), n, stride=W), :] = value
 
-    for src, row, kind, c, col in halo_columns(low, high):
-        n = CB if kind == "coarse" else B
-        put_column(kind, c, col, 0, n, src[row : row + n, :])
+    def put_columns(low, high):
+        for src, row, kind, c, col in halo_columns(low, high):
+            n = CB if kind == "coarse" else B
+            put_column(kind, c, col, 0, n, src[row : row + n, :])
+
+    by_side(swap_first, swap_second, put_columns)
     for off_below in (0, 1):
 
         @pl.when(odd == 1 - off_below)
         def _(off_below=off_below):
             for corner, below in ((on_corner.at[off_below], 1 - off_below), (off_corner, off_below)):
-                for _, _, kind, c, col, at, n in corner_columns(low, high):
+                for _, _, kind, c, col, at, n in corner_columns(None, None):
                     first = -n if below else (CB if kind == "coarse" else B)
                     put_column(kind, c, col, first, n, corner[at : at + n, :])
 
@@ -433,14 +430,14 @@
     lax.fori_loop(0, B, put, 0, unroll=2)
 
 
-def call(kernel, outs, args, scratch=(), in_hbm=0, out_hbm=0, cost=0, vmem=48 * 1024 * 1024):
+def call(kernel, outs, args, scratch=(), in_hbm=0, cost=0, vmem=48 * 1024 * 1024):
     hbm = pl.BlockSpec(memory_space=pltpu.HBM)
     whole = pl.BlockSpec(memory_space=pltpu.VMEM)
     return pl.pallas_call(
         kernel,
         out_shape=[jax.ShapeDtypeStruct(s, F32) for s in outs],
         in_specs=[hbm] * in_hbm + [whole] * (len(args) - in_hbm),
-        out_specs=[hbm] * out_hbm + [whole] * (len(outs) - out_hbm),
+        out_specs=[whole] * len(outs),
         scratch_shapes=list(scratch),
         compiler_params=pltpu.CompilerParams(vmem_limit_bytes=vmem),
         cost_estimate=pl.CostEstimate(flops=cost, bytes_accessed=2_000_000, transcendentals=0),
@@ -461,29 +458,23 @@
     ]
     n_plane = lax.axis_size("plane")
     n_slab = lax.axis_size("slab")
-    forward = [(i, i + 1) for i in range(n_plane - 1)]
-    backward = [(b, a) for a, b in forward]
-    swap = [(i, i + 1) for i in range(1, n_slab - 1, 2)]
-    swap += [(b, a) for a, b in swap]
+
+    def swaps(first, count):
+        pairs = [(i, i + 1) for i in range(first, count - 1, 2)]
+        return pairs + [(b, a) for a, b in pairs]
 
     args = [*fields, aggregate]
-    fwd, bwd, code = call(
+    first, second, code = call(
         pack_kernel,
-        [(PF_ROWS, Z), (PB_ROWS, Z), (16, Z)],
+        [(P_ROWS, Z), (P_ROWS, Z), (16, Z)],
         args,
-        [
-            *landing(args),
-            pltpu.VMEM((PF_ROWS, Z), F32),
-            pltpu.VMEM((PB_ROWS, Z), F32),
-            pltpu.SemaphoreType.DMA((6,)),
-        ],
+        landing(args),
         in_hbm=6,
-        out_hbm=2,
         cost=1_000_000,
         vmem=FULL,
     )
-    low = lax.ppermute(fwd, "plane", forward)
-    high = lax.ppermute(bwd, "plane", backward)
+    first = lax.ppermute(first, "plane", swaps(0, n_plane))
+    second = lax.ppermute(second, "plane", swaps(1, n_plane))
     *own, on, off = call(
         own_kernel,
         [(1152, Z), (1152, Z), (384, Z), (384, Z), (384, Z), (16, Z), (Q_ROWS, Z), (Q_ROWS, Z)],
@@ -493,13 +484,13 @@
         cost=1_000_000,
     )
     cores = [[i, i + 1] for i in range(0, n_slab, 2)]
-    off = lax.ppermute(off, "slab", swap)
+    off = lax.ppermute(off, "slab", swaps(1, n_slab))
     on = lax.all_gather(on, "slab", axis_index_groups=cores)
-    low, high, on = lax.optimization_barrier((low, high, on))
+    first, second, on = lax.optimization_barrier((first, second, on))
     code, on_corner, off_corner = call(
-        join_kernel, [(16, Z), (T_ROWS, Z), (T_ROWS, Z)], [low, high, own[5]], cost=1_000_000
-    )
-    off_corner = lax.ppermute(off_corner, "slab", swap)
+        join_kernel, [(16, Z), (T_ROWS, Z), (T_ROWS, Z)], [first, second, own[5]], cost=1_000_000
+    )
+    off_corner = lax.ppermute(off_corner, "slab", swaps(1, n_slab))
     on_corner = lax.all_gather(on_corner, "slab", axis_index_groups=cores)
     field = (3, ROWS * W, Z)
     shapes = [field, field, (ROWS * W, Z), (ROWS * W, Z), (3, 256, Z), (6, 32, Z), (32, Z)]
@@ -507,7 +498,7 @@
     disp, rec, ind = call(
         smooth_kernel,
         [(48, B, Z), (96, B, Z), (B, B, Z)],
-        [on, off, on_corner, off_corner, low, high, *own[:5], code],
+        [on, off, on_corner, off_corner, first, second, *own[:5], code],
         [pltpu.VMEM(shape, F32) for shape in shapes],
         cost=50_000_000,
     )

time: 55.1 us -> 55 us (level)
  the two profiles are of different devices: /device:TPU:502 before, /device:TPU:138 now
where the time goes in v4:
time: 55 us; the launch traced here: 54.7 us
  starting transfers between devices  24.6 us (45%)
  Pallas kernels  12.1 us (22%)
  waiting for transfers between devices  11.9 us (22%)
  blocking collectives  4.6 us (8%)
  between operations  0.78 us (1%)
  local copies, waits for them, and re-layouts  0.71 us (1%)
    pallas_call x4, Pallas kernels, call(): pl.pallas_call(kernel, out_shape=[jax.ShapeDtypeStruct(s, F32) for s in o...  12.1 us
    ppermute x1, starting transfers between devices, body(): second = lax.ppermute(second, 'plane', swaps(1, n_plane))  10.4 us
    ppermute x1, starting transfers between devices, body(): first = lax.ppermute(first, 'plane', swaps(0, n_plane))  7.92 us
    ppermute x1, waiting for transfers between devices, body(): second = lax.ppermute(second, 'plane', swaps(1, n_plane))  6.74 us
    ppermute x1, waiting for transfers between devices, body(): off_corner = lax.ppermute(off_corner, 'slab', swaps(1, n_slab))  5.12 us
    ppermute x1, starting transfers between devices, body(): off = lax.ppermute(off, 'slab', swaps(1, n_slab))  4.41 us
    all_gather x1, blocking collectives, body(): on = lax.all_gather(on, 'slab', axis_index_groups=cores)  2.51 us
    all_gather x1, blocking collectives, body(): on_corner = lax.all_gather(on_corner, 'slab', axis_index_groups=cores)  2.09 us
  transfers between devices with their start and end apart: 4, of which 2 were waited for; matrix products, arithmetic and copies ran while one was open for 0% of the time, Pallas kernels for 2%

profile of v4, /device:TPU:138, one launch (start us, length us, event | category | flops | bytes accessed | tf_op | source)
XLA Modules:
  0.0 54.7 jit_solution(15457819316975626240)
XLA Ops:
  0.6 0.0 copy-start
  0.6 0.0 copy-start.1
  0.7 0.0 copy-start.2
  0.7 0.0 copy-start.3
  0.7 0.0 copy-start.4
  0.7 2.4 %shard_map.85 = (f32[624,128]{1,0:T(8,128)}, f32[624,128]{1,0:T(8,128)}, f32[16,128]{1,0:T(8,128)}) custom-call(f32[768,128]{1,0:T(8,128)} %bitcast.11, f32[768,128]{1,0:T(8,128)} %bitcast.13, f32[256,128]{1,0:T(8,128)} %bitcast.15, f32[256,128]{1,0:T(8,128)} %bitcast.17, f32[192,128]{1,0:T(8,128)} %bitcast.19, s32[16,16]{1,0:T(8,128)} %agg_h.1), custom_call_target="tpu_custom_call" | custom-call | flops 1000000 | bytes 2000000 | tf_op jit(solution)/shard_map/pallas_call | solution.py:436
  3.1 7.9 %collective-permute-start = (f32[624,128]{1,0:T(8,128)}, f32[624,128]{1,0:T(8,128)S(1)}, u32[]{:S(2)}, u32[]{:S(2)}) collective-permute-start(f32[624,128]{1,0:T(8,128)} %get-tuple-element.23), channel_id=1, source_target_pairs={{0,1},{2,3},{4,5},{6,7},{8,9},{10,11},{12,13},{14,15},{16,17},{18,... | collective-permute-start | bytes 958472 | tf_op jit(solution)/shard_map/ppermute | solution.py:476
  11.0 10.4 %collective-permute-start.1 = (f32[624,128]{1,0:T(8,128)}, f32[624,128]{1,0:T(8,128)S(1)}, u32[]{:S(2)}, u32[]{:S(2)}) collective-permute-start(f32[624,128]{1,0:T(8,128)} %get-tuple-element.24), channel_id=1, source_target_pairs={{1,2},{3,4},{5,6},{7,8},{9,10},{11,12},{13,14},{15,16},{17,18},{19... | collective-permute-start | bytes 958472 | tf_op jit(solution)/shard_map/ppermute | solution.py:477
  21.4 0.0 copy-done
  21.4 0.0 copy-done.1
  21.4 0.0 copy-done.2
  21.4 0.0 copy-start.5
  21.4 0.7 %copy-done.5 = f32[16,128]{1,0:T(8,128)S(1)} copy-done((f32[16,128]{1,0:T(8,128)S(1)}, f32[16,128]{1,0:T(8,128)}, u32[]{:S(2)}) %copy-start.5) | copy-done | bytes 8216
  22.1 1.2 %shard_map.86 = (f32[1152,128]{1,0:T(8,128)S(1)}, f32[1152,128]{1,0:T(8,128)S(1)}, f32[384,128]{1,0:T(8,128)S(1)}, f32[384,128]{1,0:T(8,128)S(1)}, f32[384,128]{...) custom-call(f32[768,128]{1,0:T(8,128)S(1)} %bitcast.12, ...), custom_call_target="tpu_custom_call" | custom-call | flops 1000000 | bytes 2000000 | tf_op jit(solution)/shard_map/pallas_call | solution.py:436
  23.3 4.4 %collective-permute-start.2 = (f32[960,128]{1,0:T(8,128)S(1)}, f32[960,128]{1,0:T(8,128)S(1)}, u32[]{:S(2)}, u32[]{:S(2)}) collective-permute-start(f32[960,128]{1,0:T(8,128)S(1)} %get-tuple-element.28), channel_id=1, source_target_pairs={{32,64},{96,128},{160,192},{224,256},{288,320},{352,384},{416,448}... | collective-permute-start | bytes 1474568 | tf_op jit(solution)/shard_map/ppermute | solution.py:487
  27.7 2.5 %all-gather = f32[1920,128]{1,0:T(8,128)S(1)} all-gather(f32[960,128]{1,0:T(8,128)S(1)} %get-tuple-element.26), channel_id=2, replica_groups={{0,32},{64,96},{128,160},{192,224},{256,288},{320,352},{384,416},{448,4..., dimensions={0}, use_global_device_ids=true | all-gather | bytes 1474560 | tf_op jit(solution)/shard_map/all_gather | solution.py:488
  30.2 0.0 collective-permute-done.first.swap_first
  30.2 6.7 %collective-permute-done.1.second.swap_second = f32[624,128]{1,0:T(8,128)S(1)} collective-permute-done((f32[624,128]{1,0:T(8,128)}, f32[624,128]{1,0:T(8,128)S(1)}, u32[]{:S(2)}, u32[]{:S(2)}) %collective-permute-start.1) | collective-permute-done | bytes 319520 | tf_op jit(solution)/shard_map/ppermute | solution.py:477
  37.0 0.1 shard_map.87
  37.1 1.9 %collective-permute-start.3 = (f32[392,128]{1,0:T(8,128)S(1)}, f32[392,128]{1,0:T(8,128)S(1)}, u32[]{:S(2)}, u32[]{:S(2)}) collective-permute-start(f32[392,128]{1,0:T(8,128)S(1)} %get-tuple-element.33), channel_id=1, source_target_pairs={{32,64},{96,128},{160,192},{224,256},{288,320},{352,384},{416,448}... | collective-permute-start | bytes 602120 | tf_op jit(solution)/shard_map/ppermute | solution.py:493
  39.0 2.1 %all-gather.1 = f32[784,128]{1,0:T(8,128)S(1)} all-gather(f32[392,128]{1,0:T(8,128)S(1)} %get-tuple-element.32), channel_id=3, replica_groups={{0,32},{64,96},{128,160},{192,224},{256,288},{320,352},{384,416},{448,4..., dimensions={0}, use_global_device_ids=true | all-gather | bytes 602112 | tf_op jit(solution)/shard_map/all_gather | solution.py:494
  41.1 0.0 collective-permute-done.2.off
  41.1 5.1 %collective-permute-done.3.off_corner = f32[392,128]{1,0:T(8,128)S(1)} collective-permute-done((f32[392,128]{1,0:T(8,128)S(1)}, f32[392,128]{1,0:T(8,128)S(1)}, u32[]{:S(2)}, u32[]{:S(2)}) %collective-permute-start.3) | collective-permute-done | bytes 200736 | tf_op jit(solution)/shard_map/ppermute | solution.py:493
  46.2 8.5 %shard_map.88 = (f32[48,16,128]{2,1,0:T(8,128)}, f32[96,16,128]{2,1,0:T(8,128)}, f32[16,16,128]{2,1,0:T(8,128)}) custom-call(f32[2,960,128]{2,1,0:T(8,128)S(1)} %bitcast.9, f32[960,128]{1,0:T(8,128)S(1)} %collective-permute-done.2.off, f32[2,392,128]{2,1,0:T(8,128)S(1)} %bitcast.10, f32[392,128]{1,0:T(8,128)S(1)} %collective-permute-done.3.off_corner, ...), custom_call_target="tpu_custom_call" | custom-call | flops 50000000 | bytes 2000000 | tf_op jit(solution)/shard_map/pallas_call | solution.py:436
  (2 shorter events, 0.0 us)
Async XLA Ops:
  0.6 20.7 %copy-start = (f32[3,16,16,128]{3,2,1,0:T(8,128)S(1)}, f32[3,16,16,128]{3,2,1,0:T(8,128)}, u32[]{:S(2)}) copy-start(f32[3,16,16,128]{3,2,1,0:T(8,128)} %param.6) | copy-start | bytes 1179652
  0.6 20.7 %copy-start.1 = (f32[3,16,16,128]{3,2,1,0:T(8,128)S(1)}, f32[3,16,16,128]{3,2,1,0:T(8,128)}, u32[]{:S(2)}) copy-start(f32[3,16,16,128]{3,2,1,0:T(8,128)} %param.7) | copy-start | bytes 1179652
  0.7 20.7 %copy-start.2 = (f32[16,16,128]{2,1,0:T(8,128)S(1)}, f32[16,16,128]{2,1,0:T(8,128)}, u32[]{:S(2)}) copy-start(f32[16,16,128]{2,1,0:T(8,128)} %param.8) | copy-start | bytes 393220
  0.7 20.7 %copy-start.3 = (f32[16,16,128]{2,1,0:T(8,128)S(1)}, f32[16,16,128]{2,1,0:T(8,128)}, u32[]{:S(2)}) copy-start(f32[16,16,128]{2,1,0:T(8,128)} %param.11) | copy-start | bytes 393220
  0.7 20.7 %copy-start.4 = (f32[3,8,8,128]{3,2,1,0:T(8,128)S(1)}, f32[3,8,8,128]{3,2,1,0:T(8,128)}, u32[]{:S(2)}) copy-start(f32[3,8,8,128]{3,2,1,0:T(8,128)} %param.9) | copy-start | bytes 294916
  3.1 27.2 %collective-permute-start = (f32[624,128]{1,0:T(8,128)}, f32[624,128]{1,0:T(8,128)S(1)}, u32[]{:S(2)}, u32[]{:S(2)}) collective-permute-start(f32[624,128]{1,0:T(8,128)} %get-tuple-element.23), channel_id=1, source_target_pairs={{0,1},{2,3},{4,5},{6,7},{8,9},{10,11},{12,13},{14,15},{16,17},{18,... | collective-permute-start | bytes 958472 | tf_op jit(solution)/shard_map/ppermute | solution.py:476
  11.0 26.0 %collective-permute-start.1 = (f32[624,128]{1,0:T(8,128)}, f32[624,128]{1,0:T(8,128)S(1)}, u32[]{:S(2)}, u32[]{:S(2)}) collective-permute-start(f32[624,128]{1,0:T(8,128)} %get-tuple-element.24), channel_id=1, source_target_pairs={{1,2},{3,4},{5,6},{7,8},{9,10},{11,12},{13,14},{15,16},{17,18},{19... | collective-permute-start | bytes 958472 | tf_op jit(solution)/shard_map/ppermute | solution.py:477
  21.4 0.7 %copy-start.5 = (f32[16,128]{1,0:T(8,128)S(1)}, f32[16,128]{1,0:T(8,128)}, u32[]{:S(2)}) copy-start(f32[16,128]{1,0:T(8,128)} %get-tuple-element.25.code) | copy-start | bytes 24580
  23.3 17.8 %collective-permute-start.2 = (f32[960,128]{1,0:T(8,128)S(1)}, f32[960,128]{1,0:T(8,128)S(1)}, u32[]{:S(2)}, u32[]{:S(2)}) collective-permute-start(f32[960,128]{1,0:T(8,128)S(1)} %get-tuple-element.28), channel_id=1, source_target_pairs={{32,64},{96,128},{160,192},{224,256},{288,320},{352,384},{416,448}... | collective-permute-start | bytes 1474568 | tf_op jit(solution)/shard_map/ppermute | solution.py:487
  37.1 9.1 %collective-permute-start.3 = (f32[392,128]{1,0:T(8,128)S(1)}, f32[392,128]{1,0:T(8,128)S(1)}, u32[]{:S(2)}, u32[]{:S(2)}) collective-permute-start(f32[392,128]{1,0:T(8,128)S(1)} %get-tuple-element.33), channel_id=1, source_target_pairs={{32,64},{96,128},{160,192},{224,256},{288,320},{352,384},{416,448}... | collective-permute-start | bytes 602120 | tf_op jit(solution)/shard_map/ppermute | solution.py:493

commit v5 on v4

--- a/solution.py
+++ b/solution.py
@@ -19,6 +19,11 @@
 
 PS, PL_, PH, PK, PA, PC = 0, 240, 432, 496, 592, 608
 P_ROWS = 624
+US, UL, UH, UK, UC, UA = 0, 152, 248, 280, 376, 384
+U_ROWS = 400
+VS, VL, VH, VC = 0, 96, 192, 224
+V_ROWS = 240
+CORNER = {"start": 5, "load": 4, "shift": 4, "cons": 1, "coarse": 4}
 
 QS, QL, QH, QC, QK = 0, 360, 648, 744, 768
 Q_ROWS = 960
@@ -32,13 +37,53 @@
 
 
 def fetch(sources, targets, sems):
-    copies = [pltpu.make_async_copy(a, b, sems.at[k]) for k, (a, b) in enumerate(zip(sources, targets))]
+    copies = [pltpu.make_async_copy(a, b.at[0 : a.shape[0]], sems.at[k]) for k, (a, b) in enumerate(zip(sources, targets))]
     for copy in copies:
         copy.start()
     for copy in copies:
         copy.wait()
 
 
+class Whole:
+    def __init__(self, ref):
+        self.ref = ref
+        self.code = ref.at[PA : PA + 16]
+
+    def pieces(self, kind, c, w):
+        row = {"start": PS + 80 * c, "load": PL_ + 64 * c, "shift": PH, "cons": PC, "coarse": PK + 32 * c}[kind]
+        size = CB if kind == "coarse" else B
+        return [(self.ref, row + size * w, 0, size)]
+
+
+class Split:
+    def __init__(self, ends, middle):
+        self.ends = ends
+        self.middle = middle
+        self.code = ends.at[UA : UA + 16]
+
+    def pieces(self, kind, c, w):
+        n = CORNER[kind]
+        row = {"start": US + 50 * c, "load": UL + 32 * c, "shift": UH, "cons": UC, "coarse": UK + 32 * c}[kind]
+        row += 2 * n * w
+        if kind == "coarse":
+            return [(self.ends, row, 0, CB)]
+        between = {"start": VS + 30 * c, "load": VL + 32 * c, "shift": VH, "cons": VC}[kind]
+        size = B - 2 * n
+        return [
+            (self.ends, row, 0, n),
+            (self.ends, row + n, B - n, n),
+            (self.middle, between + size * w, n, size),
+        ]
+
+
+def corner(payload, kind, c, w, top):
+    n = CORNER[kind]
+    want = ((CB if kind == "coarse" else B) - n) * top
+    for ref, row, begin, size in payload.pieces(kind, c, w):
+        if begin <= want and want + n <= begin + size:
+            return ref[row + want - begin : row + want - begin + n, :]
+
+
 def by_side(first, second, run):
     odd = lax.axis_index("plane") % 2
     for side in (0, 1):
@@ -49,7 +94,7 @@
 
 
 def pack_kernel(
-    start_h, load_h, shift_h, cons_h, coarse_h, agg_h, first, second, code_o,
+    start_h, load_h, shift_h, cons_h, coarse_h, agg_h, first, ends, middle, code_o,
     start, load, shift, cons, coarse, agg, sems,
 ):
     slab = lax.axis_index("slab")
@@ -62,31 +107,22 @@
     step_a = value // coarse_cols - (slab * CB + lax.broadcasted_iota(jnp.int32, (B, B), 0) // 2) + 1
     step_b = value % coarse_cols - (plane * CB + lax.broadcasted_iota(jnp.int32, (B, B), 1) // 2) + 1
     code = (1 + 16 * step_a + step_b).astype(F32)
-    for out, row in ((first, PA), (second, PA), (code_o, 0)):
+    for out, row in ((first, PA), (ends, UA), (code_o, 0)):
         out[row : row + 16, :] = jnp.zeros((16, Z), F32)
         out[row : row + 16, 0:B] = code
 
-    def pack(bwd, fwd):
-        for c in range(3):
-            for w in range(5):
-                row = PS + 16 * (5 * c + w)
-                fwd[row : row + 16, :] = start[pl.ds(256 * c + 11 + w, 16, stride=16), :]
-                bwd[row : row + 16, :] = start[pl.ds(256 * c + w, 16, stride=16), :]
-            for w in range(4):
-                row = PL_ + 16 * (4 * c + w)
-                fwd[row : row + 16, :] = load[pl.ds(256 * c + 12 + w, 16, stride=16), :]
-                bwd[row : row + 16, :] = load[pl.ds(256 * c + w, 16, stride=16), :]
-                row = PK + 8 * (4 * c + w)
-                fwd[row : row + 8, :] = coarse[pl.ds(64 * c + 4 + w, 8, stride=8), :]
-                bwd[row : row + 8, :] = coarse[pl.ds(64 * c + w, 8, stride=8), :]
-        for w in range(4):
-            row = PH + 16 * w
-            fwd[row : row + 16, :] = shift[pl.ds(12 + w, 16, stride=16), :]
-            bwd[row : row + 16, :] = shift[pl.ds(w, 16, stride=16), :]
-        fwd[PC : PC + 16, :] = cons[pl.ds(15, 16, stride=16), :]
-        bwd[PC : PC + 16, :] = cons[pl.ds(0, 16, stride=16), :]
-
-    by_side(first, second, pack)
+    arrays = {"start": start, "load": load, "shift": shift, "cons": cons, "coarse": coarse}
+
+    def pack(below, above):
+        for payload, side in ((below, 1), (above, 0)):
+            for kind, c, w, col in side_columns(side):
+                size = CB if kind == "coarse" else B
+                own_col = col - size if side else col + size
+                column = arrays[kind][pl.ds(size * size * c + own_col, size, stride=size), :]
+                for ref, row, begin, n in payload.pieces(kind, c, w):
+                    ref[row : row + n, :] = column[begin : begin + n]
+
+    by_side(Whole(first), Split(ends, middle), pack)
 
 
 OWN = ((0, 2, 2, 5), (1, 1, 0, 6), (2, 1, 1, 5))
@@ -124,34 +160,34 @@
     out[QC : QC + 24, :] = top_rows(top, ec, 0, B, W, 24)
 
 
-def halo_columns(low, high):
-    for side, src in ((0, low), (1, high)):
-        for c in range(3):
-            for w in range(5):
-                yield src, PS + 16 * (5 * c + w), "start", c, w - 5 + 21 * side
-            for w in range(4):
-                yield src, PL_ + 16 * (4 * c + w), "load", c, w - 4 + 20 * side
-                yield src, PK + 8 * (4 * c + w), "coarse", c, w + 12 * side
+def side_columns(side):
+    for c in range(3):
+        for w in range(5):
+            yield "start", c, w, w - 5 + 21 * side
         for w in range(4):
-            yield src, PH + 16 * w, "shift", 0, w - 4 + 20 * side
-    yield low, PC, "cons", 0, -1
-
-
-def corner_columns(low, high):
+            yield "load", c, w, w - 4 + 20 * side
+            yield "coarse", c, w, w - 4 + 12 * side
+    for w in range(4):
+        yield "shift", 0, w, w - 4 + 20 * side
+    if side == 0:
+        yield "cons", 0, 0, -1
+
+
+def corner_columns():
     at = {"start": TS, "load": TL, "shift": TH, "coarse": TK, "cons": TC}
-    for src, row, kind, c, col in halo_columns(low, high):
-        n = {"start": 5, "cons": 1}.get(kind, 4)
-        yield src, row, kind, c, col, at[kind], n
-        at[kind] += n
-
-
-def join_kernel(first, second, ea, code_o, on, off):
+    for side in (0, 1):
+        for kind, c, w, col in side_columns(side):
+            yield side, kind, c, w, col, at[kind], CORNER[kind]
+            at[kind] += CORNER[kind]
+
+
+def join_kernel(first, ends, ea, code_o, on, off):
     odd = lax.axis_index("slab") % 2
 
     def join(low, high):
         lane = lax.broadcasted_iota(jnp.int32, (B, Z), 1)
-        left = pltpu.roll(low[PA : PA + 16, :], Z - 11, 1)
-        right = pltpu.roll(high[PA : PA + 16, :], 21, 1)
+        left = pltpu.roll(low.code[...], Z - 11, 1)
+        right = pltpu.roll(high.code[...], 21, 1)
         code = jnp.where(lane < 5, left, jnp.where(lane < 21, ea[...], jnp.where(lane < 26, right, 0.0)))
         code_o[...] = code
         for on_top in (0, 1):
@@ -160,15 +196,14 @@
             def _(on_top=on_top):
                 for out, top in ((on, on_top), (off, 1 - on_top)):
                     out[TA : TA + 8, :] = code[8 * top : 8 * top + 8, :]
-                    for src, row, kind, _, _, at, n in corner_columns(low, high):
-                        begin = row + ((CB if kind == "coarse" else B) - n) * top
-                        out[at : at + n, :] = src[begin : begin + n, :]
-
-    by_side(first, second, join)
+                    for side, kind, c, w, _, at, n in corner_columns():
+                        out[at : at + n, :] = corner((low, high)[side], kind, c, w, top)
+
+    by_side(Whole(first), Split(ends, None), join)
 
 
 def smooth_kernel(
-    on, off, on_corner, off_corner, swap_first, swap_second, es, el, eh, ec, ek, code_own,
+    on, off, on_corner, off_corner, first, ends, middle, es, el, eh, ec, ek, code_own,
     disp, rec, ind,
     fd, fr, fh, fc, fk, fx, fa, d0, d1, d2, d3, gx, ey, st,
 ):
@@ -201,7 +236,7 @@
 
     def put_column(kind, c, col, row, n, value):
         if kind == "coarse":
-            fk[c, pl.ds(16 * (row + 4) + col, n, stride=16), :] = value
+            fk[c, pl.ds(16 * (row + 4) + col + 4, n, stride=16), :] = value
         elif kind == "start" and col in (-5, 20):
             fx[2 * c + (col > 0), row + 8 : row + 8 + n, :] = value
         elif kind in ("start", "load"):
@@ -210,19 +245,20 @@
             {"shift": fh, "cons": fc}[kind][pl.ds((row + 5) * W + place(col), n, stride=W), :] = value
 
     def put_columns(low, high):
-        for src, row, kind, c, col in halo_columns(low, high):
-            n = CB if kind == "coarse" else B
-            put_column(kind, c, col, 0, n, src[row : row + n, :])
-
-    by_side(swap_first, swap_second, put_columns)
+        for payload, side in ((low, 0), (high, 1)):
+            for kind, c, w, col in side_columns(side):
+                for ref, row, begin, n in payload.pieces(kind, c, w):
+                    put_column(kind, c, col, begin, n, ref[row : row + n, :])
+
+    by_side(Whole(first), Split(ends, middle), put_columns)
     for off_below in (0, 1):
 
         @pl.when(odd == 1 - off_below)
         def _(off_below=off_below):
-            for corner, below in ((on_corner.at[off_below], 1 - off_below), (off_corner, off_below)):
-                for _, _, kind, c, col, at, n in corner_columns(None, None):
-                    first = -n if below else (CB if kind == "coarse" else B)
-                    put_column(kind, c, col, first, n, corner[at : at + n, :])
+            for src, below in ((on_corner.at[off_below], 1 - off_below), (off_corner, off_below)):
+                for _, kind, c, _, col, at, n in corner_columns():
+                    begin = -n if below else (CB if kind == "coarse" else B)
+                    put_column(kind, c, col, begin, n, src[at : at + n, :])
 
     row = lax.broadcasted_iota(jnp.int32, (32, Z), 0)
     lane = lax.broadcasted_iota(jnp.int32, (32, Z), 1)
@@ -243,7 +279,7 @@
     which = lax.broadcasted_iota(jnp.int32, (count_nodes, columns), 1).astype(F32)
     hot = (wide == which).astype(F32).astype(jnp.bfloat16)
     for c in range(3):
-        table = fk[c]
+        table = fk[c, 0:256, :]
         high = table.astype(jnp.bfloat16)
         rest = table - high.astype(F32)
         mid = rest.astype(jnp.bfloat16)
@@ -253,7 +289,7 @@
             + jnp.dot(hot, mid, preferred_element_type=F32)
             + jnp.dot(hot, low, preferred_element_type=F32)
         )
-        fd[c] = fd[c] + moved[0 : ROWS * W]
+        fd[c, 0 : ROWS * W, :] = fd[c, 0 : ROWS * W, :] + moved[0 : ROWS * W]
         for q in range(2):
             fx[2 * c + q] = fx[2 * c + q] + moved[ROWS * W + 32 * q : ROWS * W + 32 * (q + 1)]
 
@@ -444,8 +480,8 @@
     )(*args)
 
 
-def landing(args):
-    return [pltpu.VMEM(a.shape, a.dtype) for a in args] + [pltpu.SemaphoreType.DMA((len(args),))]
+def landing(args, more=0):
+    return [pltpu.VMEM((a.shape[0] + more, a.shape[1]), a.dtype) for a in args] + [pltpu.SemaphoreType.DMA((len(args),))]
 
 
 def body(start_disp, load, shift, coarse, aggregate, consistency):
@@ -464,9 +500,9 @@
         return pairs + [(b, a) for a, b in pairs]
 
     args = [*fields, aggregate]
-    first, second, code = call(
+    first, ends, middle, code = call(
         pack_kernel,
-        [(P_ROWS, Z), (P_ROWS, Z), (16, Z)],
+        [(P_ROWS, Z), (U_ROWS, Z), (V_ROWS, Z), (16, Z)],
         args,
         landing(args),
         in_hbm=6,
@@ -474,31 +510,34 @@
         vmem=FULL,
     )
     first = lax.ppermute(first, "plane", swaps(0, n_plane))
-    second = lax.ppermute(second, "plane", swaps(1, n_plane))
+    ends = lax.ppermute(ends, "plane", swaps(1, n_plane))
     *own, on, off = call(
         own_kernel,
         [(1152, Z), (1152, Z), (384, Z), (384, Z), (384, Z), (16, Z), (Q_ROWS, Z), (Q_ROWS, Z)],
         [*fields, code],
-        landing(fields),
+        landing(fields, 8),
         in_hbm=5,
         cost=1_000_000,
     )
     cores = [[i, i + 1] for i in range(0, n_slab, 2)]
     off = lax.ppermute(off, "slab", swaps(1, n_slab))
     on = lax.all_gather(on, "slab", axis_index_groups=cores)
-    first, second, on = lax.optimization_barrier((first, second, on))
+    middle = lax.ppermute(middle, "plane", swaps(1, n_plane))
+    first, ends = lax.optimization_barrier((first, ends))
     code, on_corner, off_corner = call(
-        join_kernel, [(16, Z), (T_ROWS, Z), (T_ROWS, Z)], [first, second, own[5]], cost=1_000_000
+        join_kernel, [(16, Z), (T_ROWS, Z), (T_ROWS, Z)], [first, ends, own[5]], cost=1_000_000
     )
     off_corner = lax.ppermute(off_corner, "slab", swaps(1, n_slab))
+    on_corner, on = lax.optimization_barrier((on_corner, on))
     on_corner = lax.all_gather(on_corner, "slab", axis_index_groups=cores)
     field = (3, ROWS * W, Z)
-    shapes = [field, field, (ROWS * W, Z), (ROWS * W, Z), (3, 256, Z), (6, 32, Z), (32, Z)]
+    longer = (ROWS * W + 96, Z)
+    shapes = [(3, *longer), (3, *longer), longer, longer, (3, 256 + 64, Z), (6, 32, Z), (32, Z)]
     shapes += [field] * 4 + [(9, 18 * W, Z), (7, 17 * W, Z), (54 + 112, W, Z)]
     disp, rec, ind = call(
         smooth_kernel,
         [(48, B, Z), (96, B, Z), (B, B, Z)],
-        [on, off, on_corner, off_corner, first, second, *own[:5], code],
+        [on, off, on_corner, off_corner, first, ends, middle, *own[:5], code],
         [pltpu.VMEM(shape, F32) for shape in shapes],
         cost=50_000_000,
     )

time: 55 us -> 51.2 us (0.931)
  the two profiles are of different devices: /device:TPU:138 before, /device:TPU:13 now
where the time goes in v5:
time: 51.2 us; the launch traced here: 50.9 us
  starting transfers between devices  29.5 us (58%)
  Pallas kernels  12.1 us (24%)
  blocking collectives  4.59 us (9%)
  waiting for transfers between devices  3.16 us (6%)
  between operations  0.81 us (2%)
  local copies, waits for them, and re-layouts  0.71 us (1%)
    pallas_call x4, Pallas kernels, call(): pl.pallas_call(kernel, out_shape=[jax.ShapeDtypeStruct(s, F32) for s in o...  12.1 us
    ppermute x1, starting transfers between devices, body(): ends = lax.ppermute(ends, 'plane', swaps(1, n_plane))  11.3 us
    ppermute x1, starting transfers between devices, body(): first = lax.ppermute(first, 'plane', swaps(0, n_plane))  7.64 us
    ppermute x1, starting transfers between devices, body(): off_corner = lax.ppermute(off_corner, 'slab', swaps(1, n_slab))  4.49 us
    ppermute x1, starting transfers between devices, body(): off = lax.ppermute(off, 'slab', swaps(1, n_slab))  4.16 us
    ppermute x1, waiting for transfers between devices, body(): middle = lax.ppermute(middle, 'plane', swaps(1, n_plane))  3.15 us
    all_gather x1, blocking collectives, body(): on = lax.all_gather(on, 'slab', axis_index_groups=cores)  2.51 us
    all_gather x1, blocking collectives, body(): on_corner = lax.all_gather(on_corner, 'slab', axis_index_groups=cores)  2.08 us
  transfers between devices with their start and end apart: 5, of which 1 were waited for; matrix products, arithmetic and copies ran while one was open for 0% of the time, Pallas kernels for 2%

profile of v5, /device:TPU:13, one launch (start us, length us, event | category | flops | bytes accessed | tf_op | source)
XLA Modules:
  0.0 50.9 jit_solution(2796328560386955685)
XLA Ops:
  0.6 0.0 copy-start
  0.6 0.0 copy-start.1
  0.7 0.0 copy-start.2
  0.7 0.0 copy-start.3
  0.7 0.0 copy-start.4
  0.7 2.4 %shard_map.85 = (f32[624,128]{1,0:T(8,128)}, f32[400,128]{1,0:T(8,128)}, f32[240,128]{1,0:T(8,128)}, f32[16,128]{1,0:T(8,128)}) custom-call(f32[768,128]{1,0:T(8,128)} %bitcast.11, f32[768,128]{1,0:T(8,128)} %bitcast.13, f32[256,128]{1,0:T(8,128)} %bitcast.15, f32[256,128]{1,0:T(8,128)} %bitcast.17, f32[192,128]{1,0:T(8,128)} %bitcast.19, s32[16,16]{1,0:T(8,128)} %agg_h.1), custom_call_target="tpu_custom_call" | custom-call | flops 1000000 | bytes 2000000 | tf_op jit(solution)/shard_map/pallas_call | solution.py:472
  3.1 7.6 %collective-permute-start = (f32[624,128]{1,0:T(8,128)}, f32[624,128]{1,0:T(8,128)S(1)}, u32[]{:S(2)}, u32[]{:S(2)}) collective-permute-start(f32[624,128]{1,0:T(8,128)} %get-tuple-element.25), channel_id=1, source_target_pairs={{0,1},{2,3},{4,5},{6,7},{8,9},{10,11},{12,13},{14,15},{16,17},{18,... | collective-permute-start | bytes 958472 | tf_op jit(solution)/shard_map/ppermute | solution.py:512
  10.7 11.3 %collective-permute-start.1 = (f32[400,128]{1,0:T(8,128)}, f32[400,128]{1,0:T(8,128)S(1)}, u32[]{:S(2)}, u32[]{:S(2)}) collective-permute-start(f32[400,128]{1,0:T(8,128)} %get-tuple-element.26), channel_id=1, source_target_pairs={{1,2},{3,4},{5,6},{7,8},{9,10},{11,12},{13,14},{15,16},{17,18},{19... | collective-permute-start | bytes 614408 | tf_op jit(solution)/shard_map/ppermute | solution.py:513
  22.0 0.0 copy-done
  22.1 0.7 %copy-done.5 = f32[16,128]{1,0:T(8,128)S(1)} copy-done((f32[16,128]{1,0:T(8,128)S(1)}, f32[16,128]{1,0:T(8,128)}, u32[]{:S(2)}) %copy-start.5) | copy-done | bytes 8216
  22.7 1.2 %shard_map.86 = (f32[1152,128]{1,0:T(8,128)S(1)}, f32[1152,128]{1,0:T(8,128)S(1)}, f32[384,128]{1,0:T(8,128)S(1)}, f32[384,128]{1,0:T(8,128)S(1)}, f32[384,128]{...) custom-call(f32[768,128]{1,0:T(8,128)S(1)} %bitcast.12, ...), custom_call_target="tpu_custom_call" | custom-call | flops 1000000 | bytes 2000000 | tf_op jit(solution)/shard_map/pallas_call | solution.py:472
  23.9 4.2 %collective-permute-start.2 = (f32[960,128]{1,0:T(8,128)S(1)}, f32[960,128]{1,0:T(8,128)S(1)}, u32[]{:S(2)}, u32[]{:S(2)}) collective-permute-start(f32[960,128]{1,0:T(8,128)S(1)} %get-tuple-element.34), channel_id=1, source_target_pairs={{32,64},{96,128},{160,192},{224,256},{288,320},{352,384},{416,448}... | collective-permute-start | bytes 1474568 | tf_op jit(solution)/shard_map/ppermute | solution.py:523
  28.1 0.0 copy-done.6
  28.1 1.9 %collective-permute-start.4 = (f32[240,128]{1,0:T(8,128)S(1)}, f32[240,128]{1,0:T(8,128)S(1)}, u32[]{:S(2)}, u32[]{:S(2)}) collective-permute-start(f32[240,128]{1,0:T(8,128)S(1)} %copy-done.6), channel_id=1, source_target_pairs={{1,2},{3,4},{5,6},{7,8},{9,10},{11,12},{13,14},{15,16},{17,18},{19... | collective-permute-start | bytes 368648 | tf_op jit(solution)/shard_map/ppermute | solution.py:525
  30.0 0.0 collective-permute-done.1.ends
  30.0 0.0 collective-permute-done.first
  30.0 0.1 shard_map.87
  30.1 4.5 %collective-permute-start.3 = (f32[392,128]{1,0:T(8,128)S(1)}, f32[392,128]{1,0:T(8,128)S(1)}, u32[]{:S(2)}, u32[]{:S(2)}) collective-permute-start(f32[392,128]{1,0:T(8,128)S(1)} %get-tuple-element.36), channel_id=1, source_target_pairs={{32,64},{96,128},{160,192},{224,256},{288,320},{352,384},{416,448}... | collective-permute-start | bytes 602120 | tf_op jit(solution)/shard_map/ppermute | solution.py:530
  34.6 2.5 %all-gather = f32[1920,128]{1,0:T(8,128)S(1)} all-gather(f32[960,128]{1,0:T(8,128)S(1)} %get-tuple-element.32), channel_id=2, replica_groups={{0,32},{64,96},{128,160},{192,224},{256,288},{320,352},{384,416},{448,4..., dimensions={0}, use_global_device_ids=true | all-gather | bytes 1474560 | tf_op jit(solution)/shard_map/all_gather | solution.py:524
  37.1 2.1 %all-gather.1 = f32[784,128]{1,0:T(8,128)S(1)} all-gather(f32[392,128]{1,0:T(8,128)S(1)} %get-tuple-element.35), channel_id=3, replica_groups={{0,32},{64,96},{128,160},{192,224},{256,288},{320,352},{384,416},{448,4..., dimensions={0}, use_global_device_ids=true | all-gather | bytes 602112 | tf_op jit(solution)/shard_map/all_gather | solution.py:532
  39.2 3.1 %collective-permute-done.4.middle = f32[240,128]{1,0:T(8,128)S(1)} collective-permute-done((f32[240,128]{1,0:T(8,128)S(1)}, f32[240,128]{1,0:T(8,128)S(1)}, u32[]{:S(2)}, u32[]{:S(2)}) %collective-permute-start.4) | collective-permute-done | bytes 122912 | tf_op jit(solution)/shard_map/ppermute | solution.py:525
  42.4 0.0 collective-permute-done.2.off
  42.4 0.0 collective-permute-done.3.off_corner
  42.4 8.5 %shard_map.88 = (f32[48,16,128]{2,1,0:T(8,128)}, f32[96,16,128]{2,1,0:T(8,128)}, f32[16,16,128]{2,1,0:T(8,128)}) custom-call(f32[2,960,128]{2,1,0:T(8,128)S(1)} %bitcast.9, f32[960,128]{1,0:T(8,128)S(1)} %collective-permute-done.2.off, f32[2,392,128]{2,1,0:T(8,128)S(1)} %bitcast.10, f32[392,128]{1,0:T(8,128)S(1)} %collective-permute-done.3.off_corner, ...), custom_call_target="tpu_custom_call" | custom-call | flops 50000000 | bytes 2000000 | tf_op jit(solution)/shard_map/pallas_call | solution.py:472
  (6 shorter events, 0.0 us)
Async XLA Ops:
  0.6 21.4 %copy-start = (f32[3,16,16,128]{3,2,1,0:T(8,128)S(1)}, f32[3,16,16,128]{3,2,1,0:T(8,128)}, u32[]{:S(2)}) copy-start(f32[3,16,16,128]{3,2,1,0:T(8,128)} %param.6) | copy-start | bytes 1179652
  0.6 21.4 %copy-start.1 = (f32[3,16,16,128]{3,2,1,0:T(8,128)S(1)}, f32[3,16,16,128]{3,2,1,0:T(8,128)}, u32[]{:S(2)}) copy-start(f32[3,16,16,128]{3,2,1,0:T(8,128)} %param.7) | copy-start | bytes 1179652
  0.7 21.4 %copy-start.2 = (f32[16,16,128]{2,1,0:T(8,128)S(1)}, f32[16,16,128]{2,1,0:T(8,128)}, u32[]{:S(2)}) copy-start(f32[16,16,128]{2,1,0:T(8,128)} %param.8) | copy-start | bytes 393220
  0.7 21.4 %copy-start.3 = (f32[16,16,128]{2,1,0:T(8,128)S(1)}, f32[16,16,128]{2,1,0:T(8,128)}, u32[]{:S(2)}) copy-start(f32[16,16,128]{2,1,0:T(8,128)} %param.11) | copy-start | bytes 393220
  0.7 21.4 %copy-start.4 = (f32[3,8,8,128]{3,2,1,0:T(8,128)S(1)}, f32[3,8,8,128]{3,2,1,0:T(8,128)}, u32[]{:S(2)}) copy-start(f32[3,8,8,128]{3,2,1,0:T(8,128)} %param.9) | copy-start | bytes 294916
  3.1 27.0 %collective-permute-start = (f32[624,128]{1,0:T(8,128)}, f32[624,128]{1,0:T(8,128)S(1)}, u32[]{:S(2)}, u32[]{:S(2)}) collective-permute-start(f32[624,128]{1,0:T(8,128)} %get-tuple-element.25), channel_id=1, source_target_pairs={{0,1},{2,3},{4,5},{6,7},{8,9},{10,11},{12,13},{14,15},{16,17},{18,... | collective-permute-start | bytes 958472 | tf_op jit(solution)/shard_map/ppermute | solution.py:512
  10.7 19.3 %collective-permute-start.1 = (f32[400,128]{1,0:T(8,128)}, f32[400,128]{1,0:T(8,128)S(1)}, u32[]{:S(2)}, u32[]{:S(2)}) collective-permute-start(f32[400,128]{1,0:T(8,128)} %get-tuple-element.26), channel_id=1, source_target_pairs={{1,2},{3,4},{5,6},{7,8},{9,10},{11,12},{13,14},{15,16},{17,18},{19... | collective-permute-start | bytes 614408 | tf_op jit(solution)/shard_map/ppermute | solution.py:513
  22.0 0.7 %copy-start.5 = (f32[16,128]{1,0:T(8,128)S(1)}, f32[16,128]{1,0:T(8,128)}, u32[]{:S(2)}) copy-start(f32[16,128]{1,0:T(8,128)} %get-tuple-element.29.code) | copy-start | bytes 24580
  22.7 5.3 %copy-start.6 = (f32[240,128]{1,0:T(8,128)S(1)}, f32[240,128]{1,0:T(8,128)}, u32[]{:S(2)}) copy-start(f32[240,128]{1,0:T(8,128)} %get-tuple-element.37) | copy-start | bytes 368644
  23.9 18.5 %collective-permute-start.2 = (f32[960,128]{1,0:T(8,128)S(1)}, f32[960,128]{1,0:T(8,128)S(1)}, u32[]{:S(2)}, u32[]{:S(2)}) collective-permute-start(f32[960,128]{1,0:T(8,128)S(1)} %get-tuple-element.34), channel_id=1, source_target_pairs={{32,64},{96,128},{160,192},{224,256},{288,320},{352,384},{416,448}... | collective-permute-start | bytes 1474568 | tf_op jit(solution)/shard_map/ppermute | solution.py:523
  28.1 14.3 %collective-permute-start.4 = (f32[240,128]{1,0:T(8,128)S(1)}, f32[240,128]{1,0:T(8,128)S(1)}, u32[]{:S(2)}, u32[]{:S(2)}) collective-permute-start(f32[240,128]{1,0:T(8,128)S(1)} %copy-done.6), channel_id=1, source_target_pairs={{1,2},{3,4},{5,6},{7,8},{9,10},{11,12},{13,14},{15,16},{17,18},{19... | collective-permute-start | bytes 368648 | tf_op jit(solution)/shard_map/ppermute | solution.py:525
  30.1 12.2 %collective-permute-start.3 = (f32[392,128]{1,0:T(8,128)S(1)}, f32[392,128]{1,0:T(8,128)S(1)}, u32[]{:S(2)}, u32[]{:S(2)}) collective-permute-start(f32[392,128]{1,0:T(8,128)S(1)} %get-tuple-element.36), channel_id=1, source_target_pairs={{32,64},{96,128},{160,192},{224,256},{288,320},{352,384},{416,448}... | collective-permute-start | bytes 602120 | tf_op jit(solution)/shard_map/ppermute | solution.py:530

commit v6 on v5

--- a/solution.py
+++ b/solution.py
@@ -342,7 +342,7 @@
                         dst[c, at, :] = keep * here_v + weight * r
             return mid, after
 
-        lax.fori_loop(first, last + 1, step, (sums(first - 1), sums(first)), unroll=8)
+        lax.fori_loop(first, last + 1, step, (sums(first - 1), sums(first)), unroll=(last + 1 - first) // 2)
 
     sigma = THETA / DELTA_C
     rho = 1.0 / sigma
@@ -375,7 +375,7 @@
                 gx[6 + c, at, :] = both_z - both
         return carry
 
-    lax.fori_loop(4, 22, gather_row, 0, unroll=6)
+    lax.fori_loop(4, 22, gather_row, 0, unroll=9)
 
     col_ok = [((g >= 0) & (g <= total_y - 2) & (place_z <= Z - 2)).astype(F32) for g in cols]
 
@@ -429,7 +429,7 @@
                 ey[q, pl.ds(aligned(n * W + 8 * l), 8), :] = t + pltpu.roll(t, 1, 1)
         return carry
 
-    lax.fori_loop(0, 17, element_row, 0, unroll=4)
+    lax.fori_loop(0, 17, element_row, 0, unroll=17)
 
     half_z = jnp.where(first_z | last_z, 1.0, 0.5)
     col_half = [jnp.where((g == 0) | (g == total_y - 1), half_z, 0.5 * half_z) for g in cols]
@@ -453,7 +453,7 @@
                 st[54 + q * 16 + i, pl.ds(l, 8, stride=3), :] = mean[q]
         return carry
 
-    lax.fori_loop(0, B, node_row, 0, unroll=4)
+    lax.fori_loop(0, B, node_row, 0, unroll=16)
 
     def put(i, carry):
         for c in range(3):
@@ -463,7 +463,7 @@
         ind[i] = st[54 + 96 + i, 4:20, :]
         return carry
 
-    lax.fori_loop(0, B, put, 0, unroll=2)
+    lax.fori_loop(0, B, put, 0, unroll=16)
 
 
 def call(kernel, outs, args, scratch=(), in_hbm=0, cost=0, vmem=48 * 1024 * 1024):

time: 51.2 us -> 49.6 us (0.969)
  Pallas kernels: 12.1 us -> 10.6 us
    pallas_call x4, Pallas kernels: 12.1 us -> 10.6 us  [call(): pl.pallas_call(kernel, out_shape=[jax.ShapeDtypeStruct(s, F32) for s in o...]
  transfers between devices with their start and end apart: 5 -> 5, of which waited for: 1 -> 1; matrix products, arithmetic and copies ran while one was open for 0% -> 0% of each run, Pallas kernels for 2% -> 3%
where the time goes in v6:
time: 49.6 us; the launch traced here: 49.3 us
  starting transfers between devices  29.5 us (59%)
  Pallas kernels  10.6 us (21%)
  blocking collectives  4.59 us (9%)
  waiting for transfers between devices  3.16 us (6%)
  between operations  0.81 us (2%)
  local copies, waits for them, and re-layouts  0.71 us (1%)
    ppermute x1, starting transfers between devices, body(): ends = lax.ppermute(ends, 'plane', swaps(1, n_plane))  11.3 us
    pallas_call x4, Pallas kernels, call(): pl.pallas_call(kernel, out_shape=[jax.ShapeDtypeStruct(s, F32) for s in o...  10.6 us
    ppermute x1, starting transfers between devices, body(): first = lax.ppermute(first, 'plane', swaps(0, n_plane))  7.64 us
    ppermute x1, starting transfers between devices, body(): off_corner = lax.ppermute(off_corner, 'slab', swaps(1, n_slab))  4.49 us
    ppermute x1, starting transfers between devices, body(): off = lax.ppermute(off, 'slab', swaps(1, n_slab))  4.16 us
    ppermute x1, waiting for transfers between devices, body(): middle = lax.ppermute(middle, 'plane', swaps(1, n_plane))  3.15 us
    all_gather x1, blocking collectives, body(): on = lax.all_gather(on, 'slab', axis_index_groups=cores)  2.51 us
    all_gather x1, blocking collectives, body(): on_corner = lax.all_gather(on_corner, 'slab', axis_index_groups=cores)  2.08 us
  transfers between devices with their start and end apart: 5, of which 1 were waited for; matrix products, arithmetic and copies ran while one was open for 0% of the time, Pallas kernels for 3%

profile of v6, /device:TPU:13, one launch (start us, length us, event | category | flops | bytes accessed | tf_op | source)
XLA Modules:
  0.0 49.3 jit_solution(15152077801276436857)
XLA Ops:
  0.6 0.0 copy-start
  0.6 0.0 copy-start.1
  0.7 0.0 copy-start.2
  0.7 0.0 copy-start.3
  0.7 0.0 copy-start.4
  0.7 2.4 %shard_map.85 = (f32[624,128]{1,0:T(8,128)}, f32[400,128]{1,0:T(8,128)}, f32[240,128]{1,0:T(8,128)}, f32[16,128]{1,0:T(8,128)}) custom-call(f32[768,128]{1,0:T(8,128)} %bitcast.11, f32[768,128]{1,0:T(8,128)} %bitcast.13, f32[256,128]{1,0:T(8,128)} %bitcast.15, f32[256,128]{1,0:T(8,128)} %bitcast.17, f32[192,128]{1,0:T(8,128)} %bitcast.19, s32[16,16]{1,0:T(8,128)} %agg_h.1), custom_call_target="tpu_custom_call" | custom-call | flops 1000000 | bytes 2000000 | tf_op jit(solution)/shard_map/pallas_call | solution.py:472
  3.1 7.6 %collective-permute-start = (f32[624,128]{1,0:T(8,128)}, f32[624,128]{1,0:T(8,128)S(1)}, u32[]{:S(2)}, u32[]{:S(2)}) collective-permute-start(f32[624,128]{1,0:T(8,128)} %get-tuple-element.25), channel_id=1, source_target_pairs={{0,1},{2,3},{4,5},{6,7},{8,9},{10,11},{12,13},{14,15},{16,17},{18,... | collective-permute-start | bytes 958472 | tf_op jit(solution)/shard_map/ppermute | solution.py:512
  10.7 11.3 %collective-permute-start.1 = (f32[400,128]{1,0:T(8,128)}, f32[400,128]{1,0:T(8,128)S(1)}, u32[]{:S(2)}, u32[]{:S(2)}) collective-permute-start(f32[400,128]{1,0:T(8,128)} %get-tuple-element.26), channel_id=1, source_target_pairs={{1,2},{3,4},{5,6},{7,8},{9,10},{11,12},{13,14},{15,16},{17,18},{19... | collective-permute-start | bytes 614408 | tf_op jit(solution)/shard_map/ppermute | solution.py:513
  22.0 0.0 copy-done
  22.1 0.7 %copy-done.5 = f32[16,128]{1,0:T(8,128)S(1)} copy-done((f32[16,128]{1,0:T(8,128)S(1)}, f32[16,128]{1,0:T(8,128)}, u32[]{:S(2)}) %copy-start.5) | copy-done | bytes 8216
  22.7 1.2 %shard_map.86 = (f32[1152,128]{1,0:T(8,128)S(1)}, f32[1152,128]{1,0:T(8,128)S(1)}, f32[384,128]{1,0:T(8,128)S(1)}, f32[384,128]{1,0:T(8,128)S(1)}, f32[384,128]{...) custom-call(f32[768,128]{1,0:T(8,128)S(1)} %bitcast.12, ...), custom_call_target="tpu_custom_call" | custom-call | flops 1000000 | bytes 2000000 | tf_op jit(solution)/shard_map/pallas_call | solution.py:472
  23.9 4.2 %collective-permute-start.2 = (f32[960,128]{1,0:T(8,128)S(1)}, f32[960,128]{1,0:T(8,128)S(1)}, u32[]{:S(2)}, u32[]{:S(2)}) collective-permute-start(f32[960,128]{1,0:T(8,128)S(1)} %get-tuple-element.34), channel_id=1, source_target_pairs={{32,64},{96,128},{160,192},{224,256},{288,320},{352,384},{416,448}... | collective-permute-start | bytes 1474568 | tf_op jit(solution)/shard_map/ppermute | solution.py:523
  28.1 0.0 copy-done.6
  28.1 1.9 %collective-permute-start.4 = (f32[240,128]{1,0:T(8,128)S(1)}, f32[240,128]{1,0:T(8,128)S(1)}, u32[]{:S(2)}, u32[]{:S(2)}) collective-permute-start(f32[240,128]{1,0:T(8,128)S(1)} %copy-done.6), channel_id=1, source_target_pairs={{1,2},{3,4},{5,6},{7,8},{9,10},{11,12},{13,14},{15,16},{17,18},{19... | collective-permute-start | bytes 368648 | tf_op jit(solution)/shard_map/ppermute | solution.py:525
  30.0 0.0 collective-permute-done.1.ends
  30.0 0.0 collective-permute-done.first
  30.0 0.1 shard_map.87
  30.1 4.5 %collective-permute-start.3 = (f32[392,128]{1,0:T(8,128)S(1)}, f32[392,128]{1,0:T(8,128)S(1)}, u32[]{:S(2)}, u32[]{:S(2)}) collective-permute-start(f32[392,128]{1,0:T(8,128)S(1)} %get-tuple-element.36), channel_id=1, source_target_pairs={{32,64},{96,128},{160,192},{224,256},{288,320},{352,384},{416,448}... | collective-permute-start | bytes 602120 | tf_op jit(solution)/shard_map/ppermute | solution.py:530
  34.6 2.5 %all-gather = f32[1920,128]{1,0:T(8,128)S(1)} all-gather(f32[960,128]{1,0:T(8,128)S(1)} %get-tuple-element.32), channel_id=2, replica_groups={{0,32},{64,96},{128,160},{192,224},{256,288},{320,352},{384,416},{448,4..., dimensions={0}, use_global_device_ids=true | all-gather | bytes 1474560 | tf_op jit(solution)/shard_map/all_gather | solution.py:524
  37.1 2.1 %all-gather.1 = f32[784,128]{1,0:T(8,128)S(1)} all-gather(f32[392,128]{1,0:T(8,128)S(1)} %get-tuple-element.35), channel_id=3, replica_groups={{0,32},{64,96},{128,160},{192,224},{256,288},{320,352},{384,416},{448,4..., dimensions={0}, use_global_device_ids=true | all-gather | bytes 602112 | tf_op jit(solution)/shard_map/all_gather | solution.py:532
  39.2 3.1 %collective-permute-done.4.middle = f32[240,128]{1,0:T(8,128)S(1)} collective-permute-done((f32[240,128]{1,0:T(8,128)S(1)}, f32[240,128]{1,0:T(8,128)S(1)}, u32[]{:S(2)}, u32[]{:S(2)}) %collective-permute-start.4) | collective-permute-done | bytes 122912 | tf_op jit(solution)/shard_map/ppermute | solution.py:525
  42.4 0.0 collective-permute-done.2.off
  42.4 0.0 collective-permute-done.3.off_corner
  42.4 6.9 %shard_map.88 = (f32[48,16,128]{2,1,0:T(8,128)}, f32[96,16,128]{2,1,0:T(8,128)}, f32[16,16,128]{2,1,0:T(8,128)}) custom-call(f32[2,960,128]{2,1,0:T(8,128)S(1)} %bitcast.9, f32[960,128]{1,0:T(8,128)S(1)} %collective-permute-done.2.off, f32[2,392,128]{2,1,0:T(8,128)S(1)} %bitcast.10, f32[392,128]{1,0:T(8,128)S(1)} %collective-permute-done.3.off_corner, ...), custom_call_target="tpu_custom_call" | custom-call | flops 50000000 | bytes 2000000 | tf_op jit(solution)/shard_map/pallas_call | solution.py:472
  (6 shorter events, 0.0 us)
Async XLA Ops:
  0.6 21.4 %copy-start = (f32[3,16,16,128]{3,2,1,0:T(8,128)S(1)}, f32[3,16,16,128]{3,2,1,0:T(8,128)}, u32[]{:S(2)}) copy-start(f32[3,16,16,128]{3,2,1,0:T(8,128)} %param.6) | copy-start | bytes 1179652
  0.6 21.4 %copy-start.1 = (f32[3,16,16,128]{3,2,1,0:T(8,128)S(1)}, f32[3,16,16,128]{3,2,1,0:T(8,128)}, u32[]{:S(2)}) copy-start(f32[3,16,16,128]{3,2,1,0:T(8,128)} %param.7) | copy-start | bytes 1179652
  0.7 21.4 %copy-start.2 = (f32[16,16,128]{2,1,0:T(8,128)S(1)}, f32[16,16,128]{2,1,0:T(8,128)}, u32[]{:S(2)}) copy-start(f32[16,16,128]{2,1,0:T(8,128)} %param.8) | copy-start | bytes 393220
  0.7 21.4 %copy-start.3 = (f32[16,16,128]{2,1,0:T(8,128)S(1)}, f32[16,16,128]{2,1,0:T(8,128)}, u32[]{:S(2)}) copy-start(f32[16,16,128]{2,1,0:T(8,128)} %param.11) | copy-start | bytes 393220
  0.7 21.4 %copy-start.4 = (f32[3,8,8,128]{3,2,1,0:T(8,128)S(1)}, f32[3,8,8,128]{3,2,1,0:T(8,128)}, u32[]{:S(2)}) copy-start(f32[3,8,8,128]{3,2,1,0:T(8,128)} %param.9) | copy-start | bytes 294916
  3.1 27.0 %collective-permute-start = (f32[624,128]{1,0:T(8,128)}, f32[624,128]{1,0:T(8,128)S(1)}, u32[]{:S(2)}, u32[]{:S(2)}) collective-permute-start(f32[624,128]{1,0:T(8,128)} %get-tuple-element.25), channel_id=1, source_target_pairs={{0,1},{2,3},{4,5},{6,7},{8,9},{10,11},{12,13},{14,15},{16,17},{18,... | collective-permute-start | bytes 958472 | tf_op jit(solution)/shard_map/ppermute | solution.py:512
  10.7 19.3 %collective-permute-start.1 = (f32[400,128]{1,0:T(8,128)}, f32[400,128]{1,0:T(8,128)S(1)}, u32[]{:S(2)}, u32[]{:S(2)}) collective-permute-start(f32[400,128]{1,0:T(8,128)} %get-tuple-element.26), channel_id=1, source_target_pairs={{1,2},{3,4},{5,6},{7,8},{9,10},{11,12},{13,14},{15,16},{17,18},{19... | collective-permute-start | bytes 614408 | tf_op jit(solution)/shard_map/ppermute | solution.py:513
  22.0 0.7 %copy-start.5 = (f32[16,128]{1,0:T(8,128)S(1)}, f32[16,128]{1,0:T(8,128)}, u32[]{:S(2)}) copy-start(f32[16,128]{1,0:T(8,128)} %get-tuple-element.29.code) | copy-start | bytes 24580
  22.7 5.3 %copy-start.6 = (f32[240,128]{1,0:T(8,128)S(1)}, f32[240,128]{1,0:T(8,128)}, u32[]{:S(2)}) copy-start(f32[240,128]{1,0:T(8,128)} %get-tuple-element.37) | copy-start | bytes 368644
  23.9 18.5 %collective-permute-start.2 = (f32[960,128]{1,0:T(8,128)S(1)}, f32[960,128]{1,0:T(8,128)S(1)}, u32[]{:S(2)}, u32[]{:S(2)}) collective-permute-start(f32[960,128]{1,0:T(8,128)S(1)} %get-tuple-element.34), channel_id=1, source_target_pairs={{32,64},{96,128},{160,192},{224,256},{288,320},{352,384},{416,448}... | collective-permute-start | bytes 1474568 | tf_op jit(solution)/shard_map/ppermute | solution.py:523
  28.1 14.3 %collective-permute-start.4 = (f32[240,128]{1,0:T(8,128)S(1)}, f32[240,128]{1,0:T(8,128)S(1)}, u32[]{:S(2)}, u32[]{:S(2)}) collective-permute-start(f32[240,128]{1,0:T(8,128)S(1)} %copy-done.6), channel_id=1, source_target_pairs={{1,2},{3,4},{5,6},{7,8},{9,10},{11,12},{13,14},{15,16},{17,18},{19... | collective-permute-start | bytes 368648 | tf_op jit(solution)/shard_map/ppermute | solution.py:525
  30.1 12.2 %collective-permute-start.3 = (f32[392,128]{1,0:T(8,128)S(1)}, f32[392,128]{1,0:T(8,128)S(1)}, u32[]{:S(2)}, u32[]{:S(2)}) collective-permute-start(f32[392,128]{1,0:T(8,128)S(1)} %get-tuple-element.36), channel_id=1, source_target_pairs={{32,64},{96,128},{160,192},{224,256},{288,320},{352,384},{416,448}... | collective-permute-start | bytes 602120 | tf_op jit(solution)/shard_map/ppermute | solution.py:530

commit v7 on v6

--- a/solution.py
+++ b/solution.py
@@ -93,24 +93,27 @@
             run(*((first, second) if side else (second, first)))
 
 
-def pack_kernel(
-    start_h, load_h, shift_h, cons_h, coarse_h, agg_h, first, ends, middle, code_o,
-    start, load, shift, cons, coarse, agg, sems,
-):
+def aggregate_code(agg):
     slab = lax.axis_index("slab")
     plane = lax.axis_index("plane")
     coarse_cols = CB * lax.axis_size("plane")
+    value = agg[0:B, :]
+    step_a = value // coarse_cols - (slab * CB + lax.broadcasted_iota(jnp.int32, (B, B), 0) // 2) + 1
+    step_b = value % coarse_cols - (plane * CB + lax.broadcasted_iota(jnp.int32, (B, B), 1) // 2) + 1
+    return (1 + 16 * step_a + step_b).astype(F32)
+
+
+def pack_kernel(
+    start_h, load_h, shift_h, cons_h, coarse_h, agg_h, first, ends, middle,
+    start, load, shift, cons, coarse, agg, sems,
+):
     fetch(
         (start_h, load_h, shift_h, cons_h, coarse_h, agg_h), (start, load, shift, cons, coarse, agg), sems
     )
-    value = agg[...]
-    step_a = value // coarse_cols - (slab * CB + lax.broadcasted_iota(jnp.int32, (B, B), 0) // 2) + 1
-    step_b = value % coarse_cols - (plane * CB + lax.broadcasted_iota(jnp.int32, (B, B), 1) // 2) + 1
-    code = (1 + 16 * step_a + step_b).astype(F32)
-    for out, row in ((first, PA), (ends, UA), (code_o, 0)):
+    code = aggregate_code(agg)
+    for out, row in ((first, PA), (ends, UA)):
         out[row : row + 16, :] = jnp.zeros((16, Z), F32)
         out[row : row + 16, 0:B] = code
-
     arrays = {"start": start, "load": load, "shift": shift, "cons": cons, "coarse": coarse}
 
     def pack(below, above):
@@ -133,10 +136,12 @@
 
 
 def own_kernel(
-    start_h, load_h, shift_h, cons_h, coarse_h, code, es, el, eh, ec, ek, ea, on, off,
-    start, load, shift, cons, coarse, sems,
+    start_h, load_h, shift_h, cons_h, coarse_h, agg_h, es, el, eh, ec, ek, ea, on, off,
+    start, load, shift, cons, coarse, agg, sems,
 ):
-    fetch((start_h, load_h, shift_h, cons_h, coarse_h), (start, load, shift, cons, coarse), sems)
+    fetch(
+        (start_h, load_h, shift_h, cons_h, coarse_h, agg_h), (start, load, shift, cons, coarse, agg), sems
+    )
 
     for ci in range(3 * B):
         for l, s0, j0, n in OWN:
@@ -145,7 +150,9 @@
                 dst[at : at + n, :] = src[pl.ds(ci * B + j0, n, stride=3), :]
     for ca in range(3 * CB):
         ek[16 * ca + 4 : 16 * ca + 12, :] = coarse[8 * ca : 8 * ca + 8, :]
-    ea[...] = pltpu.roll(code[...], 5, 1)
+    ea[...] = jnp.zeros((B, Z), F32)
+    ea[:, 0:B] = aggregate_code(agg)
+    ea[...] = pltpu.roll(ea[...], 5, 1)
     odd = lax.axis_index("slab") % 2
     for out, top in ((on, 1 - odd), (off, odd)):
         whole_rows(top, out, es, el, eh, ec, ek)
@@ -500,9 +507,9 @@
         return pairs + [(b, a) for a, b in pairs]
 
     args = [*fields, aggregate]
-    first, ends, middle, code = call(
+    first, ends, middle = call(
         pack_kernel,
-        [(P_ROWS, Z), (U_ROWS, Z), (V_ROWS, Z), (16, Z)],
+        [(P_ROWS, Z), (U_ROWS, Z), (V_ROWS, Z)],
         args,
         landing(args),
         in_hbm=6,
@@ -514,9 +521,9 @@
     *own, on, off = call(
         own_kernel,
         [(1152, Z), (1152, Z), (384, Z), (384, Z), (384, Z), (16, Z), (Q_ROWS, Z), (Q_ROWS, Z)],
-        [*fields, code],
-        landing(fields, 8),
-        in_hbm=5,
+        args,
+        landing(args, 8),
+        in_hbm=6,
         cost=1_000_000,
     )
     cores = [[i, i + 1] for i in range(0, n_slab, 2)]

time: 49.6 us -> 49.2 us (level)
  the two profiles are of different devices: /device:TPU:13 before, /device:TPU:119 now
where the time goes in v7:
time: 49.2 us; the launch traced here: 48.9 us
  starting transfers between devices  28.8 us (59%)
  Pallas kernels  10.6 us (22%)
  blocking collectives  4.59 us (9%)
  waiting for transfers between devices  4.08 us (8%)
  between operations  0.81 us (2%)
    pallas_call x4, Pallas kernels, call(): pl.pallas_call(kernel, out_shape=[jax.ShapeDtypeStruct(s, F32) for s in o...  10.6 us
    ppermute x1, starting transfers between devices, body(): ends = lax.ppermute(ends, 'plane', swaps(1, n_plane))  10.5 us
    ppermute x1, starting transfers between devices, body(): first = lax.ppermute(first, 'plane', swaps(0, n_plane))  7.63 us
    ppermute x1, starting transfers between devices, body(): off_corner = lax.ppermute(off_corner, 'slab', swaps(1, n_slab))  5.51 us
    ppermute x1, starting transfers between devices, body(): off = lax.ppermute(off, 'slab', swaps(1, n_slab))  3.26 us
    all_gather x1, blocking collectives, body(): on = lax.all_gather(on, 'slab', axis_index_groups=cores)  2.51 us
    ppermute x1, waiting for transfers between devices, body(): off_corner = lax.ppermute(off_corner, 'slab', swaps(1, n_slab))  2.27 us
    all_gather x1, blocking collectives, body(): on_corner = lax.all_gather(on_corner, 'slab', axis_index_groups=cores)  2.08 us
  transfers between devices with their start and end apart: 5, of which 3 were waited for; matrix products, arithmetic and copies ran while one was open for 0% of the time, Pallas kernels for 3%

profile of v7, /device:TPU:119, one launch (start us, length us, event | category | flops | bytes accessed | tf_op | source)
XLA Modules:
  0.0 48.9 jit_solution(6259994017314769203)
XLA Ops:
  0.6 0.0 copy-start
  0.7 2.4 %shard_map.85 = (f32[624,128]{1,0:T(8,128)}, f32[400,128]{1,0:T(8,128)}, f32[240,128]{1,0:T(8,128)}) custom-call(f32[768,128]{1,0:T(8,128)} %bitcast.11, f32[768,128]{1,0:T(8,128)} %bitcast.13, f32[256,128]{1,0:T(8,128)} %bitcast.15, f32[256,128]{1,0:T(8,128)} %bitcast.17, f32[192,128]{1,0:T(8,128)} %bitcast.19, s32[16,16]{1,0:T(8,128)} %agg_h.3), custom_call_target="tpu_custom_call" | custom-call | flops 1000000 | bytes 2000000 | tf_op jit(solution)/shard_map/pallas_call | solution.py:479
  3.1 7.6 %collective-permute-start = (f32[624,128]{1,0:T(8,128)}, f32[624,128]{1,0:T(8,128)S(1)}, u32[]{:S(2)}, u32[]{:S(2)}) collective-permute-start(f32[624,128]{1,0:T(8,128)} %get-tuple-element.24), channel_id=1, source_target_pairs={{0,1},{2,3},{4,5},{6,7},{8,9},{10,11},{12,13},{14,15},{16,17},{18,... | collective-permute-start | bytes 958472 | tf_op jit(solution)/shard_map/ppermute | solution.py:519
  10.7 0.0 copy-start.6
  10.7 10.5 %collective-permute-start.1 = (f32[400,128]{1,0:T(8,128)}, f32[400,128]{1,0:T(8,128)S(1)}, u32[]{:S(2)}, u32[]{:S(2)}) collective-permute-start(f32[400,128]{1,0:T(8,128)} %get-tuple-element.25), channel_id=1, source_target_pairs={{1,2},{3,4},{5,6},{7,8},{9,10},{11,12},{13,14},{15,16},{17,18},{19... | collective-permute-start | bytes 614408 | tf_op jit(solution)/shard_map/ppermute | solution.py:520
  21.2 0.0 copy-done
  21.3 0.0 copy-done.1
  21.3 0.0 copy-done.2
  21.3 0.0 copy-done.3
  21.3 0.0 copy-done.4
  21.3 0.0 copy-done.5
  21.3 1.2 %shard_map.86 = (f32[1152,128]{1,0:T(8,128)S(1)}, f32[1152,128]{1,0:T(8,128)S(1)}, f32[384,128]{1,0:T(8,128)S(1)}, f32[384,128]{1,0:T(8,128)S(1)}, f32[384,128]{...) custom-call(f32[768,128]{1,0:T(8,128)S(1)} %bitcast.12, ...), custom_call_target="tpu_custom_call" | custom-call | flops 1000000 | bytes 2000000 | tf_op jit(solution)/shard_map/pallas_call | solution.py:479
  22.5 3.3 %collective-permute-start.2 = (f32[960,128]{1,0:T(8,128)S(1)}, f32[960,128]{1,0:T(8,128)S(1)}, u32[]{:S(2)}, u32[]{:S(2)}) collective-permute-start(f32[960,128]{1,0:T(8,128)S(1)} %get-tuple-element.32), channel_id=1, source_target_pairs={{32,64},{96,128},{160,192},{224,256},{288,320},{352,384},{416,448}... | collective-permute-start | bytes 1474568 | tf_op jit(solution)/shard_map/ppermute | solution.py:530
  25.8 1.9 %collective-permute-start.4 = (f32[240,128]{1,0:T(8,128)S(1)}, f32[240,128]{1,0:T(8,128)S(1)}, u32[]{:S(2)}, u32[]{:S(2)}) collective-permute-start(f32[240,128]{1,0:T(8,128)S(1)} %copy-done.6), channel_id=1, source_target_pairs={{1,2},{3,4},{5,6},{7,8},{9,10},{11,12},{13,14},{15,16},{17,18},{19... | collective-permute-start | bytes 368648 | tf_op jit(solution)/shard_map/ppermute | solution.py:532
  27.7 0.5 %collective-permute-done.1.ends = f32[400,128]{1,0:T(8,128)S(1)} collective-permute-done((f32[400,128]{1,0:T(8,128)}, f32[400,128]{1,0:T(8,128)S(1)}, u32[]{:S(2)}, u32[]{:S(2)}) %collective-permute-start.1) | collective-permute-done | bytes 204832 | tf_op jit(solution)/shard_map/ppermute | solution.py:520
  28.3 0.0 collective-permute-done.first
  28.3 0.1 shard_map.87
  28.3 5.5 %collective-permute-start.3 = (f32[392,128]{1,0:T(8,128)S(1)}, f32[392,128]{1,0:T(8,128)S(1)}, u32[]{:S(2)}, u32[]{:S(2)}) collective-permute-start(f32[392,128]{1,0:T(8,128)S(1)} %get-tuple-element.34), channel_id=1, source_target_pairs={{32,64},{96,128},{160,192},{224,256},{288,320},{352,384},{416,448}... | collective-permute-start | bytes 602120 | tf_op jit(solution)/shard_map/ppermute | solution.py:537
  33.9 2.5 %all-gather = f32[1920,128]{1,0:T(8,128)S(1)} all-gather(f32[960,128]{1,0:T(8,128)S(1)} %get-tuple-element.30), channel_id=2, replica_groups={{0,32},{64,96},{128,160},{192,224},{256,288},{320,352},{384,416},{448,4..., dimensions={0}, use_global_device_ids=true | all-gather | bytes 1474560 | tf_op jit(solution)/shard_map/all_gather | solution.py:531
  36.4 2.1 %all-gather.1 = f32[784,128]{1,0:T(8,128)S(1)} all-gather(f32[392,128]{1,0:T(8,128)S(1)} %get-tuple-element.33), channel_id=3, replica_groups={{0,32},{64,96},{128,160},{192,224},{256,288},{320,352},{384,416},{448,4..., dimensions={0}, use_global_device_ids=true | all-gather | bytes 602112 | tf_op jit(solution)/shard_map/all_gather | solution.py:539
  38.5 0.0 collective-permute-done.4.middle
  38.5 1.3 %collective-permute-done.2.off = f32[960,128]{1,0:T(8,128)S(1)} collective-permute-done((f32[960,128]{1,0:T(8,128)S(1)}, f32[960,128]{1,0:T(8,128)S(1)}, u32[]{:S(2)}, u32[]{:S(2)}) %collective-permute-start.2) | collective-permute-done | bytes 491552 | tf_op jit(solution)/shard_map/ppermute | solution.py:530
  39.7 2.3 %collective-permute-done.3.off_corner = f32[392,128]{1,0:T(8,128)S(1)} collective-permute-done((f32[392,128]{1,0:T(8,128)S(1)}, f32[392,128]{1,0:T(8,128)S(1)}, u32[]{:S(2)}, u32[]{:S(2)}) %collective-permute-start.3) | collective-permute-done | bytes 200736 | tf_op jit(solution)/shard_map/ppermute | solution.py:537
  42.0 6.9 %shard_map.88 = (f32[48,16,128]{2,1,0:T(8,128)}, f32[96,16,128]{2,1,0:T(8,128)}, f32[16,16,128]{2,1,0:T(8,128)}) custom-call(f32[2,960,128]{2,1,0:T(8,128)S(1)} %bitcast.9, f32[960,128]{1,0:T(8,128)S(1)} %collective-permute-done.2.off, f32[2,392,128]{2,1,0:T(8,128)S(1)} %bitcast.10, f32[392,128]{1,0:T(8,128)S(1)} %collective-permute-done.3.off_corner, ...), custom_call_target="tpu_custom_call" | custom-call | flops 50000000 | bytes 2000000 | tf_op jit(solution)/shard_map/pallas_call | solution.py:479
  (6 shorter events, 0.0 us)
Async XLA Ops:
  0.6 20.6 %copy-start = (f32[3,16,16,128]{3,2,1,0:T(8,128)S(1)}, f32[3,16,16,128]{3,2,1,0:T(8,128)}, u32[]{:S(2)}) copy-start(f32[3,16,16,128]{3,2,1,0:T(8,128)} %param.6) | copy-start | bytes 1179652
  0.6 20.6 %copy-start.1 = (f32[3,16,16,128]{3,2,1,0:T(8,128)S(1)}, f32[3,16,16,128]{3,2,1,0:T(8,128)}, u32[]{:S(2)}) copy-start(f32[3,16,16,128]{3,2,1,0:T(8,128)} %param.7) | copy-start | bytes 1179652
  0.7 20.6 %copy-start.2 = (f32[16,16,128]{2,1,0:T(8,128)S(1)}, f32[16,16,128]{2,1,0:T(8,128)}, u32[]{:S(2)}) copy-start(f32[16,16,128]{2,1,0:T(8,128)} %param.8) | copy-start | bytes 393220
  0.7 20.6 %copy-start.3 = (f32[16,16,128]{2,1,0:T(8,128)S(1)}, f32[16,16,128]{2,1,0:T(8,128)}, u32[]{:S(2)}) copy-start(f32[16,16,128]{2,1,0:T(8,128)} %param.11) | copy-start | bytes 393220
  0.7 20.6 %copy-start.4 = (f32[3,8,8,128]{3,2,1,0:T(8,128)S(1)}, f32[3,8,8,128]{3,2,1,0:T(8,128)}, u32[]{:S(2)}) copy-start(f32[3,8,8,128]{3,2,1,0:T(8,128)} %param.9) | copy-start | bytes 294916
  0.7 20.6 %copy-start.5 = (s32[16,16]{1,0:T(8,128)S(1)}, s32[16,16]{1,0:T(8,128)}, u32[]{:S(2)}) copy-start(s32[16,16]{1,0:T(8,128)} %agg_h.3) | copy-start | bytes 3076
  3.1 25.2 %collective-permute-start = (f32[624,128]{1,0:T(8,128)}, f32[624,128]{1,0:T(8,128)S(1)}, u32[]{:S(2)}, u32[]{:S(2)}) collective-permute-start(f32[624,128]{1,0:T(8,128)} %get-tuple-element.24), channel_id=1, source_target_pairs={{0,1},{2,3},{4,5},{6,7},{8,9},{10,11},{12,13},{14,15},{16,17},{18,... | collective-permute-start | bytes 958472 | tf_op jit(solution)/shard_map/ppermute | solution.py:519
  10.7 15.1 %copy-start.6 = (f32[240,128]{1,0:T(8,128)S(1)}, f32[240,128]{1,0:T(8,128)}, u32[]{:S(2)}) copy-start(f32[240,128]{1,0:T(8,128)} %get-tuple-element.35) | copy-start | bytes 368644
  10.7 17.5 %collective-permute-start.1 = (f32[400,128]{1,0:T(8,128)}, f32[400,128]{1,0:T(8,128)S(1)}, u32[]{:S(2)}, u32[]{:S(2)}) collective-permute-start(f32[400,128]{1,0:T(8,128)} %get-tuple-element.25), channel_id=1, source_target_pairs={{1,2},{3,4},{5,6},{7,8},{9,10},{11,12},{13,14},{15,16},{17,18},{19... | collective-permute-start | bytes 614408 | tf_op jit(solution)/shard_map/ppermute | solution.py:520
  22.5 17.2 %collective-permute-start.2 = (f32[960,128]{1,0:T(8,128)S(1)}, f32[960,128]{1,0:T(8,128)S(1)}, u32[]{:S(2)}, u32[]{:S(2)}) collective-permute-start(f32[960,128]{1,0:T(8,128)S(1)} %get-tuple-element.32), channel_id=1, source_target_pairs={{32,64},{96,128},{160,192},{224,256},{288,320},{352,384},{416,448}... | collective-permute-start | bytes 1474568 | tf_op jit(solution)/shard_map/ppermute | solution.py:530
  25.8 12.7 %collective-permute-start.4 = (f32[240,128]{1,0:T(8,128)S(1)}, f32[240,128]{1,0:T(8,128)S(1)}, u32[]{:S(2)}, u32[]{:S(2)}) collective-permute-start(f32[240,128]{1,0:T(8,128)S(1)} %copy-done.6), channel_id=1, source_target_pairs={{1,2},{3,4},{5,6},{7,8},{9,10},{11,12},{13,14},{15,16},{17,18},{19... | collective-permute-start | bytes 368648 | tf_op jit(solution)/shard_map/ppermute | solution.py:532
  28.3 13.7 %collective-permute-start.3 = (f32[392,128]{1,0:T(8,128)S(1)}, f32[392,128]{1,0:T(8,128)S(1)}, u32[]{:S(2)}, u32[]{:S(2)}) collective-permute-start(f32[392,128]{1,0:T(8,128)S(1)} %get-tuple-element.34), channel_id=1, source_target_pairs={{32,64},{96,128},{160,192},{224,256},{288,320},{352,384},{416,448}... | collective-permute-start | bytes 602120 | tf_op jit(solution)/shard_map/ppermute | solution.py:537

commit v8 on v7

--- a/solution.py
+++ b/solution.py
@@ -527,6 +527,7 @@
         cost=1_000_000,
     )
     cores = [[i, i + 1] for i in range(0, n_slab, 2)]
+    off, first = lax.optimization_barrier((off, first))
     off = lax.ppermute(off, "slab", swaps(1, n_slab))
     on = lax.all_gather(on, "slab", axis_index_groups=cores)
     middle = lax.ppermute(middle, "plane", swaps(1, n_plane))

time: 49.2 us -> 58.6 us (1.19)
  the two profiles are of different devices: /device:TPU:119 before, /device:TPU:191 now
where the time goes in v8:
time: 58.6 us; the launch traced here: 58.3 us
  starting transfers between devices  40 us (68%)
  Pallas kernels  10.6 us (18%)
  blocking collectives  4.59 us (8%)
  waiting for transfers between devices  2.22 us (4%)
  between operations  0.82 us (1%)
    ppermute x1, starting transfers between devices, body(): middle = lax.ppermute(middle, 'plane', swaps(1, n_plane))  14.7 us
    pallas_call x4, Pallas kernels, call(): pl.pallas_call(kernel, out_shape=[jax.ShapeDtypeStruct(s, F32) for s in o...  10.6 us
    ppermute x1, starting transfers between devices, body(): ends = lax.ppermute(ends, 'plane', swaps(1, n_plane))  10.5 us
    ppermute x1, starting transfers between devices, body(): first = lax.ppermute(first, 'plane', swaps(0, n_plane))  7.63 us
    ppermute x1, starting transfers between devices, body(): off = lax.ppermute(off, 'slab', swaps(1, n_slab))  4.89 us
    all_gather x1, blocking collectives, body(): on = lax.all_gather(on, 'slab', axis_index_groups=cores)  2.51 us
    ppermute x1, starting transfers between devices, body(): off_corner = lax.ppermute(off_corner, 'slab', swaps(1, n_slab))  2.26 us
    all_gather x1, blocking collectives, body(): on_corner = lax.all_gather(on_corner, 'slab', axis_index_groups=cores)  2.08 us
  transfers between devices with their start and end apart: 5, of which 2 were waited for; matrix products, arithmetic and copies ran while one was open for 0% of the time, Pallas kernels for 2%

profile of v8, /device:TPU:191, one launch (start us, length us, event | category | flops | bytes accessed | tf_op | source)
XLA Modules:
  0.0 58.3 jit_solution(15482981508428599680)
XLA Ops:
  0.6 0.0 copy-start
  0.7 2.4 %shard_map.86 = (f32[624,128]{1,0:T(8,128)}, f32[400,128]{1,0:T(8,128)}, f32[240,128]{1,0:T(8,128)}) custom-call(f32[768,128]{1,0:T(8,128)} %bitcast.11, f32[768,128]{1,0:T(8,128)} %bitcast.13, f32[256,128]{1,0:T(8,128)} %bitcast.15, f32[256,128]{1,0:T(8,128)} %bitcast.17, f32[192,128]{1,0:T(8,128)} %bitcast.19, s32[16,16]{1,0:T(8,128)} %agg_h.3), custom_call_target="tpu_custom_call" | custom-call | flops 1000000 | bytes 2000000 | tf_op jit(solution)/shard_map/pallas_call | solution.py:479
  3.1 7.6 %collective-permute-start = (f32[624,128]{1,0:T(8,128)}, f32[624,128]{1,0:T(8,128)S(1)}, u32[]{:S(2)}, u32[]{:S(2)}) collective-permute-start(f32[624,128]{1,0:T(8,128)} %get-tuple-element.27), channel_id=1, source_target_pairs={{0,1},{2,3},{4,5},{6,7},{8,9},{10,11},{12,13},{14,15},{16,17},{18,... | collective-permute-start | bytes 958472 | tf_op jit(solution)/shard_map/ppermute | solution.py:519
  10.7 0.0 copy-start.6
  10.7 10.5 %collective-permute-start.1 = (f32[400,128]{1,0:T(8,128)}, f32[400,128]{1,0:T(8,128)S(1)}, u32[]{:S(2)}, u32[]{:S(2)}) collective-permute-start(f32[400,128]{1,0:T(8,128)} %get-tuple-element.29), channel_id=1, source_target_pairs={{1,2},{3,4},{5,6},{7,8},{9,10},{11,12},{13,14},{15,16},{17,18},{19... | collective-permute-start | bytes 614408 | tf_op jit(solution)/shard_map/ppermute | solution.py:520
  21.2 0.0 copy-done
  21.3 0.0 copy-done.1
  21.3 0.0 copy-done.2
  21.3 0.0 copy-done.3
  21.3 0.0 copy-done.4
  21.3 0.0 copy-done.5
  21.3 1.2 %shard_map.85 = (f32[1152,128]{1,0:T(8,128)S(1)}, f32[1152,128]{1,0:T(8,128)S(1)}, f32[384,128]{1,0:T(8,128)S(1)}, f32[384,128]{1,0:T(8,128)S(1)}, f32[384,128]{...) custom-call(f32[768,128]{1,0:T(8,128)S(1)} %bitcast.12, ...), custom_call_target="tpu_custom_call" | custom-call | flops 1000000 | bytes 2000000 | tf_op jit(solution)/shard_map/pallas_call | solution.py:479
  22.5 0.8 %collective-permute-done.first = f32[624,128]{1,0:T(8,128)S(1)} collective-permute-done((f32[624,128]{1,0:T(8,128)}, f32[624,128]{1,0:T(8,128)S(1)}, u32[]{:S(2)}, u32[]{:S(2)}) %collective-permute-start) | collective-permute-done | bytes 319520 | tf_op jit(solution)/shard_map/ppermute | solution.py:519
  23.3 4.9 %collective-permute-start.2 = (f32[960,128]{1,0:T(8,128)S(1)}, f32[960,128]{1,0:T(8,128)S(1)}, u32[]{:S(2)}, u32[]{:S(2)}) collective-permute-start(f32[960,128]{1,0:T(8,128)S(1)} %get-tuple-element.36), channel_id=1, source_target_pairs={{32,64},{96,128},{160,192},{224,256},{288,320},{352,384},{416,448}... | collective-permute-start | bytes 1474568 | tf_op jit(solution)/shard_map/ppermute | solution.py:531
  28.2 14.7 %collective-permute-start.4 = (f32[240,128]{1,0:T(8,128)S(1)}, f32[240,128]{1,0:T(8,128)S(1)}, u32[]{:S(2)}, u32[]{:S(2)}) collective-permute-start(f32[240,128]{1,0:T(8,128)S(1)} %copy-done.6), channel_id=1, source_target_pairs={{1,2},{3,4},{5,6},{7,8},{9,10},{11,12},{13,14},{15,16},{17,18},{19... | collective-permute-start | bytes 368648 | tf_op jit(solution)/shard_map/ppermute | solution.py:533
  43.0 0.0 collective-permute-done.1.ends
  43.0 0.1 shard_map.87
  43.1 2.3 %collective-permute-start.3 = (f32[392,128]{1,0:T(8,128)S(1)}, f32[392,128]{1,0:T(8,128)S(1)}, u32[]{:S(2)}, u32[]{:S(2)}) collective-permute-start(f32[392,128]{1,0:T(8,128)S(1)} %get-tuple-element.38), channel_id=1, source_target_pairs={{32,64},{96,128},{160,192},{224,256},{288,320},{352,384},{416,448}... | collective-permute-start | bytes 602120 | tf_op jit(solution)/shard_map/ppermute | solution.py:538
  45.4 2.5 %all-gather = f32[1920,128]{1,0:T(8,128)S(1)} all-gather(f32[960,128]{1,0:T(8,128)S(1)} %get-tuple-element.34), channel_id=2, replica_groups={{0,32},{64,96},{128,160},{192,224},{256,288},{320,352},{384,416},{448,4..., dimensions={0}, use_global_device_ids=true | all-gather | bytes 1474560 | tf_op jit(solution)/shard_map/all_gather | solution.py:532
  47.9 2.1 %all-gather.1 = f32[784,128]{1,0:T(8,128)S(1)} all-gather(f32[392,128]{1,0:T(8,128)S(1)} %get-tuple-element.37), channel_id=3, replica_groups={{0,32},{64,96},{128,160},{192,224},{256,288},{320,352},{384,416},{448,4..., dimensions={0}, use_global_device_ids=true | all-gather | bytes 602112 | tf_op jit(solution)/shard_map/all_gather | solution.py:540
  50.0 0.0 collective-permute-done.4.middle
  50.0 1.4 %collective-permute-done.3.off_corner = f32[392,128]{1,0:T(8,128)S(1)} collective-permute-done((f32[392,128]{1,0:T(8,128)S(1)}, f32[392,128]{1,0:T(8,128)S(1)}, u32[]{:S(2)}, u32[]{:S(2)}) %collective-permute-start.3) | collective-permute-done | bytes 200736 | tf_op jit(solution)/shard_map/ppermute | solution.py:538
  51.4 0.0 collective-permute-done.2.off
  51.4 6.9 %shard_map.88 = (f32[48,16,128]{2,1,0:T(8,128)}, f32[96,16,128]{2,1,0:T(8,128)}, f32[16,16,128]{2,1,0:T(8,128)}) custom-call(f32[2,960,128]{2,1,0:T(8,128)S(1)} %bitcast.9, f32[960,128]{1,0:T(8,128)S(1)} %collective-permute-done.2.off, f32[2,392,128]{2,1,0:T(8,128)S(1)} %bitcast.10, f32[392,128]{1,0:T(8,128)S(1)} %collective-permute-done.3.off_corner, ...), custom_call_target="tpu_custom_call" | custom-call | flops 50000000 | bytes 2000000 | tf_op jit(solution)/shard_map/pallas_call | solution.py:479
  (6 shorter events, 0.0 us)
Async XLA Ops:
  0.6 20.6 %copy-start = (f32[3,16,16,128]{3,2,1,0:T(8,128)S(1)}, f32[3,16,16,128]{3,2,1,0:T(8,128)}, u32[]{:S(2)}) copy-start(f32[3,16,16,128]{3,2,1,0:T(8,128)} %param.6) | copy-start | bytes 1179652
  0.6 20.6 %copy-start.1 = (f32[3,16,16,128]{3,2,1,0:T(8,128)S(1)}, f32[3,16,16,128]{3,2,1,0:T(8,128)}, u32[]{:S(2)}) copy-start(f32[3,16,16,128]{3,2,1,0:T(8,128)} %param.7) | copy-start | bytes 1179652
  0.7 20.6 %copy-start.2 = (f32[16,16,128]{2,1,0:T(8,128)S(1)}, f32[16,16,128]{2,1,0:T(8,128)}, u32[]{:S(2)}) copy-start(f32[16,16,128]{2,1,0:T(8,128)} %param.8) | copy-start | bytes 393220
  0.7 20.6 %copy-start.3 = (f32[16,16,128]{2,1,0:T(8,128)S(1)}, f32[16,16,128]{2,1,0:T(8,128)}, u32[]{:S(2)}) copy-start(f32[16,16,128]{2,1,0:T(8,128)} %param.11) | copy-start | bytes 393220
  0.7 20.6 %copy-start.4 = (f32[3,8,8,128]{3,2,1,0:T(8,128)S(1)}, f32[3,8,8,128]{3,2,1,0:T(8,128)}, u32[]{:S(2)}) copy-start(f32[3,8,8,128]{3,2,1,0:T(8,128)} %param.9) | copy-start | bytes 294916
  0.7 20.6 %copy-start.5 = (s32[16,16]{1,0:T(8,128)S(1)}, s32[16,16]{1,0:T(8,128)}, u32[]{:S(2)}) copy-start(s32[16,16]{1,0:T(8,128)} %agg_h.3) | copy-start | bytes 3076
  3.1 20.3 %collective-permute-start = (f32[624,128]{1,0:T(8,128)}, f32[624,128]{1,0:T(8,128)S(1)}, u32[]{:S(2)}, u32[]{:S(2)}) collective-permute-start(f32[624,128]{1,0:T(8,128)} %get-tuple-element.27), channel_id=1, source_target_pairs={{0,1},{2,3},{4,5},{6,7},{8,9},{10,11},{12,13},{14,15},{16,17},{18,... | collective-permute-start | bytes 958472 | tf_op jit(solution)/shard_map/ppermute | solution.py:519
  10.7 17.5 %copy-start.6 = (f32[240,128]{1,0:T(8,128)S(1)}, f32[240,128]{1,0:T(8,128)}, u32[]{:S(2)}) copy-start(f32[240,128]{1,0:T(8,128)} %get-tuple-element.39) | copy-start | bytes 368644
  10.7 32.3 %collective-permute-start.1 = (f32[400,128]{1,0:T(8,128)}, f32[400,128]{1,0:T(8,128)S(1)}, u32[]{:S(2)}, u32[]{:S(2)}) collective-permute-start(f32[400,128]{1,0:T(8,128)} %get-tuple-element.29), channel_id=1, source_target_pairs={{1,2},{3,4},{5,6},{7,8},{9,10},{11,12},{13,14},{15,16},{17,18},{19... | collective-permute-start | bytes 614408 | tf_op jit(solution)/shard_map/ppermute | solution.py:520
  23.3 28.0 %collective-permute-start.2 = (f32[960,128]{1,0:T(8,128)S(1)}, f32[960,128]{1,0:T(8,128)S(1)}, u32[]{:S(2)}, u32[]{:S(2)}) collective-permute-start(f32[960,128]{1,0:T(8,128)S(1)} %get-tuple-element.36), channel_id=1, source_target_pairs={{32,64},{96,128},{160,192},{224,256},{288,320},{352,384},{416,448}... | collective-permute-start | bytes 1474568 | tf_op jit(solution)/shard_map/ppermute | solution.py:531
  28.2 21.7 %collective-permute-start.4 = (f32[240,128]{1,0:T(8,128)S(1)}, f32[240,128]{1,0:T(8,128)S(1)}, u32[]{:S(2)}, u32[]{:S(2)}) collective-permute-start(f32[240,128]{1,0:T(8,128)S(1)} %copy-done.6), channel_id=1, source_target_pairs={{1,2},{3,4},{5,6},{7,8},{9,10},{11,12},{13,14},{15,16},{17,18},{19... | collective-permute-start | bytes 368648 | tf_op jit(solution)/shard_map/ppermute | solution.py:533
  43.1 8.2 %collective-permute-start.3 = (f32[392,128]{1,0:T(8,128)S(1)}, f32[392,128]{1,0:T(8,128)S(1)}, u32[]{:S(2)}, u32[]{:S(2)}) collective-permute-start(f32[392,128]{1,0:T(8,128)S(1)} %get-tuple-element.38), channel_id=1, source_target_pairs={{32,64},{96,128},{160,192},{224,256},{288,320},{352,384},{416,448}... | collective-permute-start | bytes 602120 | tf_op jit(solution)/shard_map/ppermute | solution.py:538
